TPU v7x, 32 devices: a whole 2x2x4 slice. The times are simulated.
32 devices in a mesh: dom: 4 (over z), feat: 8 (over y, x, core).
Axes of the slice: x: 2, y: 2, z: 4, core: 2. Of those that a mesh axis runs over, the one named last changes fastest.
Arguments:
- features: bfloat16 [4096, 4096], P('dom', 'feat'), may hold values from -6 to 6
- proj_weight: bfloat16 [3, 4096, 256], P(None, 'feat'), may hold values from -0.75 to 0.75
- source_block: int32 [32, 3, 4], P('dom'), may hold values from 0 to 7
- slot_count: int32 [32, 3], P('dom'), may hold values from 1 to 4
- block_pattern: int32 [32, 3, 4, 8, 128], P('dom'), may hold values from 0 to 65535
- node_type: int32 [4096], P(('dom', 'feat')), may hold values from 0 to 2
- type_gain: float32 [3, 256], replicated, may hold values from 0.1 to 1.9
- cotangent: bfloat16 [4096, 256], P(('dom', 'feat')), may hold values from -6 to 6
Outputs:
- activations: bfloat16 [4096, 256], P(('dom', 'feat'))
- weight_grad: float32 [3, 4096, 256], P(None, 'feat')
Inputs may be any that keep to these rules, and one draw needn't show every extreme that they name: `source_block`: a block index within the destination block's own partition. `slot_count`: slots at or past this count are ignored. `block_pattern`: bit j of the word at index w, i marks an edge from source node 16 w + j of the slot's block to node i of the destination block.
All inputs are finite; a program needn't handle non-finite values.
Results may differ from a plain program's by a relative error of at most 0.0055.
Values may be sent and summed in bfloat16 or wider, within the bound.
No kernel may reach another device: no remote copies, remote signals or barrier semaphores. Data moves between devices by JAX's collectives and lax.ppermute only.
A program may use at most 128 MiB of HBM per device.

v0:
```python
import functools

import jax
import jax.numpy as jnp
from jax import lax
from jax.experimental import pallas as pl
from jax.experimental.pallas import tpu as pltpu
from jax.sharding import PartitionSpec as P

BLK = 128
MIB = 1024 * 1024
BF16 = jnp.bfloat16
F32 = jnp.float32


def unpack_bits(packed):
    shifts = (2 ** jnp.arange(16)).astype(jnp.int32)
    bit_values = packed[..., None] // shifts % 2
    bit_values = jnp.swapaxes(bit_values, -3, -2)
    return bit_values.reshape(packed.shape[:-2] + (packed.shape[-1], packed.shape[-2] * 16))


def silu_grad(pre_act):
    sigmoid_value = jax.nn.sigmoid(pre_act)
    return sigmoid_value * (1.0 + pre_act * (1.0 - sigmoid_value))


def type_rows(node_type, type_gain):
    onehot = (
        node_type[:, None] == jnp.arange(type_gain.shape[0], dtype=jnp.int32)[None, :]
    ).astype(jnp.float32)
    return jnp.sum(onehot[:, :, None] * type_gain[None, :, :], axis=1)


def aggregate(features, source_block, slot_count, block_pattern):
    count_blocks = source_block.shape[0]
    relations = source_block.shape[1]
    slots_each = source_block.shape[2]
    col_width = features.shape[1]
    blocks = features.reshape(count_blocks, BLK, col_width)
    blocks_wide = blocks.astype(jnp.float32)
    live_slots = (
        jnp.arange(slots_each, dtype=jnp.int32)[None, None, :] < slot_count[:, :, None]
    ).astype(jnp.float32)
    mixed_list = []
    for relation in range(relations):
        summed = jnp.zeros((count_blocks, BLK, col_width), jnp.float32)
        degree = jnp.zeros((count_blocks, BLK), jnp.float32)
        for slot_index in range(slots_each):
            adjacency = (
                unpack_bits(block_pattern[:, relation, slot_index]).astype(jnp.float32)
                * live_slots[:, relation, slot_index][:, None, None]
            )
            picked = jnp.take(blocks, source_block[:, relation, slot_index], axis=0)
            summed = summed + jnp.einsum(
                "bij,bjc->bic",
                adjacency.astype(jnp.bfloat16),
                picked,
                preferred_element_type=jnp.float32,
            )
            degree = degree + jnp.sum(adjacency, axis=2)
        mixed_rows = ((blocks_wide + summed) / (1.0 + degree)[:, :, None]).astype(jnp.bfloat16)
        mixed_list.append(mixed_rows.reshape(count_blocks * BLK, col_width))
    return jnp.stack(mixed_list)


def general_body(
    features, proj_weight, source_block, slot_count, block_pattern, node_type, type_gain, cotangent
):
    mixed_all = aggregate(features, source_block, slot_count, block_pattern)
    pre_act = lax.psum_scatter(
        jnp.einsum("rnc,rch->nh", mixed_all, proj_weight, preferred_element_type=jnp.float32),
        "feat",
        scatter_dimension=0,
        tiled=True,
    )
    row_gains = type_rows(node_type, type_gain)
    output = (jax.nn.silu(pre_act) * row_gains).astype(jnp.bfloat16)
    slope_rows = (cotangent.astype(jnp.float32) * row_gains * silu_grad(pre_act)).astype(
        jnp.bfloat16
    )
    local_grad = jnp.einsum(
        "rnc,nh->rch",
        mixed_all,
        lax.all_gather(slope_rows, "feat", axis=0, tiled=True),
        preferred_element_type=jnp.float32,
    )
    weight_grad = lax.psum(local_grad, "dom")
    return (output, weight_grad)


def live_words(relation, slot, b, cnt_ref, pat_ref):
    live = jnp.where(slot < cnt_ref[relation, b], 0xFFFF, 0)
    return pat_ref[b, relation, slot] & live


def start_adjacency(places):
    sub = lax.broadcasted_iota(jnp.int32, (BLK, BLK), 0)
    lane = lax.broadcasted_iota(jnp.int32, (BLK, BLK), 1)
    eye = jnp.where(sub == lane, 1.0, 0.0).astype(BF16)
    for b, (ref, lanes) in enumerate(places):
        ref[:, lanes] = jnp.zeros((ref.shape[0], BLK), BF16)
        ref[b * BLK : (b + 1) * BLK, lanes] = eye


def add_edges(relation, places, src_ref, cnt_ref, pat_ref):
    bit = jnp.left_shift(1, lax.broadcasted_iota(jnp.int32, (16, BLK), 0))
    for s in range(src_ref.shape[1]):
        for b, (ref, lanes) in enumerate(places):
            words = live_words(relation, s, b, cnt_ref, pat_ref)
            row0 = pl.multiple_of(src_ref[relation, s, b] * BLK, BLK)
            parts = [
                jnp.where((words[w : w + 1, :] & bit) != 0, 1.0, 0.0)
                for w in range(words.shape[0])
            ]
            ref[pl.ds(row0, BLK), lanes] += jnp.concatenate(parts, axis=0).astype(BF16)


def inverse_degrees(relation, inv_ref, src_ref, cnt_ref, pat_ref):
    for b in range(src_ref.shape[2]):
        degree = jnp.zeros((8, BLK), jnp.int32)
        for s in range(src_ref.shape[1]):
            words = live_words(relation, s, b, cnt_ref, pat_ref)
            c = words - ((words >> 1) & 0x5555)
            c = (c & 0x3333) + ((c >> 2) & 0x3333)
            c = (c + (c >> 4)) & 0x0F0F
            degree = degree + ((c + (c >> 8)) & 0x1F)
        total = jnp.sum(degree.astype(F32), axis=0, keepdims=True)
        inv_ref[relation, 0:1, b * BLK : (b + 1) * BLK] = 1.0 / (1.0 + total)


def forward_kernel(n_feat, src_ref, cnt_ref, pat_ref, x_ref, w_ref, inv_ref, *rest):
    relations, slots, blocks = src_ref.shape
    piece_refs, adj_refs = rest[:n_feat], rest[n_feat : n_feat + relations]
    pre_ref = rest[n_feat + relations]
    places = [
        [(adj_ref, slice(b * BLK, (b + 1) * BLK)) for b in range(blocks)] for adj_ref in adj_refs
    ]

    for relation in range(relations):
        start_adjacency(places[relation])
    for relation in range(relations):
        inverse_degrees(relation, inv_ref, src_ref, cnt_ref, pat_ref)
        add_edges(relation, places[relation], src_ref, cnt_ref, pat_ref)
        y_t = lax.dot_general(
            w_ref[relation].T, x_ref[...], (((1,), (1,)), ((), ())), preferred_element_type=F32
        ).astype(BF16)
        p_t = jnp.dot(y_t, adj_refs[relation][...], preferred_element_type=F32)
        p_t = p_t * inv_ref[relation, 0:1, :]
        if relation == 0:
            pre_ref[...] = p_t
        else:
            pre_ref[...] += p_t

    me = lax.axis_index("feat")
    for k, piece in enumerate(piece_refs):
        first = pl.multiple_of((me ^ k) * BLK, BLK)
        piece[...] = pre_ref[:, pl.ds(first, BLK)].T.astype(BF16)


def forward(features, proj_weight, source_block, slot_count, block_pattern, n_feat):
    nodes, cols = features.shape
    relations, _, hidden = proj_weight.shape
    smem = pl.BlockSpec(memory_space=pltpu.SMEM)
    vmem = pl.BlockSpec(memory_space=pltpu.VMEM)
    inv_deg, *out = pl.pallas_call(
        functools.partial(forward_kernel, n_feat),
        name="forward",
        out_shape=[jax.ShapeDtypeStruct((relations, 8, nodes), F32)]
        + [jax.ShapeDtypeStruct((nodes // n_feat, hidden), BF16)] * n_feat
        + [jax.ShapeDtypeStruct((nodes, nodes), BF16)] * relations,
        in_specs=[smem, smem, vmem, vmem, vmem],
        out_specs=[vmem] * (1 + n_feat + relations),
        scratch_shapes=[pltpu.VMEM((hidden, nodes), F32)],
        compiler_params=pltpu.CompilerParams(vmem_limit_bytes=24 * MIB),
    )(source_block, slot_count, block_pattern, features, proj_weight)
    return inv_deg, out[:n_feat], out[n_feat:]


def transposed_kernel(x_ref, inv_ref, xt_ref, *col_refs):
    nodes = x_ref.shape[0]
    for b in range(nodes // BLK):
        rows = slice(b * BLK, (b + 1) * BLK)
        xt_ref[:, rows] = x_ref[rows, :].T
        for r, col_ref in enumerate(col_refs):
            wide = jnp.broadcast_to(inv_ref[r, 0:1, rows], (BLK, BLK))
            col_ref[rows, :] = wide.T


def transposed(features, inv_deg):
    nodes, cols = features.shape
    relations = inv_deg.shape[0]
    x_t, *col = pl.pallas_call(
        transposed_kernel,
        name="transposed",
        out_shape=[jax.ShapeDtypeStruct((cols, nodes), BF16)]
        + [jax.ShapeDtypeStruct((nodes, BLK), F32)] * relations,
        compiler_params=pltpu.CompilerParams(vmem_limit_bytes=8 * MIB),
        cost_estimate=pl.CostEstimate(
            flops=2 * nodes * cols, bytes_accessed=6 * nodes * cols, transcendentals=0
        ),
    )(features, inv_deg)
    return x_t, col


def combine_kernel(n_feat, *refs):
    type_ref, gain_ref, cot_ref, act_ref, slope_ref = refs[n_feat:]
    rows = act_ref.shape[0]
    pre = refs[0][...].astype(F32)
    for piece in refs[1:n_feat]:
        pre = pre + piece[...].astype(F32)
    types = jnp.broadcast_to(type_ref[...].astype(F32), (rows, rows)).T
    types = jnp.concatenate([types] * (act_ref.shape[1] // rows), axis=1)
    gain = jnp.zeros(act_ref.shape, F32)
    for t in range(gain_ref.shape[0]):
        gain = jnp.where(types == t, gain_ref[t : t + 1, :], gain)
    sig = jax.nn.sigmoid(pre)
    act_ref[...] = (pre * sig * gain).astype(BF16)
    grad = sig * (1.0 + pre * (1.0 - sig))
    slope_ref[...] = (cot_ref[...].astype(F32) * gain * grad).astype(BF16)


def combine(pieces, node_type, type_gain, cotangent):
    return pl.pallas_call(
        functools.partial(combine_kernel, len(pieces)),
        name="combine",
        out_shape=[jax.ShapeDtypeStruct(cotangent.shape, BF16)] * 2,
        compiler_params=pltpu.CompilerParams(vmem_limit_bytes=6 * MIB),
    )(*pieces, node_type[None, :], type_gain, cotangent)


def gradient_kernel(n_feat, xt_ref, adj_ref, col_ref, *rest):
    sent_ref, scaled_ref = rest[n_feat:]
    me = lax.axis_index("feat")
    for k, piece in zip(ORDER, rest[:n_feat]):
        rows = pl.ds(pl.multiple_of((me ^ k) * BLK, BLK), BLK)
        inv = jnp.concatenate([col_ref[rows, :]] * (piece.shape[1] // BLK), axis=1)
        scaled_ref[rows, :] = (piece[...].astype(F32) * inv).astype(BF16)
    spread = jnp.dot(adj_ref[...], scaled_ref[...], preferred_element_type=F32).astype(BF16)
    grad = jnp.dot(xt_ref[...], spread, preferred_element_type=F32)
    sent_ref[...] = grad.astype(BF16)


def gradient(x_t, adj, col, slopes):
    cols, nodes = x_t.shape
    hidden = slopes[0].shape[1]
    vmem = pl.BlockSpec(memory_space=pltpu.VMEM)
    return pl.pallas_call(
        functools.partial(gradient_kernel, len(slopes)),
        name="gradient",
        out_shape=jax.ShapeDtypeStruct((cols, hidden), BF16),
        in_specs=[vmem] * (3 + len(slopes)),
        out_specs=vmem,
        scratch_shapes=[pltpu.VMEM((nodes, hidden), BF16)],
        compiler_params=pltpu.CompilerParams(vmem_limit_bytes=8 * MIB),
        cost_estimate=pl.CostEstimate(
            flops=2 * nodes * hidden * (nodes + cols),
            bytes_accessed=2 * nodes * nodes + 6 * cols * hidden,
            transcendentals=0,
        ),
    )(x_t, adj, col, *slopes)


def rounded(x):
    return lax.reduce_precision(x, 8, 7)


def chain_sum(chunks, n_dom):
    half = n_dom // 2
    at = lax.axis_index("dom")
    inner = []
    for sent in chunks:
        for hop in range(half - 1):
            perm = [(hop, hop + 1), (n_dom - 1 - hop, n_dom - 2 - hop)]
            got = lax.ppermute(sent, "dom", perm)
            sent = rounded(sent.astype(F32) + got.astype(F32)).astype(BF16)
        inner.append(sent)
    middle = []
    for i, sent in enumerate(inner):
        if i >= 2:
            sent, _ = lax.optimization_barrier((sent, middle[i - 2]))
        got = lax.ppermute(sent, "dom", [(half - 1, half), (half, half - 1)])
        middle.append(rounded(sent.astype(F32) + got.astype(F32)).astype(BF16))
    outer = []
    for i, sent in enumerate(middle):
        if i >= 2:
            sent, outer[i - 2] = lax.optimization_barrier((sent, outer[i - 2]))
        for hop in range(half - 1):
            low, high = half - 1 - hop, half + hop
            got = lax.ppermute(sent, "dom", [(low, low - 1), (high, high + 1)])
            sent = jnp.where((at < low) | (at > high), got, sent)
        outer.append(sent)
    return [sent.astype(F32) for sent in outer]


ORDER = (6, 7, 4, 5, 2, 3, 1, 0)


def exchange(value_of, n_feat):
    got = []
    for k in ORDER[:-1]:
        got.append(lax.ppermute(value_of(k), "feat", [(i, i ^ k) for i in range(n_feat)]))
    return got + [value_of(0)]


def dense_body(
    n_dom,
    n_feat,
    features,
    proj_weight,
    source_block,
    slot_count,
    block_pattern,
    node_type,
    type_gain,
    cotangent,
):
    source_block = jnp.transpose(source_block, (1, 2, 0))
    slot_count = jnp.transpose(slot_count, (1, 0))
    inv_deg, pieces, adj = forward(
        features, proj_weight, source_block, slot_count, block_pattern, n_feat
    )
    received = exchange(lambda k: pieces[k], n_feat)
    x_t, col = transposed(features, inv_deg)
    activations, slope = combine(received, node_type, type_gain, cotangent)
    slopes = exchange(lambda k: slope, n_feat)
    chunks = [
        gradient(x_t, adj[relation], col[relation], slopes)
        for relation in range(proj_weight.shape[0])
    ]
    return activations, jnp.stack(chain_sum(chunks, n_dom))


def body(n_dom, n_feat, *args):
    nodes, relations = args[0].shape[0], args[2].shape[1]
    fits = 2 * relations * nodes * nodes <= 8 * MIB
    if fits and n_feat == 8 and n_dom % 2 == 0 and nodes == n_feat * BLK:
        return dense_body(n_dom, n_feat, *args)
    return general_body(*args)


def solution(mesh):
    placed = (
        P("dom", "feat"),
        P(None, "feat", None),
        P("dom", None, None),
        P("dom", None),
        P("dom", None, None, None, None),
        P(("dom", "feat")),
        P(),
        P(("dom", "feat"), None),
    )
    return jax.shard_map(
        functools.partial(body, mesh.shape["dom"], mesh.shape["feat"]),
        mesh=mesh,
        in_specs=placed,
        out_specs=(P(("dom", "feat"), None), P(None, "feat", None)),
        check_vma=False,
    )
```

profile of v0, /device:TPU:0, one launch (start us, length us, event | category | flops | bytes accessed | tf_op | source)
XLA Modules:
  0.0 81.7 jit_solution(134067151796549681)
XLA Ops:
  0.7 1.2 %copy-done = bf16[1024,512]{1,0:T(8,128)(2,1)S(1)} copy-done((bf16[1024,512]{1,0:T(8,128)(2,1)S(1)}, bf16[1024,512]{1,0:T(8,128)(2,1)}, u32[]{:S(2)}) %copy-start) | copy-done | bytes 1048600
  1.9 1.1 %copy-done.1 = bf16[3,512,256]{2,1,0:T(8,128)(2,1)S(1)} copy-done((bf16[3,512,256]{2,1,0:T(8,128)(2,1)S(1)}, bf16[3,512,256]{2,1,0:T(8,128)(2,1)}, u32[]{:S(2)}) %copy-start.1) | copy-done | bytes 786456
  3.0 1.0 %copy-done.2 = s32[8,3,4,8,128]{4,3,2,1,0:T(8,128)S(1)} copy-done((s32[8,3,4,8,128]{4,3,2,1,0:T(8,128)S(1)}, s32[8,3,4,8,128]{4,3,2,1,0:T(8,128)}, u32[]{:S(2)}) %copy-start.2) | copy-done | bytes 393240
  4.0 0.7 copy-done.4
  4.7 0.7 copy-done.6
  5.4 6.4 %forward.1 = (f32[3,8,1024]{2,1,0:T(8,128)S(1)}, bf16[128,256]{1,0:T(8,128)(2,1)S(1)}, bf16[128,256]{1,0:T(8,128)(2,1)S(1)}, bf16[128,256]{1,0:T(8,128)(2,1)S(1)...) custom-call(s32[3,4,8]{2,1,0:T(4,128)S(1)} %bitcast.8, ...), custom_call_target="tpu_custom_call" | custom-call | tf_op jit(solution)/shard_map/forward/pallas_call | solution.py:166
  11.8 4.0 %collective-permute-start = (bf16[128,256]{1,0:T(8,128)(2,1)S(1)}, bf16[128,256]{1,0:T(8,128)(2,1)S(1)}, u32[]{:S(2)}, u32[]{:S(2)}) collective-permute-start(bf16[128,256]{1,0:T(8,128)(2,1)S(1)} %get-tuple-element.23), channel_id=1, source_target_pairs={{0,6},{1,7},{2,4},{3,5},{4,2},{5,3},{6,0},{7,1},{8,14},{9,15},{10,... | collective-permute-start | bytes 196616 | tf_op jit(solution)/shard_map/ppermute | solution.py:302
  15.8 1.2 %collective-permute-start.2 = (bf16[128,256]{1,0:T(8,128)(2,1)S(1)}, bf16[128,256]{1,0:T(8,128)(2,1)S(1)}, u32[]{:S(2)}, u32[]{:S(2)}) collective-permute-start(bf16[128,256]{1,0:T(8,128)(2,1)S(1)} %get-tuple-element.25), channel_id=1, source_target_pairs={{0,4},{1,5},{2,6},{3,7},{4,0},{5,1},{6,2},{7,3},{8,12},{9,13},{10,... | collective-permute-start | bytes 196616 | tf_op jit(solution)/shard_map/ppermute | solution.py:302
  16.9 0.6 collective-permute-start.3
  17.5 1.7 %collective-permute-start.4 = (bf16[128,256]{1,0:T(8,128)(2,1)S(1)}, bf16[128,256]{1,0:T(8,128)(2,1)S(1)}, u32[]{:S(2)}, u32[]{:S(2)}) collective-permute-start(bf16[128,256]{1,0:T(8,128)(2,1)S(1)} %get-tuple-element.27), channel_id=1, source_target_pairs={{0,2},{1,3},{2,0},{3,1},{4,6},{5,7},{6,4},{7,5},{8,10},{9,11},{10,... | collective-permute-start | bytes 196616 | tf_op jit(solution)/shard_map/ppermute | solution.py:302
  19.2 0.1 collective-permute-start.5
  19.3 1.6 %collective-permute-done.1.refs_1_ = bf16[128,256]{1,0:T(8,128)(2,1)S(1)} collective-permute-done((bf16[128,256]{1,0:T(8,128)(2,1)S(1)}, bf16[128,256]{1,0:T(8,128)(2,1)S(1)}, u32[]{:S(2)}, u32[]{:S(2)}) %collective-permute-start.1) | collective-permute-done | bytes 65568 | tf_op jit(solution)/shard_map/ppermute | solution.py:302
  20.9 1.2 %collective-permute-done.2.refs_2_ = bf16[128,256]{1,0:T(8,128)(2,1)S(1)} collective-permute-done((bf16[128,256]{1,0:T(8,128)(2,1)S(1)}, bf16[128,256]{1,0:T(8,128)(2,1)S(1)}, u32[]{:S(2)}, u32[]{:S(2)}) %collective-permute-start.2) | collective-permute-done | bytes 65568 | tf_op jit(solution)/shard_map/ppermute | solution.py:302
  22.1 0.3 collective-permute-done.3.refs_3_
  22.4 1.0 %collective-permute-done.5.refs_5_ = bf16[128,256]{1,0:T(8,128)(2,1)S(1)} collective-permute-done((bf16[128,256]{1,0:T(8,128)(2,1)S(1)}, bf16[128,256]{1,0:T(8,128)(2,1)S(1)}, u32[]{:S(2)}, u32[]{:S(2)}) %collective-permute-start.5) | collective-permute-done | bytes 65568 | tf_op jit(solution)/shard_map/ppermute | solution.py:302
  23.4 0.8 combine.1
  24.2 2.1 %collective-permute-start.7 = (bf16[128,256]{1,0:T(8,128)(2,1)S(1)}, bf16[128,256]{1,0:T(8,128)(2,1)S(1)}, u32[]{:S(2)}, u32[]{:S(2)}) collective-permute-start(bf16[128,256]{1,0:T(8,128)(2,1)S(1)} %get-tuple-element.36.rest_7_), channel_id=1, source_target_pairs={{0,6},{1,7},{2,4},{3,5},{4,2},{5,3},{6,0},{7,1},{8,14},{9,15},{10,... | collective-permute-start | bytes 196616 | tf_op jit(solution)/shard_map/ppermute | solution.py:302
  26.3 1.5 %collective-permute-start.9 = (bf16[128,256]{1,0:T(8,128)(2,1)S(1)}, bf16[128,256]{1,0:T(8,128)(2,1)S(1)}, u32[]{:S(2)}, u32[]{:S(2)}) collective-permute-start(bf16[128,256]{1,0:T(8,128)(2,1)S(1)} %get-tuple-element.36.rest_7_), channel_id=1, source_target_pairs={{0,4},{1,5},{2,6},{3,7},{4,0},{5,1},{6,2},{7,3},{8,12},{9,13},{10,... | collective-permute-start | bytes 196616 | tf_op jit(solution)/shard_map/ppermute | solution.py:302
  27.8 0.7 collective-permute-start.10
  28.6 1.0 %collective-permute-start.11 = (bf16[128,256]{1,0:T(8,128)(2,1)S(1)}, bf16[128,256]{1,0:T(8,128)(2,1)S(1)}, u32[]{:S(2)}, u32[]{:S(2)}) collective-permute-start(bf16[128,256]{1,0:T(8,128)(2,1)S(1)} %get-tuple-element.36.rest_7_), channel_id=1, source_target_pairs={{0,2},{1,3},{2,0},{3,1},{4,6},{5,7},{6,4},{7,5},{8,10},{9,11},{10,... | collective-permute-start | bytes 196616 | tf_op jit(solution)/shard_map/ppermute | solution.py:302
  29.6 0.3 collective-permute-start.12
  29.8 1.8 %collective-permute-done.8.rest_1_ = bf16[128,256]{1,0:T(8,128)(2,1)S(1)} collective-permute-done((bf16[128,256]{1,0:T(8,128)(2,1)S(1)}, bf16[128,256]{1,0:T(8,128)(2,1)S(1)}, u32[]{:S(2)}, u32[]{:S(2)}) %collective-permute-start.8) | collective-permute-done | bytes 65568 | tf_op jit(solution)/shard_map/ppermute | solution.py:302
  31.7 0.9 %transposed.1 = (bf16[512,1024]{1,0:T(8,128)(2,1)S(1)}, f32[1024,128]{1,0:T(8,128)S(1)}, f32[1024,128]{1,0:T(8,128)S(1)}, f32[1024,128]{1,0:T(8,128)S(1)}) custom-call(bf16[1024,512]{1,0:T(8,128)(2,1)S(1)} %copy-done, f32[3,8,1024]{2,1,0:T(8,128)S(1)} %get-tuple-element.32.inv_ref), custom_call_target="tpu_custom_call" | custom-call | flops 1048576 | bytes 3145728 | tf_op jit(solution)/shard_map/transposed/pallas_call | solution.py:193
  32.6 0.1 collective-permute-done.9.rest_2_
  32.7 1.2 %collective-permute-done.10.rest_3_ = bf16[128,256]{1,0:T(8,128)(2,1)S(1)} collective-permute-done((bf16[128,256]{1,0:T(8,128)(2,1)S(1)}, bf16[128,256]{1,0:T(8,128)(2,1)S(1)}, u32[]{:S(2)}, u32[]{:S(2)}) %collective-permute-start.10) | collective-permute-done | bytes 65568 | tf_op jit(solution)/shard_map/ppermute | solution.py:302
  33.9 1.5 %gradient.4 = bf16[512,256]{1,0:T(8,128)(2,1)S(1)} custom-call(bf16[512,1024]{1,0:T(8,128)(2,1)S(1)} %get-tuple-element.33.xt_ref, bf16[1024,1024]{1,0:T(8,128)(2,1)S(1)} %get-tuple-element.37.adj_ref, f32[1024,128]{1,0:T(8,128)S(1)} %get-tuple-element.38.col_ref, bf16[128,256]{1,0:T(8,128)(2,1)S(1)} %collective-permute-done.7.rest_0_, ...), custom_call_target="tpu_custom_call" | custom-call | flops 805306368 | bytes 2883584 | tf_op jit(solution)/shard_map/gradient/pallas_call | solution.py:248
  35.5 3.8 %collective-permute-start.15 = (bf16[512,256]{1,0:T(8,128)(2,1)S(1)}, bf16[512,256]{1,0:T(8,128)(2,1)S(1)}, u32[]{:S(2)}, u32[]{:S(2)}) collective-permute-start(bf16[512,256]{1,0:T(8,128)(2,1)S(1)} %gradient.4), channel_id=1, source_target_pairs={{0,8},{24,16},{1,9},{25,17},{2,10},{26,18},{3,11},{27,19},{4,12},{... | collective-permute-start | bytes 786440 | tf_op jit(solution)/shard_map/ppermute | solution.py:275
  39.2 1.5 %gradient.5 = bf16[512,256]{1,0:T(8,128)(2,1)S(1)} custom-call(bf16[512,1024]{1,0:T(8,128)(2,1)S(1)} %get-tuple-element.33.xt_ref, bf16[1024,1024]{1,0:T(8,128)(2,1)S(1)} %get-tuple-element.41.adj_ref, f32[1024,128]{1,0:T(8,128)S(1)} %get-tuple-element.42.col_ref, bf16[128,256]{1,0:T(8,128)(2,1)S(1)} %collective-permute-done.7.rest_0_, ...), custom_call_target="tpu_custom_call" | custom-call | flops 805306368 | bytes 2883584 | tf_op jit(solution)/shard_map/gradient/pallas_call | solution.py:248
  40.7 1.3 %collective-permute-start.19 = (bf16[512,256]{1,0:T(8,128)(2,1)S(1)}, bf16[512,256]{1,0:T(8,128)(2,1)S(1)}, u32[]{:S(2)}, u32[]{:S(2)}) collective-permute-start(bf16[512,256]{1,0:T(8,128)(2,1)S(1)} %gradient.5), channel_id=1, source_target_pairs={{0,8},{24,16},{1,9},{25,17},{2,10},{26,18},{3,11},{27,19},{4,12},{... | collective-permute-start | bytes 786440 | tf_op jit(solution)/shard_map/ppermute | solution.py:275
  42.1 1.5 %gradient.3 = bf16[512,256]{1,0:T(8,128)(2,1)S(1)} custom-call(bf16[512,1024]{1,0:T(8,128)(2,1)S(1)} %get-tuple-element.33.xt_ref, bf16[1024,1024]{1,0:T(8,128)(2,1)S(1)} %get-tuple-element.34.adj_ref, f32[1024,128]{1,0:T(8,128)S(1)} %get-tuple-element.35.col_ref, bf16[128,256]{1,0:T(8,128)(2,1)S(1)} %collective-permute-done.7.rest_0_, ...), custom_call_target="tpu_custom_call" | custom-call | flops 805306368 | bytes 2883584 | tf_op jit(solution)/shard_map/gradient/pallas_call | solution.py:248
  43.6 1.3 %collective-permute-start.14 = (bf16[512,256]{1,0:T(8,128)(2,1)S(1)}, bf16[512,256]{1,0:T(8,128)(2,1)S(1)}, u32[]{:S(2)}, u32[]{:S(2)}) collective-permute-start(bf16[512,256]{1,0:T(8,128)(2,1)S(1)} %gradient.3), channel_id=1, source_target_pairs={{0,8},{24,16},{1,9},{25,17},{2,10},{26,18},{3,11},{27,19},{4,12},{... | collective-permute-start | bytes 786440 | tf_op jit(solution)/shard_map/ppermute | solution.py:275
  44.9 1.0 %collective-permute-done.15 = bf16[512,256]{1,0:T(8,128)(2,1)S(1)} collective-permute-done((bf16[512,256]{1,0:T(8,128)(2,1)S(1)}, bf16[512,256]{1,0:T(8,128)(2,1)S(1)}, u32[]{:S(2)}, u32[]{:S(2)}) %collective-permute-start.15) | collective-permute-done | bytes 262176 | tf_op jit(solution)/shard_map/ppermute | solution.py:275
  45.9 0.1 reduce-precision_convert_fusion.4
  45.9 0.7 collective-permute-start.16
  46.6 4.9 %collective-permute-done.19 = bf16[512,256]{1,0:T(8,128)(2,1)S(1)} collective-permute-done((bf16[512,256]{1,0:T(8,128)(2,1)S(1)}, bf16[512,256]{1,0:T(8,128)(2,1)S(1)}, u32[]{:S(2)}, u32[]{:S(2)}) %collective-permute-start.19) | collective-permute-done | bytes 262176 | tf_op jit(solution)/shard_map/ppermute | solution.py:275
  51.6 0.7 collective-permute-start.20
  52.2 4.0 %collective-permute-done.14 = bf16[512,256]{1,0:T(8,128)(2,1)S(1)} collective-permute-done((bf16[512,256]{1,0:T(8,128)(2,1)S(1)}, bf16[512,256]{1,0:T(8,128)(2,1)S(1)}, u32[]{:S(2)}, u32[]{:S(2)}) %collective-permute-start.14) | collective-permute-done | bytes 262176 | tf_op jit(solution)/shard_map/ppermute | solution.py:275
  56.4 0.1 reduce-precision_convert_fusion.3
  56.4 0.7 collective-permute-start.17
  57.1 1.3 %collective-permute-start.18 = (bf16[512,256]{1,0:T(8,128)(2,1)S(1)}, bf16[512,256]{1,0:T(8,128)(2,1)S(1)}, u32[]{:S(2)}, u32[]{:S(2)}) collective-permute-start(bf16[512,256]{1,0:T(8,128)(2,1)S(1)} %reduce-precision_convert_fusion.3), channel_id=1, source_target_pairs={{8,0},{16,24},{9,1},{17,25},{10,2},{18,26},{11,3},{19,27},{12,4},{... | collective-permute-start | bytes 786440 | tf_op jit(solution)/shard_map/ppermute | solution.py:290
  58.4 0.1 reduce-precision_convert_fusion
  58.5 1.3 %collective-permute-start.21 = (bf16[512,256]{1,0:T(8,128)(2,1)S(1)}, bf16[512,256]{1,0:T(8,128)(2,1)S(1)}, u32[]{:S(2)}, u32[]{:S(2)}) collective-permute-start(bf16[512,256]{1,0:T(8,128)(2,1)S(1)} %reduce-precision_convert_fusion), channel_id=1, source_target_pairs={{8,0},{16,24},{9,1},{17,25},{10,2},{18,26},{11,3},{19,27},{12,4},{... | collective-permute-start | bytes 786440 | tf_op jit(solution)/shard_map/ppermute | solution.py:290
  59.8 0.1 reduce-precision_convert_fusion.2
  59.9 11.0 %collective-permute-done.18 = bf16[512,256]{1,0:T(8,128)(2,1)S(1)} collective-permute-done((bf16[512,256]{1,0:T(8,128)(2,1)S(1)}, bf16[512,256]{1,0:T(8,128)(2,1)S(1)}, u32[]{:S(2)}, u32[]{:S(2)}) %collective-permute-start.18) | collective-permute-done | bytes 262176 | tf_op jit(solution)/shard_map/ppermute | solution.py:290
  70.9 1.3 %collective-permute-start.22 = (bf16[512,256]{1,0:T(8,128)(2,1)S(1)}, bf16[512,256]{1,0:T(8,128)(2,1)S(1)}, u32[]{:S(2)}, u32[]{:S(2)}) collective-permute-start(bf16[512,256]{1,0:T(8,128)(2,1)S(1)} %reduce-precision_convert_fusion.2), channel_id=1, source_target_pairs={{8,0},{16,24},{9,1},{17,25},{10,2},{18,26},{11,3},{19,27},{12,4},{... | collective-permute-start | bytes 786440 | tf_op jit(solution)/shard_map/ppermute | solution.py:290
  72.2 4.3 %collective-permute-done.21 = bf16[512,256]{1,0:T(8,128)(2,1)S(1)} collective-permute-done((bf16[512,256]{1,0:T(8,128)(2,1)S(1)}, bf16[512,256]{1,0:T(8,128)(2,1)S(1)}, u32[]{:S(2)}, u32[]{:S(2)}) %collective-permute-start.21) | collective-permute-done | bytes 262176 | tf_op jit(solution)/shard_map/ppermute | solution.py:290
  76.6 3.8 %collective-permute-done.22 = bf16[512,256]{1,0:T(8,128)(2,1)S(1)} collective-permute-done((bf16[512,256]{1,0:T(8,128)(2,1)S(1)}, bf16[512,256]{1,0:T(8,128)(2,1)S(1)}, u32[]{:S(2)}, u32[]{:S(2)}) %collective-permute-start.22) | collective-permute-done | bytes 262176 | tf_op jit(solution)/shard_map/ppermute | solution.py:290
  80.4 1.3 %maximum_convert_fusion = f32[3,512,256]{2,1,0:T(8,128)} fusion(bf16[1,512,256]{2,1,0:T(8,128)(2,1)S(1)} %select_bitcast_fusion, bf16[1,512,256]{2,1,0:T(8,128)(2,1)S(1)} %select_bitcast_fusion.1, bf16[1,512,256]{2,1,0:T(8,128)(2,1)S(1)} %bitcast.11), kind=kLoop, calls=%fused_computation | loop fusion | flops 1179648 | bytes 2359296 | tf_op jit(solution)/shard_map/stack | solution.py:331
  (30 shorter events, 0.4 us)
Async XLA Ops:
  0.6 22.8 %copy-start.7 = (s32[128]{0:T(128)S(1)}, s32[128]{0:T(128)}, u32[]{:S(2)}) copy-start(s32[128]{0:T(128)} %param.13) | copy-start | bytes 1540
  0.6 1.2 %copy-start = (bf16[1024,512]{1,0:T(8,128)(2,1)S(1)}, bf16[1024,512]{1,0:T(8,128)(2,1)}, u32[]{:S(2)}) copy-start(bf16[1024,512]{1,0:T(8,128)(2,1)} %x_ref.3) | copy-start | bytes 3145732
  1.9 1.1 %copy-start.1 = (bf16[3,512,256]{2,1,0:T(8,128)(2,1)S(1)}, bf16[3,512,256]{2,1,0:T(8,128)(2,1)}, u32[]{:S(2)}) copy-start(bf16[3,512,256]{2,1,0:T(8,128)(2,1)} %w_ref.1) | copy-start | bytes 2359300
  3.0 1.0 %copy-start.2 = (s32[8,3,4,8,128]{4,3,2,1,0:T(8,128)S(1)}, s32[8,3,4,8,128]{4,3,2,1,0:T(8,128)}, u32[]{:S(2)}) copy-start(s32[8,3,4,8,128]{4,3,2,1,0:T(8,128)} %pat_ref.1) | copy-start | bytes 1179652
  4.0 0.7 copy-start.4
  4.7 0.7 copy-start.6
  5.4 18.0 %copy-start.3 = (bf16[128,256]{1,0:T(8,128)(2,1)S(1)}, bf16[128,256]{1,0:T(8,128)(2,1)}, u32[]{:S(2)}) copy-start(bf16[128,256]{1,0:T(8,128)(2,1)} %refs_10_.1) | copy-start | bytes 196612
  5.4 18.0 %copy-start.5 = (f32[3,256]{1,0:T(4,128)S(1)}, f32[3,256]{1,0:T(4,128)}, u32[]{:S(2)}) copy-start(f32[3,256]{1,0:T(4,128)} %refs_9_.1) | copy-start | bytes 9220
  11.8 7.4 %collective-permute-start = (bf16[128,256]{1,0:T(8,128)(2,1)S(1)}, bf16[128,256]{1,0:T(8,128)(2,1)S(1)}, u32[]{:S(2)}, u32[]{:S(2)}) collective-permute-start(bf16[128,256]{1,0:T(8,128)(2,1)S(1)} %get-tuple-element.23), channel_id=1, source_target_pairs={{0,6},{1,7},{2,4},{3,5},{4,2},{5,3},{6,0},{7,1},{8,14},{9,15},{10,... | collective-permute-start | bytes 196616 | tf_op jit(solution)/shard_map/ppermute | solution.py:302
  15.8 5.1 %collective-permute-start.1 = (bf16[128,256]{1,0:T(8,128)(2,1)S(1)}, bf16[128,256]{1,0:T(8,128)(2,1)S(1)}, u32[]{:S(2)}, u32[]{:S(2)}) collective-permute-start(bf16[128,256]{1,0:T(8,128)(2,1)S(1)} %get-tuple-element.24), channel_id=1, source_target_pairs={{0,7},{1,6},{2,5},{3,4},{4,3},{5,2},{6,1},{7,0},{8,15},{9,14},{10,... | collective-permute-start | bytes 196616 | tf_op jit(solution)/shard_map/ppermute | solution.py:302
  15.8 6.3 %collective-permute-start.2 = (bf16[128,256]{1,0:T(8,128)(2,1)S(1)}, bf16[128,256]{1,0:T(8,128)(2,1)S(1)}, u32[]{:S(2)}, u32[]{:S(2)}) collective-permute-start(bf16[128,256]{1,0:T(8,128)(2,1)S(1)} %get-tuple-element.25), channel_id=1, source_target_pairs={{0,4},{1,5},{2,6},{3,7},{4,0},{5,1},{6,2},{7,3},{8,12},{9,13},{10,... | collective-permute-start | bytes 196616 | tf_op jit(solution)/shard_map/ppermute | solution.py:302
  16.9 5.4 %collective-permute-start.3 = (bf16[128,256]{1,0:T(8,128)(2,1)S(1)}, bf16[128,256]{1,0:T(8,128)(2,1)S(1)}, u32[]{:S(2)}, u32[]{:S(2)}) collective-permute-start(bf16[128,256]{1,0:T(8,128)(2,1)S(1)} %get-tuple-element.26), channel_id=1, source_target_pairs={{0,5},{1,4},{2,7},{3,6},{4,1},{5,0},{6,3},{7,2},{8,13},{9,12},{10,... | collective-permute-start | bytes 196616 | tf_op jit(solution)/shard_map/ppermute | solution.py:302
  17.5 4.9 %collective-permute-start.4 = (bf16[128,256]{1,0:T(8,128)(2,1)S(1)}, bf16[128,256]{1,0:T(8,128)(2,1)S(1)}, u32[]{:S(2)}, u32[]{:S(2)}) collective-permute-start(bf16[128,256]{1,0:T(8,128)(2,1)S(1)} %get-tuple-element.27), channel_id=1, source_target_pairs={{0,2},{1,3},{2,0},{3,1},{4,6},{5,7},{6,4},{7,5},{8,10},{9,11},{10,... | collective-permute-start | bytes 196616 | tf_op jit(solution)/shard_map/ppermute | solution.py:302
  19.2 4.2 %collective-permute-start.5 = (bf16[128,256]{1,0:T(8,128)(2,1)S(1)}, bf16[128,256]{1,0:T(8,128)(2,1)S(1)}, u32[]{:S(2)}, u32[]{:S(2)}) collective-permute-start(bf16[128,256]{1,0:T(8,128)(2,1)S(1)} %get-tuple-element.28), channel_id=1, source_target_pairs={{0,3},{1,2},{2,1},{3,0},{4,7},{5,6},{6,5},{7,4},{8,11},{9,10},{10,... | collective-permute-start | bytes 196616 | tf_op jit(solution)/shard_map/ppermute | solution.py:302
  20.9 2.5 %collective-permute-start.6 = (bf16[128,256]{1,0:T(8,128)(2,1)S(1)}, bf16[128,256]{1,0:T(8,128)(2,1)S(1)}, u32[]{:S(2)}, u32[]{:S(2)}) collective-permute-start(bf16[128,256]{1,0:T(8,128)(2,1)S(1)} %get-tuple-element.29), channel_id=1, source_target_pairs={{0,1},{1,0},{2,3},{3,2},{4,5},{5,4},{6,7},{7,6},{8,9},{9,8},{10,11... | collective-permute-start | bytes 196616 | tf_op jit(solution)/shard_map/ppermute | solution.py:302
  24.2 5.4 %collective-permute-start.7 = (bf16[128,256]{1,0:T(8,128)(2,1)S(1)}, bf16[128,256]{1,0:T(8,128)(2,1)S(1)}, u32[]{:S(2)}, u32[]{:S(2)}) collective-permute-start(bf16[128,256]{1,0:T(8,128)(2,1)S(1)} %get-tuple-element.36.rest_7_), channel_id=1, source_target_pairs={{0,6},{1,7},{2,4},{3,5},{4,2},{5,3},{6,0},{7,1},{8,14},{9,15},{10,... | collective-permute-start | bytes 196616 | tf_op jit(solution)/shard_map/ppermute | solution.py:302
  26.3 5.3 %collective-permute-start.8 = (bf16[128,256]{1,0:T(8,128)(2,1)S(1)}, bf16[128,256]{1,0:T(8,128)(2,1)S(1)}, u32[]{:S(2)}, u32[]{:S(2)}) collective-permute-start(bf16[128,256]{1,0:T(8,128)(2,1)S(1)} %get-tuple-element.36.rest_7_), channel_id=1, source_target_pairs={{0,7},{1,6},{2,5},{3,4},{4,3},{5,2},{6,1},{7,0},{8,15},{9,14},{10,... | collective-permute-start | bytes 196616 | tf_op jit(solution)/shard_map/ppermute | solution.py:302
  26.3 6.4 %collective-permute-start.9 = (bf16[128,256]{1,0:T(8,128)(2,1)S(1)}, bf16[128,256]{1,0:T(8,128)(2,1)S(1)}, u32[]{:S(2)}, u32[]{:S(2)}) collective-permute-start(bf16[128,256]{1,0:T(8,128)(2,1)S(1)} %get-tuple-element.36.rest_7_), channel_id=1, source_target_pairs={{0,4},{1,5},{2,6},{3,7},{4,0},{5,1},{6,2},{7,3},{8,12},{9,13},{10,... | collective-permute-start | bytes 196616 | tf_op jit(solution)/shard_map/ppermute | solution.py:302
  27.8 6.1 %collective-permute-start.10 = (bf16[128,256]{1,0:T(8,128)(2,1)S(1)}, bf16[128,256]{1,0:T(8,128)(2,1)S(1)}, u32[]{:S(2)}, u32[]{:S(2)}) collective-permute-start(bf16[128,256]{1,0:T(8,128)(2,1)S(1)} %get-tuple-element.36.rest_7_), channel_id=1, source_target_pairs={{0,5},{1,4},{2,7},{3,6},{4,1},{5,0},{6,3},{7,2},{8,13},{9,12},{10,... | collective-permute-start | bytes 196616 | tf_op jit(solution)/shard_map/ppermute | solution.py:302
  28.6 5.4 %collective-permute-start.11 = (bf16[128,256]{1,0:T(8,128)(2,1)S(1)}, bf16[128,256]{1,0:T(8,128)(2,1)S(1)}, u32[]{:S(2)}, u32[]{:S(2)}) collective-permute-start(bf16[128,256]{1,0:T(8,128)(2,1)S(1)} %get-tuple-element.36.rest_7_), channel_id=1, source_target_pairs={{0,2},{1,3},{2,0},{3,1},{4,6},{5,7},{6,4},{7,5},{8,10},{9,11},{10,... | collective-permute-start | bytes 196616 | tf_op jit(solution)/shard_map/ppermute | solution.py:302
  29.6 4.4 %collective-permute-start.12 = (bf16[128,256]{1,0:T(8,128)(2,1)S(1)}, bf16[128,256]{1,0:T(8,128)(2,1)S(1)}, u32[]{:S(2)}, u32[]{:S(2)}) collective-permute-start(bf16[128,256]{1,0:T(8,128)(2,1)S(1)} %get-tuple-element.36.rest_7_), channel_id=1, source_target_pairs={{0,3},{1,2},{2,1},{3,0},{4,7},{5,6},{6,5},{7,4},{8,11},{9,10},{10,... | collective-permute-start | bytes 196616 | tf_op jit(solution)/shard_map/ppermute | solution.py:302
  31.6 2.3 %collective-permute-start.13 = (bf16[128,256]{1,0:T(8,128)(2,1)S(1)}, bf16[128,256]{1,0:T(8,128)(2,1)S(1)}, u32[]{:S(2)}, u32[]{:S(2)}) collective-permute-start(bf16[128,256]{1,0:T(8,128)(2,1)S(1)} %get-tuple-element.36.rest_7_), channel_id=1, source_target_pairs={{0,1},{1,0},{2,3},{3,2},{4,5},{5,4},{6,7},{7,6},{8,9},{9,8},{10,11... | collective-permute-start | bytes 196616 | tf_op jit(solution)/shard_map/ppermute | solution.py:302
  35.5 10.4 %collective-permute-start.15 = (bf16[512,256]{1,0:T(8,128)(2,1)S(1)}, bf16[512,256]{1,0:T(8,128)(2,1)S(1)}, u32[]{:S(2)}, u32[]{:S(2)}) collective-permute-start(bf16[512,256]{1,0:T(8,128)(2,1)S(1)} %gradient.4), channel_id=1, source_target_pairs={{0,8},{24,16},{1,9},{25,17},{2,10},{26,18},{3,11},{27,19},{4,12},{... | collective-permute-start | bytes 786440 | tf_op jit(solution)/shard_map/ppermute | solution.py:275
  40.7 10.7 %collective-permute-start.19 = (bf16[512,256]{1,0:T(8,128)(2,1)S(1)}, bf16[512,256]{1,0:T(8,128)(2,1)S(1)}, u32[]{:S(2)}, u32[]{:S(2)}) collective-permute-start(bf16[512,256]{1,0:T(8,128)(2,1)S(1)} %gradient.5), channel_id=1, source_target_pairs={{0,8},{24,16},{1,9},{25,17},{2,10},{26,18},{3,11},{27,19},{4,12},{... | collective-permute-start | bytes 786440 | tf_op jit(solution)/shard_map/ppermute | solution.py:275
  43.6 12.7 %collective-permute-start.14 = (bf16[512,256]{1,0:T(8,128)(2,1)S(1)}, bf16[512,256]{1,0:T(8,128)(2,1)S(1)}, u32[]{:S(2)}, u32[]{:S(2)}) collective-permute-start(bf16[512,256]{1,0:T(8,128)(2,1)S(1)} %gradient.3), channel_id=1, source_target_pairs={{0,8},{24,16},{1,9},{25,17},{2,10},{26,18},{3,11},{27,19},{4,12},{... | collective-permute-start | bytes 786440 | tf_op jit(solution)/shard_map/ppermute | solution.py:275
  45.9 10.4 %collective-permute-start.16 = (bf16[512,256]{1,0:T(8,128)(2,1)S(1)}, bf16[512,256]{1,0:T(8,128)(2,1)S(1)}, u32[]{:S(2)}, u32[]{:S(2)}) collective-permute-start(bf16[512,256]{1,0:T(8,128)(2,1)S(1)} %reduce-precision_convert_fusion.4), channel_id=1, source_target_pairs={{8,16},{16,8},{9,17},{17,9},{10,18},{18,10},{11,19},{19,11},{12,20... | collective-permute-start | bytes 786440 | tf_op jit(solution)/shard_map/ppermute | solution.py:282
  51.6 6.9 %collective-permute-start.20 = (bf16[512,256]{1,0:T(8,128)(2,1)S(1)}, bf16[512,256]{1,0:T(8,128)(2,1)S(1)}, u32[]{:S(2)}, u32[]{:S(2)}) collective-permute-start(bf16[512,256]{1,0:T(8,128)(2,1)S(1)} %reduce-precision_convert_fusion.1), channel_id=1, source_target_pairs={{8,16},{16,8},{9,17},{17,9},{10,18},{18,10},{11,19},{19,11},{12,20... | collective-permute-start | bytes 786440 | tf_op jit(solution)/shard_map/ppermute | solution.py:282
  56.4 3.4 %collective-permute-start.17 = (bf16[512,256]{1,0:T(8,128)(2,1)S(1)}, bf16[512,256]{1,0:T(8,128)(2,1)S(1)}, u32[]{:S(2)}, u32[]{:S(2)}) collective-permute-start(bf16[512,256]{1,0:T(8,128)(2,1)S(1)} %reduce-precision_convert_fusion.5), channel_id=1, source_target_pairs={{8,16},{16,8},{9,17},{17,9},{10,18},{18,10},{11,19},{19,11},{12,20... | collective-permute-start | bytes 786440 | tf_op jit(solution)/shard_map/ppermute | solution.py:282
  57.1 13.8 %collective-permute-start.18 = (bf16[512,256]{1,0:T(8,128)(2,1)S(1)}, bf16[512,256]{1,0:T(8,128)(2,1)S(1)}, u32[]{:S(2)}, u32[]{:S(2)}) collective-permute-start(bf16[512,256]{1,0:T(8,128)(2,1)S(1)} %reduce-precision_convert_fusion.3), channel_id=1, source_target_pairs={{8,0},{16,24},{9,1},{17,25},{10,2},{18,26},{11,3},{19,27},{12,4},{... | collective-permute-start | bytes 786440 | tf_op jit(solution)/shard_map/ppermute | solution.py:290
  58.5 18.0 %collective-permute-start.21 = (bf16[512,256]{1,0:T(8,128)(2,1)S(1)}, bf16[512,256]{1,0:T(8,128)(2,1)S(1)}, u32[]{:S(2)}, u32[]{:S(2)}) collective-permute-start(bf16[512,256]{1,0:T(8,128)(2,1)S(1)} %reduce-precision_convert_fusion), channel_id=1, source_target_pairs={{8,0},{16,24},{9,1},{17,25},{10,2},{18,26},{11,3},{19,27},{12,4},{... | collective-permute-start | bytes 786440 | tf_op jit(solution)/shard_map/ppermute | solution.py:290
  70.9 9.5 %collective-permute-start.22 = (bf16[512,256]{1,0:T(8,128)(2,1)S(1)}, bf16[512,256]{1,0:T(8,128)(2,1)S(1)}, u32[]{:S(2)}, u32[]{:S(2)}) collective-permute-start(bf16[512,256]{1,0:T(8,128)(2,1)S(1)} %reduce-precision_convert_fusion.2), channel_id=1, source_target_pairs={{8,0},{16,24},{9,1},{17,25},{10,2},{18,26},{11,3},{19,27},{12,4},{... | collective-permute-start | bytes 786440 | tf_op jit(solution)/shard_map/ppermute | solution.py:290
where the time goes:
time: 82.1 us; the launch traced here: 81.7 us
  waiting for transfers between devices  36.3 us (44%)
  starting transfers between devices  25.5 us (31%)
  Pallas kernels  12.6 us (15%)
  local copies, waits for them, and re-layouts  4.74 us (6%)
  other arithmetic  1.76 us (2%)
  between operations  0.86 us (1%)
    ppermute x3, waiting for transfers between devices, chain_sum(): got = lax.ppermute(sent, 'dom', [(low, low - 1), (high, high + 1)])  19.1 us
    ppermute x14, starting transfers between devices, exchange(): lax.ppermute(value_of(k), 'feat', [(i, i ^ k) for i in range(n_feat)])  13.2 us
    ppermute x3, waiting for transfers between devices, chain_sum(): got = lax.ppermute(sent, 'dom', perm)  9.88 us
    ppermute x14, waiting for transfers between devices, exchange(): lax.ppermute(value_of(k), 'feat', [(i, i ^ k) for i in range(n_feat)])  7.26 us
    pallas_call x1, Pallas kernels, forward(): pl.pallas_call(functools.partial(forward_kernel, n_feat), name='forward',...  6.4 us
    ppermute x3, starting transfers between devices, chain_sum(): got = lax.ppermute(sent, 'dom', perm)  6.36 us
    unnamed x16, local copies, waits for them, and re-layouts  4.74 us
    pallas_call x3, Pallas kernels, gradient(): pl.pallas_call(functools.partial(gradient_kernel, len(slopes)), name='gra...  4.54 us
  transfers between devices with their start and end apart: 23, of which 13 were waited for; matrix products, arithmetic and copies ran while one was open for 1% of the time, Pallas kernels for 5%

commit v1 on v0

--- a/solution.py
+++ b/solution.py
@@ -129,19 +129,41 @@
         inv_ref[relation, 0:1, b * BLK : (b + 1) * BLK] = 1.0 / (1.0 + total)
 
 
-def forward_kernel(n_feat, src_ref, cnt_ref, pat_ref, x_ref, w_ref, inv_ref, *rest):
-    relations, slots, blocks = src_ref.shape
-    piece_refs, adj_refs = rest[:n_feat], rest[n_feat : n_feat + relations]
-    pre_ref = rest[n_feat + relations]
-    places = [
-        [(adj_ref, slice(b * BLK, (b + 1) * BLK)) for b in range(blocks)] for adj_ref in adj_refs
-    ]
-
+def adjacency_kernel(src_ref, cnt_ref, pat_ref, inv_ref, *adj_refs):
+    blocks = src_ref.shape[2]
+    for relation, adj_ref in enumerate(adj_refs):
+        places = [(adj_ref, slice(b * BLK, (b + 1) * BLK)) for b in range(blocks)]
+        start_adjacency(places)
+        inverse_degrees(relation, inv_ref, src_ref, cnt_ref, pat_ref)
+        add_edges(relation, places, src_ref, cnt_ref, pat_ref)
+
+
+def adjacency(source_block, slot_count, block_pattern):
+    relations, _, blocks = source_block.shape
+    nodes = blocks * BLK
+    smem = pl.BlockSpec(memory_space=pltpu.SMEM)
+    vmem = pl.BlockSpec(memory_space=pltpu.VMEM)
+    inv_deg, *adj = pl.pallas_call(
+        adjacency_kernel,
+        name="adjacency",
+        out_shape=[jax.ShapeDtypeStruct((relations, 8, nodes), F32)]
+        + [jax.ShapeDtypeStruct((nodes, nodes), BF16)] * relations,
+        in_specs=[smem, smem, vmem],
+        out_specs=[vmem] * (1 + relations),
+        compiler_params=pltpu.CompilerParams(vmem_limit_bytes=16 * MIB),
+        cost_estimate=pl.CostEstimate(
+            flops=1000 * relations * nodes * nodes,
+            bytes_accessed=2 * relations * nodes * nodes,
+            transcendentals=0,
+        ),
+    )(source_block, slot_count, block_pattern)
+    return inv_deg, adj
+
+
+def forward_kernel(n_feat, relations, inv_ref, *refs):
+    adj_refs, refs = refs[:relations], refs[relations:]
+    x_ref, w_ref, piece_refs, pre_ref = refs[0], refs[1], refs[2:-1], refs[-1]
     for relation in range(relations):
-        start_adjacency(places[relation])
-    for relation in range(relations):
-        inverse_degrees(relation, inv_ref, src_ref, cnt_ref, pat_ref)
-        add_edges(relation, places[relation], src_ref, cnt_ref, pat_ref)
         y_t = lax.dot_general(
             w_ref[relation].T, x_ref[...], (((1,), (1,)), ((), ())), preferred_element_type=F32
         ).astype(BF16)
@@ -158,23 +180,24 @@
         piece[...] = pre_ref[:, pl.ds(first, BLK)].T.astype(BF16)
 
 
-def forward(features, proj_weight, source_block, slot_count, block_pattern, n_feat):
+def forward(inv_deg, adj, features, proj_weight, n_feat):
     nodes, cols = features.shape
     relations, _, hidden = proj_weight.shape
-    smem = pl.BlockSpec(memory_space=pltpu.SMEM)
     vmem = pl.BlockSpec(memory_space=pltpu.VMEM)
-    inv_deg, *out = pl.pallas_call(
-        functools.partial(forward_kernel, n_feat),
+    return pl.pallas_call(
+        functools.partial(forward_kernel, n_feat, relations),
         name="forward",
-        out_shape=[jax.ShapeDtypeStruct((relations, 8, nodes), F32)]
-        + [jax.ShapeDtypeStruct((nodes // n_feat, hidden), BF16)] * n_feat
-        + [jax.ShapeDtypeStruct((nodes, nodes), BF16)] * relations,
-        in_specs=[smem, smem, vmem, vmem, vmem],
-        out_specs=[vmem] * (1 + n_feat + relations),
+        out_shape=[jax.ShapeDtypeStruct((nodes // n_feat, hidden), BF16)] * n_feat,
+        in_specs=[vmem] * (3 + relations),
+        out_specs=[vmem] * n_feat,
         scratch_shapes=[pltpu.VMEM((hidden, nodes), F32)],
-        compiler_params=pltpu.CompilerParams(vmem_limit_bytes=24 * MIB),
-    )(source_block, slot_count, block_pattern, features, proj_weight)
-    return inv_deg, out[:n_feat], out[n_feat:]
+        compiler_params=pltpu.CompilerParams(vmem_limit_bytes=16 * MIB),
+        cost_estimate=pl.CostEstimate(
+            flops=2 * relations * nodes * hidden * (nodes + cols),
+            bytes_accessed=2 * relations * nodes * nodes,
+            transcendentals=0,
+        ),
+    )(inv_deg, *adj, features, proj_weight)
 
 
 def transposed_kernel(x_ref, inv_ref, xt_ref, *col_refs):
@@ -230,27 +253,29 @@
 
 
 def gradient_kernel(n_feat, xt_ref, adj_ref, col_ref, *rest):
-    sent_ref, scaled_ref = rest[n_feat:]
+    sent_refs, scaled_ref = rest[n_feat:-1], rest[-1]
     me = lax.axis_index("feat")
     for k, piece in zip(ORDER, rest[:n_feat]):
         rows = pl.ds(pl.multiple_of((me ^ k) * BLK, BLK), BLK)
         inv = jnp.concatenate([col_ref[rows, :]] * (piece.shape[1] // BLK), axis=1)
         scaled_ref[rows, :] = (piece[...].astype(F32) * inv).astype(BF16)
     spread = jnp.dot(adj_ref[...], scaled_ref[...], preferred_element_type=F32).astype(BF16)
-    grad = jnp.dot(xt_ref[...], spread, preferred_element_type=F32)
-    sent_ref[...] = grad.astype(BF16)
-
-
-def gradient(x_t, adj, col, slopes):
+    rows = xt_ref.shape[0] // len(sent_refs)
+    for i, sent_ref in enumerate(sent_refs):
+        x_t = xt_ref[i * rows : (i + 1) * rows, :]
+        sent_ref[...] = jnp.dot(x_t, spread, preferred_element_type=F32).astype(BF16)
+
+
+def gradient(parts, x_t, adj, col, slopes):
     cols, nodes = x_t.shape
     hidden = slopes[0].shape[1]
     vmem = pl.BlockSpec(memory_space=pltpu.VMEM)
     return pl.pallas_call(
         functools.partial(gradient_kernel, len(slopes)),
         name="gradient",
-        out_shape=jax.ShapeDtypeStruct((cols, hidden), BF16),
+        out_shape=[jax.ShapeDtypeStruct((cols // parts, hidden), BF16)] * parts,
         in_specs=[vmem] * (3 + len(slopes)),
-        out_specs=vmem,
+        out_specs=[vmem] * parts,
         scratch_shapes=[pltpu.VMEM((nodes, hidden), BF16)],
         compiler_params=pltpu.CompilerParams(vmem_limit_bytes=8 * MIB),
         cost_estimate=pl.CostEstimate(
@@ -261,15 +286,41 @@
     )(x_t, adj, col, *slopes)
 
 
+def finish_kernel(n_dom, got_ref, sent_ref, *rest):
+    at = lax.axis_index("dom")
+    received = jnp.where((at == 0) | (at == n_dom - 1), 1.0, 0.0)
+    got, sent = got_ref[...].astype(F32), sent_ref[...].astype(F32)
+    rest[-1][0] = jnp.where(jnp.full(got.shape, received) > 0.5, got, sent)
+
+
+def finish(place, shape, n_dom, got, sent, out):
+    rows, cols = got.shape
+    block = pl.BlockSpec((rows, cols), lambda i: (0, 0))
+    before = [] if out is None else [out]
+    return pl.pallas_call(
+        functools.partial(finish_kernel, n_dom),
+        name="finish",
+        grid=(1,),
+        out_shape=jax.ShapeDtypeStruct(shape, F32),
+        in_specs=[block, block] + [pl.BlockSpec(memory_space=pl.ANY)] * len(before),
+        out_specs=pl.BlockSpec((1, rows, cols), lambda i: (*place, 0)),
+        input_output_aliases={2: 0} if before else {},
+        compiler_params=pltpu.CompilerParams(vmem_limit_bytes=8 * MIB),
+        cost_estimate=pl.CostEstimate(
+            flops=2000000000, bytes_accessed=8 * rows * cols, transcendentals=0
+        ),
+    )(got, sent, *before)
+
+
 def rounded(x):
     return lax.reduce_precision(x, 8, 7)
 
 
-def chain_sum(chunks, n_dom):
+def chain_sum(chunks, n_dom, shape):
     half = n_dom // 2
     at = lax.axis_index("dom")
     inner = []
-    for sent in chunks:
+    for _, sent in chunks:
         for hop in range(half - 1):
             perm = [(hop, hop + 1), (n_dom - 1 - hop, n_dom - 2 - hop)]
             got = lax.ppermute(sent, "dom", perm)
@@ -281,16 +332,16 @@
             sent, _ = lax.optimization_barrier((sent, middle[i - 2]))
         got = lax.ppermute(sent, "dom", [(half - 1, half), (half, half - 1)])
         middle.append(rounded(sent.astype(F32) + got.astype(F32)).astype(BF16))
-    outer = []
+    out = None
     for i, sent in enumerate(middle):
-        if i >= 2:
-            sent, outer[i - 2] = lax.optimization_barrier((sent, outer[i - 2]))
+        got = sent
         for hop in range(half - 1):
             low, high = half - 1 - hop, half + hop
+            if hop:
+                sent = jnp.where((at < low + 1) | (at > high - 1), got, sent)
             got = lax.ppermute(sent, "dom", [(low, low - 1), (high, high + 1)])
-            sent = jnp.where((at < low) | (at > high), got, sent)
-        outer.append(sent)
-    return [sent.astype(F32) for sent in outer]
+        out = finish(chunks[i][0], shape, n_dom, got, sent, out)
+    return out
 
 
 ORDER = (6, 7, 4, 5, 2, 3, 1, 0)
@@ -317,18 +368,19 @@
 ):
     source_block = jnp.transpose(source_block, (1, 2, 0))
     slot_count = jnp.transpose(slot_count, (1, 0))
-    inv_deg, pieces, adj = forward(
-        features, proj_weight, source_block, slot_count, block_pattern, n_feat
-    )
+    inv_deg, adj = adjacency(source_block, slot_count, block_pattern)
+    pieces = forward(inv_deg, adj, features, proj_weight, n_feat)
     received = exchange(lambda k: pieces[k], n_feat)
     x_t, col = transposed(features, inv_deg)
     activations, slope = combine(received, node_type, type_gain, cotangent)
     slopes = exchange(lambda k: slope, n_feat)
-    chunks = [
-        gradient(x_t, adj[relation], col[relation], slopes)
-        for relation in range(proj_weight.shape[0])
-    ]
-    return activations, jnp.stack(chain_sum(chunks, n_dom))
+    chunks = []
+    for relation in range(proj_weight.shape[0]):
+        parts = 2 if relation == 0 else 1
+        made = gradient(parts, x_t, adj[relation], col[relation], slopes)
+        chunks += [((relation, i), chunk) for i, chunk in enumerate(made)]
+    shape = (proj_weight.shape[0], features.shape[1], proj_weight.shape[2])
+    return activations, chain_sum(chunks, n_dom, shape)
 
 
 def body(n_dom, n_feat, *args):

time: 82.1 us -> 80.8 us (0.984)
  waiting for transfers between devices: 36.3 us -> 30.7 us
  starting transfers between devices: 25.5 us -> 29.6 us
  Pallas kernels: 12.6 us -> 16.4 us
  local copies, waits for them, and re-layouts: 4.74 us -> 2.39 us
  other arithmetic: 1.76 us -> 0.42 us
    ppermute x3 -> x4, waiting for transfers between devices: 9.88 us -> 4.69 us  [chain_sum(): got = lax.ppermute(sent, 'dom', perm)]
    pallas_call x1 -> x6, Pallas kernels: 6.4 us -> 10.2 us  [the longest x1 4.11 us: adjacency(): pl.pallas_call(adjacency_kernel, name='adjacency', out_shape=[jax.ShapeDt...]
    unnamed x16, local copies, waits for them, and re-layouts: 4.74 us -> 2.39 us
    ppermute x3 -> x4, starting transfers between devices: 6.36 us -> 7.71 us  [chain_sum(): got = lax.ppermute(sent, 'dom', perm)]
    another operation x3 -> x0, other arithmetic: 1.34 us -> none  [dense_body(): return (activations, jnp.stack(chain_sum(chunks, n_dom)))]
    ppermute x3 -> x4, starting transfers between devices: 3.88 us -> 5.17 us  [chain_sum(): got = lax.ppermute(sent, 'dom', [(low, low - 1), (high, high + 1)])]
    ppermute x3 -> x4, waiting for transfers between devices: 19.1 us -> 18.4 us  [chain_sum(): got = lax.ppermute(sent, 'dom', [(low, low - 1), (high, high + 1)])]
    ppermute x3 -> x4, starting transfers between devices: 2.03 us -> 2.69 us  [chain_sum(): got = lax.ppermute(sent, 'dom', [(half - 1, half), (half, half - 1)])]
  transfers between devices with their start and end apart: 23 -> 26, of which waited for: 13 -> 10; matrix products, arithmetic and copies ran while one was open for 1% -> 1% of each run, Pallas kernels for 5% -> 8%
where the time goes in v1:
time: 80.8 us; the launch traced here: 80.4 us
  waiting for transfers between devices  30.7 us (38%)
  starting transfers between devices  29.6 us (37%)
  Pallas kernels  16.4 us (20%)
  local copies, waits for them, and re-layouts  2.39 us (3%)
  between operations  0.96 us (1%)
    ppermute x4, waiting for transfers between devices, chain_sum(): got = lax.ppermute(sent, 'dom', [(low, low - 1), (high, high + 1)])  18.4 us
    ppermute x14, starting transfers between devices, exchange(): lax.ppermute(value_of(k), 'feat', [(i, i ^ k) for i in range(n_feat)])  14 us
    ppermute x4, starting transfers between devices, chain_sum(): got = lax.ppermute(sent, 'dom', perm)  7.71 us
    ppermute x14, waiting for transfers between devices, exchange(): lax.ppermute(value_of(k), 'feat', [(i, i ^ k) for i in range(n_feat)])  7.6 us
    ppermute x4, starting transfers between devices, chain_sum(): got = lax.ppermute(sent, 'dom', [(low, low - 1), (high, high + 1)])  5.17 us
    ppermute x4, waiting for transfers between devices, chain_sum(): got = lax.ppermute(sent, 'dom', perm)  4.69 us
    pallas_call x3, Pallas kernels, gradient(): pl.pallas_call(functools.partial(gradient_kernel, len(slopes)), name='gra...  4.54 us
    pallas_call x1, Pallas kernels, adjacency(): pl.pallas_call(adjacency_kernel, name='adjacency', out_shape=[jax.ShapeDt...  4.11 us
  transfers between devices with their start and end apart: 26, of which 10 were waited for; matrix products, arithmetic and copies ran while one was open for 1% of the time, Pallas kernels for 8%

profile of v1, /device:TPU:0, one launch (start us, length us, event | category | flops | bytes accessed | tf_op | source)
XLA Modules:
  0.0 80.4 jit_solution(9288421506978737557)
XLA Ops:
  0.6 1.0 %copy-done.5 = s32[8,3,4,8,128]{4,3,2,1,0:T(8,128)S(1)} copy-done((s32[8,3,4,8,128]{4,3,2,1,0:T(8,128)S(1)}, s32[8,3,4,8,128]{4,3,2,1,0:T(8,128)}, u32[]{:S(2)}) %copy-start.5) | copy-done | bytes 393240
  1.6 0.7 copy-done.6
  2.3 0.7 copy-done.7
  3.0 4.1 %adjacency.1 = (f32[3,8,1024]{2,1,0:T(8,128)S(1)}, bf16[1024,1024]{1,0:T(8,128)(2,1)S(1)}, bf16[1024,1024]{1,0:T(8,128)(2,1)S(1)}, bf16[1024,1024]{1,0:T(8,128)(2,1)S(1)}) custom-call(s32[3,4,8]{2,1,0:T(4,128)S(1)} %bitcast.4, s32[3,8]{1,0:T(4,128)S(1)} %bitcast.5, s32[8,3,4,8,128]{4,3,2,1,0:T(8,128)S(1)} %copy-done.5), custom_call_target="tpu_custom_call" | custom-call | flops 3145728000 | bytes 6291456 | tf_op jit(solution)/shard_map/adjacency/pallas_call | solution.py:146
  7.2 2.9 %forward.1 = (bf16[128,256]{1,0:T(8,128)(2,1)S(1)}, bf16[128,256]{1,0:T(8,128)(2,1)S(1)}, bf16[128,256]{1,0:T(8,128)(2,1)S(1)}, bf16[128,256]{1,0:T(8,128)(2,1)S...) custom-call(f32[3,8,1024]{2,1,0:T(8,128)S(1)} %get-tuple-element.24., ...), custom_call_target="tpu_custom_call" | custom-call | flops 2415919104 | bytes 6291456 | tf_op jit(solution)/shard_map/forward/pallas_call | solution.py:187
  10.1 4.0 %collective-permute-start = (bf16[128,256]{1,0:T(8,128)(2,1)S(1)}, bf16[128,256]{1,0:T(8,128)(2,1)S(1)}, u32[]{:S(2)}, u32[]{:S(2)}) collective-permute-start(bf16[128,256]{1,0:T(8,128)(2,1)S(1)} %get-tuple-element.28), channel_id=1, source_target_pairs={{0,6},{1,7},{2,4},{3,5},{4,2},{5,3},{6,0},{7,1},{8,14},{9,15},{10,... | collective-permute-start | bytes 196616 | tf_op jit(solution)/shard_map/ppermute | solution.py:353
  14.1 1.2 %collective-permute-start.2 = (bf16[128,256]{1,0:T(8,128)(2,1)S(1)}, bf16[128,256]{1,0:T(8,128)(2,1)S(1)}, u32[]{:S(2)}, u32[]{:S(2)}) collective-permute-start(bf16[128,256]{1,0:T(8,128)(2,1)S(1)} %get-tuple-element.30), channel_id=1, source_target_pairs={{0,4},{1,5},{2,6},{3,7},{4,0},{5,1},{6,2},{7,3},{8,12},{9,13},{10,... | collective-permute-start | bytes 196616 | tf_op jit(solution)/shard_map/ppermute | solution.py:353
  15.2 0.6 collective-permute-start.3
  15.8 1.7 %collective-permute-start.4 = (bf16[128,256]{1,0:T(8,128)(2,1)S(1)}, bf16[128,256]{1,0:T(8,128)(2,1)S(1)}, u32[]{:S(2)}, u32[]{:S(2)}) collective-permute-start(bf16[128,256]{1,0:T(8,128)(2,1)S(1)} %get-tuple-element.32), channel_id=1, source_target_pairs={{0,2},{1,3},{2,0},{3,1},{4,6},{5,7},{6,4},{7,5},{8,10},{9,11},{10,... | collective-permute-start | bytes 196616 | tf_op jit(solution)/shard_map/ppermute | solution.py:353
  17.6 1.6 %collective-permute-done.1.refs_1_ = bf16[128,256]{1,0:T(8,128)(2,1)S(1)} collective-permute-done((bf16[128,256]{1,0:T(8,128)(2,1)S(1)}, bf16[128,256]{1,0:T(8,128)(2,1)S(1)}, u32[]{:S(2)}, u32[]{:S(2)}) %collective-permute-start.1) | collective-permute-done | bytes 65568 | tf_op jit(solution)/shard_map/ppermute | solution.py:353
  19.2 1.2 %collective-permute-done.2.refs_2_ = bf16[128,256]{1,0:T(8,128)(2,1)S(1)} collective-permute-done((bf16[128,256]{1,0:T(8,128)(2,1)S(1)}, bf16[128,256]{1,0:T(8,128)(2,1)S(1)}, u32[]{:S(2)}, u32[]{:S(2)}) %collective-permute-start.2) | collective-permute-done | bytes 65568 | tf_op jit(solution)/shard_map/ppermute | solution.py:353
  20.4 0.3 collective-permute-done.3.refs_3_
  20.7 1.0 %collective-permute-done.5.refs_5_ = bf16[128,256]{1,0:T(8,128)(2,1)S(1)} collective-permute-done((bf16[128,256]{1,0:T(8,128)(2,1)S(1)}, bf16[128,256]{1,0:T(8,128)(2,1)S(1)}, u32[]{:S(2)}, u32[]{:S(2)}) %collective-permute-start.5) | collective-permute-done | bytes 65568 | tf_op jit(solution)/shard_map/ppermute | solution.py:353
  21.7 0.8 combine.1
  22.5 1.1 %collective-permute-start.12 = (bf16[128,256]{1,0:T(8,128)(2,1)S(1)}, bf16[128,256]{1,0:T(8,128)(2,1)S(1)}, u32[]{:S(2)}, u32[]{:S(2)}) collective-permute-start(bf16[128,256]{1,0:T(8,128)(2,1)S(1)} %get-tuple-element.39.rest_7_), channel_id=1, source_target_pairs={{0,3},{1,2},{2,1},{3,0},{4,7},{5,6},{6,5},{7,4},{8,11},{9,10},{10,... | collective-permute-start | bytes 196616 | tf_op jit(solution)/shard_map/ppermute | solution.py:353
  23.6 1.0 %collective-permute-start.11 = (bf16[128,256]{1,0:T(8,128)(2,1)S(1)}, bf16[128,256]{1,0:T(8,128)(2,1)S(1)}, u32[]{:S(2)}, u32[]{:S(2)}) collective-permute-start(bf16[128,256]{1,0:T(8,128)(2,1)S(1)} %get-tuple-element.39.rest_7_), channel_id=1, source_target_pairs={{0,2},{1,3},{2,0},{3,1},{4,6},{5,7},{6,4},{7,5},{8,10},{9,11},{10,... | collective-permute-start | bytes 196616 | tf_op jit(solution)/shard_map/ppermute | solution.py:353
  24.6 0.8 %collective-permute-start.10 = (bf16[128,256]{1,0:T(8,128)(2,1)S(1)}, bf16[128,256]{1,0:T(8,128)(2,1)S(1)}, u32[]{:S(2)}, u32[]{:S(2)}) collective-permute-start(bf16[128,256]{1,0:T(8,128)(2,1)S(1)} %get-tuple-element.39.rest_7_), channel_id=1, source_target_pairs={{0,5},{1,4},{2,7},{3,6},{4,1},{5,0},{6,3},{7,2},{8,13},{9,12},{10,... | collective-permute-start | bytes 196616 | tf_op jit(solution)/shard_map/ppermute | solution.py:353
  25.5 0.7 collective-permute-start.9
  26.2 2.0 %collective-permute-start.8 = (bf16[128,256]{1,0:T(8,128)(2,1)S(1)}, bf16[128,256]{1,0:T(8,128)(2,1)S(1)}, u32[]{:S(2)}, u32[]{:S(2)}) collective-permute-start(bf16[128,256]{1,0:T(8,128)(2,1)S(1)} %get-tuple-element.39.rest_7_), channel_id=1, source_target_pairs={{0,7},{1,6},{2,5},{3,4},{4,3},{5,2},{6,1},{7,0},{8,15},{9,14},{10,... | collective-permute-start | bytes 196616 | tf_op jit(solution)/shard_map/ppermute | solution.py:353
  28.2 0.8 collective-permute-start.7
  29.0 0.9 %transposed.1 = (bf16[512,1024]{1,0:T(8,128)(2,1)S(1)}, f32[1024,128]{1,0:T(8,128)S(1)}, f32[1024,128]{1,0:T(8,128)S(1)}, f32[1024,128]{1,0:T(8,128)S(1)}) custom-call(bf16[1024,512]{1,0:T(8,128)(2,1)S(1)} %copy-done, f32[3,8,1024]{2,1,0:T(8,128)S(1)} %get-tuple-element.24.inv_ref), custom_call_target="tpu_custom_call" | custom-call | flops 1048576 | bytes 3145728 | tf_op jit(solution)/shard_map/transposed/pallas_call | solution.py:216
  29.9 1.9 %collective-permute-done.9.rest_2_ = bf16[128,256]{1,0:T(8,128)(2,1)S(1)} collective-permute-done((bf16[128,256]{1,0:T(8,128)(2,1)S(1)}, bf16[128,256]{1,0:T(8,128)(2,1)S(1)}, u32[]{:S(2)}, u32[]{:S(2)}) %collective-permute-start.9) | collective-permute-done | bytes 65568 | tf_op jit(solution)/shard_map/ppermute | solution.py:353
  31.8 1.6 %collective-permute-done.7.rest_0_ = bf16[128,256]{1,0:T(8,128)(2,1)S(1)} collective-permute-done((bf16[128,256]{1,0:T(8,128)(2,1)S(1)}, bf16[128,256]{1,0:T(8,128)(2,1)S(1)}, u32[]{:S(2)}, u32[]{:S(2)}) %collective-permute-start.7) | collective-permute-done | bytes 65568 | tf_op jit(solution)/shard_map/ppermute | solution.py:353
  33.4 1.5 %gradient.4 = (bf16[256,256]{1,0:T(8,128)(2,1)S(1)}, bf16[256,256]{1,0:T(8,128)(2,1)S(1)}) custom-call(bf16[512,1024]{1,0:T(8,128)(2,1)S(1)} %get-tuple-element.37.xt_ref, bf16[1024,1024]{1,0:T(8,128)(2,1)S(1)} %get-tuple-element.25.refs_0_.adj_ref, f32[1024,128]{1,0:T(8,128)S(1)} %get-tuple-element.40.col_ref, ...), custom_call_target="tpu_custom_call" | custom-call | flops 805306368 | bytes 2883584 | tf_op jit(solution)/shard_map/gradient/pallas_call | solution.py:273
  34.9 3.8 %collective-permute-start.15 = (bf16[256,256]{1,0:T(8,128)(2,1)S(1)}, bf16[256,256]{1,0:T(8,128)(2,1)S(1)}, u32[]{:S(2)}, u32[]{:S(2)}) collective-permute-start(bf16[256,256]{1,0:T(8,128)(2,1)S(1)} %get-tuple-element.41), channel_id=1, source_target_pairs={{0,8},{24,16},{1,9},{25,17},{2,10},{26,18},{3,11},{27,19},{4,12},{... | collective-permute-start | bytes 393224 | tf_op jit(solution)/shard_map/ppermute | solution.py:326
  38.7 1.3 %collective-permute-start.20 = (bf16[256,256]{1,0:T(8,128)(2,1)S(1)}, bf16[256,256]{1,0:T(8,128)(2,1)S(1)}, u32[]{:S(2)}, u32[]{:S(2)}) collective-permute-start(bf16[256,256]{1,0:T(8,128)(2,1)S(1)} %get-tuple-element.44), channel_id=1, source_target_pairs={{0,8},{24,16},{1,9},{25,17},{2,10},{26,18},{3,11},{27,19},{4,12},{... | collective-permute-start | bytes 393224 | tf_op jit(solution)/shard_map/ppermute | solution.py:326
  40.0 1.5 %gradient.3 = bf16[512,256]{1,0:T(8,128)(2,1)S(1)} custom-call(bf16[512,1024]{1,0:T(8,128)(2,1)S(1)} %get-tuple-element.37.xt_ref, bf16[1024,1024]{1,0:T(8,128)(2,1)S(1)} %get-tuple-element.27.refs_2_.adj_ref, f32[1024,128]{1,0:T(8,128)S(1)} %get-tuple-element.38.col_ref, bf16[128,256]{1,0:T(8,128)(2,1)S(1)} %collective-permute-done.7.rest_0_, ...), custom_call_target="tpu_custom_call" | custom-call | flops 805306368 | bytes 2883584 | tf_op jit(solution)/shard_map/gradient/pallas_call | solution.py:273
  41.5 1.3 %collective-permute-start.14 = (bf16[512,256]{1,0:T(8,128)(2,1)S(1)}, bf16[512,256]{1,0:T(8,128)(2,1)S(1)}, u32[]{:S(2)}, u32[]{:S(2)}) collective-permute-start(bf16[512,256]{1,0:T(8,128)(2,1)S(1)} %gradient.3), channel_id=1, source_target_pairs={{0,8},{24,16},{1,9},{25,17},{2,10},{26,18},{3,11},{27,19},{4,12},{... | collective-permute-start | bytes 786440 | tf_op jit(solution)/shard_map/ppermute | solution.py:326
  42.8 1.5 %gradient.5 = bf16[512,256]{1,0:T(8,128)(2,1)S(1)} custom-call(bf16[512,1024]{1,0:T(8,128)(2,1)S(1)} %get-tuple-element.37.xt_ref, bf16[1024,1024]{1,0:T(8,128)(2,1)S(1)} %get-tuple-element.26.refs_1_.adj_ref, f32[1024,128]{1,0:T(8,128)S(1)} %get-tuple-element.43.col_ref, bf16[128,256]{1,0:T(8,128)(2,1)S(1)} %collective-permute-done.7.rest_0_, ...), custom_call_target="tpu_custom_call" | custom-call | flops 805306368 | bytes 2883584 | tf_op jit(solution)/shard_map/gradient/pallas_call | solution.py:273
  44.4 1.3 %collective-permute-start.19 = (bf16[512,256]{1,0:T(8,128)(2,1)S(1)}, bf16[512,256]{1,0:T(8,128)(2,1)S(1)}, u32[]{:S(2)}, u32[]{:S(2)}) collective-permute-start(bf16[512,256]{1,0:T(8,128)(2,1)S(1)} %gradient.5), channel_id=1, source_target_pairs={{0,8},{24,16},{1,9},{25,17},{2,10},{26,18},{3,11},{27,19},{4,12},{... | collective-permute-start | bytes 786440 | tf_op jit(solution)/shard_map/ppermute | solution.py:326
  45.7 0.7 collective-permute-start.16
  46.5 0.7 collective-permute-start.21
  47.2 1.3 %collective-permute-start.24 = (bf16[256,256]{1,0:T(8,128)(2,1)S(1)}, bf16[256,256]{1,0:T(8,128)(2,1)S(1)}, u32[]{:S(2)}, u32[]{:S(2)}) collective-permute-start(bf16[256,256]{1,0:T(8,128)(2,1)S(1)} %reduce-precision_convert_fusion.6.sent_ref), channel_id=1, source_target_pairs={{8,0},{16,24},{9,1},{17,25},{10,2},{18,26},{11,3},{19,27},{12,4},{... | collective-permute-start | bytes 393224 | tf_op jit(solution)/shard_map/ppermute | solution.py:342
  48.5 1.3 %collective-permute-start.25 = (bf16[256,256]{1,0:T(8,128)(2,1)S(1)}, bf16[256,256]{1,0:T(8,128)(2,1)S(1)}, u32[]{:S(2)}, u32[]{:S(2)}) collective-permute-start(bf16[256,256]{1,0:T(8,128)(2,1)S(1)} %reduce-precision_convert_fusion.4.sent_ref), channel_id=1, source_target_pairs={{8,0},{16,24},{9,1},{17,25},{10,2},{18,26},{11,3},{19,27},{12,4},{... | collective-permute-start | bytes 393224 | tf_op jit(solution)/shard_map/ppermute | solution.py:342
  49.8 4.7 %collective-permute-done.19 = bf16[512,256]{1,0:T(8,128)(2,1)S(1)} collective-permute-done((bf16[512,256]{1,0:T(8,128)(2,1)S(1)}, bf16[512,256]{1,0:T(8,128)(2,1)S(1)}, u32[]{:S(2)}, u32[]{:S(2)}) %collective-permute-start.19) | collective-permute-done | bytes 262176 | tf_op jit(solution)/shard_map/ppermute | solution.py:326
  54.5 0.1 reduce-precision_convert_fusion.1
  54.6 0.7 collective-permute-start.22
  55.4 0.7 collective-permute-start.17
  56.1 3.7 %collective-permute-done.25.got_ref = bf16[256,256]{1,0:T(8,128)(2,1)S(1)} collective-permute-done((bf16[256,256]{1,0:T(8,128)(2,1)S(1)}, bf16[256,256]{1,0:T(8,128)(2,1)S(1)}, u32[]{:S(2)}, u32[]{:S(2)}) %collective-permute-start.25) | collective-permute-done | bytes 131104 | tf_op jit(solution)/shard_map/ppermute | solution.py:342
  59.7 0.7 finish.4.rest_0_
  60.5 0.1 reduce-precision_convert_fusion.sent_ref
  60.6 1.3 %collective-permute-start.23 = (bf16[512,256]{1,0:T(8,128)(2,1)S(1)}, bf16[512,256]{1,0:T(8,128)(2,1)S(1)}, u32[]{:S(2)}, u32[]{:S(2)}) collective-permute-start(bf16[512,256]{1,0:T(8,128)(2,1)S(1)} %reduce-precision_convert_fusion.sent_ref), channel_id=1, source_target_pairs={{8,0},{16,24},{9,1},{17,25},{10,2},{18,26},{11,3},{19,27},{12,4},{... | collective-permute-start | bytes 786440 | tf_op jit(solution)/shard_map/ppermute | solution.py:342
  61.9 1.3 %collective-permute-start.18 = (bf16[512,256]{1,0:T(8,128)(2,1)S(1)}, bf16[512,256]{1,0:T(8,128)(2,1)S(1)}, u32[]{:S(2)}, u32[]{:S(2)}) collective-permute-start(bf16[512,256]{1,0:T(8,128)(2,1)S(1)} %reduce-precision_convert_fusion.2.sent_ref), channel_id=1, source_target_pairs={{8,0},{16,24},{9,1},{17,25},{10,2},{18,26},{11,3},{19,27},{12,4},{... | collective-permute-start | bytes 786440 | tf_op jit(solution)/shard_map/ppermute | solution.py:342
  63.3 0.7 finish.5.rest_0_
  64.0 12.4 %collective-permute-done.23.got_ref = bf16[512,256]{1,0:T(8,128)(2,1)S(1)} collective-permute-done((bf16[512,256]{1,0:T(8,128)(2,1)S(1)}, bf16[512,256]{1,0:T(8,128)(2,1)S(1)}, u32[]{:S(2)}, u32[]{:S(2)}) %collective-permute-start.23) | collective-permute-done | bytes 262176 | tf_op jit(solution)/shard_map/ppermute | solution.py:342
  76.4 0.9 %finish.6.rest_0_ = f32[3,512,256]{2,1,0:T(8,128)} custom-call(bf16[512,256]{1,0:T(8,128)(2,1)S(1)} %collective-permute-done.23.got_ref, bf16[512,256]{1,0:T(8,128)(2,1)S(1)} %reduce-precision_convert_fusion.sent_ref, f32[3,512,256]{2,1,0:T(8,128)} %finish.5.rest_0_), custom_call_target="tpu_custom_call", output_to_operand_aliasing={{}: (2, {})} | custom-call | flops 2000000000 | bytes 1048576 | tf_op jit(solution)/shard_map/finish/pallas_call | solution.py:300
  77.3 2.3 %collective-permute-done.18.got_ref = bf16[512,256]{1,0:T(8,128)(2,1)S(1)} collective-permute-done((bf16[512,256]{1,0:T(8,128)(2,1)S(1)}, bf16[512,256]{1,0:T(8,128)(2,1)S(1)}, u32[]{:S(2)}, u32[]{:S(2)}) %collective-permute-start.18) | collective-permute-done | bytes 262176 | tf_op jit(solution)/shard_map/ppermute | solution.py:342
  79.5 0.9 %finish.7 = f32[3,512,256]{2,1,0:T(8,128)} custom-call(bf16[512,256]{1,0:T(8,128)(2,1)S(1)} %collective-permute-done.18.got_ref, bf16[512,256]{1,0:T(8,128)(2,1)S(1)} %reduce-precision_convert_fusion.2.sent_ref, f32[3,512,256]{2,1,0:T(8,128)} %finish.6.rest_0_), custom_call_target="tpu_custom_call", output_to_operand_aliasing={{}: (2, {})} | custom-call | flops 2000000000 | bytes 1048576 | tf_op jit(solution)/shard_map/finish/pallas_call | solution.py:300
  (39 shorter events, 0.4 us)
Async XLA Ops:
  0.6 1.0 %copy-start.5 = (s32[8,3,4,8,128]{4,3,2,1,0:T(8,128)S(1)}, s32[8,3,4,8,128]{4,3,2,1,0:T(8,128)}, u32[]{:S(2)}) copy-start(s32[8,3,4,8,128]{4,3,2,1,0:T(8,128)} %pat_ref.1) | copy-start | bytes 1179652
  1.6 0.7 copy-start.6
  2.3 0.7 copy-start.7
  3.0 4.1 %copy-start = (bf16[1024,512]{1,0:T(8,128)(2,1)S(1)}, bf16[1024,512]{1,0:T(8,128)(2,1)}, u32[]{:S(2)}) copy-start(bf16[1024,512]{1,0:T(8,128)(2,1)} %x_ref.1) | copy-start | bytes 3145732
  3.0 4.1 %copy-start.4 = (bf16[3,512,256]{2,1,0:T(8,128)(2,1)S(1)}, bf16[3,512,256]{2,1,0:T(8,128)(2,1)}, u32[]{:S(2)}) copy-start(bf16[3,512,256]{2,1,0:T(8,128)(2,1)} %refs_4_.1) | copy-start | bytes 2359300
  7.1 14.5 %copy-start.1 = (bf16[128,256]{1,0:T(8,128)(2,1)S(1)}, bf16[128,256]{1,0:T(8,128)(2,1)}, u32[]{:S(2)}) copy-start(bf16[128,256]{1,0:T(8,128)(2,1)} %refs_10_.1) | copy-start | bytes 196612
  7.2 14.5 %copy-start.2 = (f32[3,256]{1,0:T(4,128)S(1)}, f32[3,256]{1,0:T(4,128)}, u32[]{:S(2)}) copy-start(f32[3,256]{1,0:T(4,128)} %refs_9_.1) | copy-start | bytes 9220
  7.2 14.5 %copy-start.3 = (s32[128]{0:T(128)S(1)}, s32[128]{0:T(128)}, u32[]{:S(2)}) copy-start(s32[128]{0:T(128)} %param.13) | copy-start | bytes 1540
  10.1 7.4 %collective-permute-start = (bf16[128,256]{1,0:T(8,128)(2,1)S(1)}, bf16[128,256]{1,0:T(8,128)(2,1)S(1)}, u32[]{:S(2)}, u32[]{:S(2)}) collective-permute-start(bf16[128,256]{1,0:T(8,128)(2,1)S(1)} %get-tuple-element.28), channel_id=1, source_target_pairs={{0,6},{1,7},{2,4},{3,5},{4,2},{5,3},{6,0},{7,1},{8,14},{9,15},{10,... | collective-permute-start | bytes 196616 | tf_op jit(solution)/shard_map/ppermute | solution.py:353
  14.1 5.1 %collective-permute-start.1 = (bf16[128,256]{1,0:T(8,128)(2,1)S(1)}, bf16[128,256]{1,0:T(8,128)(2,1)S(1)}, u32[]{:S(2)}, u32[]{:S(2)}) collective-permute-start(bf16[128,256]{1,0:T(8,128)(2,1)S(1)} %get-tuple-element.29), channel_id=1, source_target_pairs={{0,7},{1,6},{2,5},{3,4},{4,3},{5,2},{6,1},{7,0},{8,15},{9,14},{10,... | collective-permute-start | bytes 196616 | tf_op jit(solution)/shard_map/ppermute | solution.py:353
  14.1 6.3 %collective-permute-start.2 = (bf16[128,256]{1,0:T(8,128)(2,1)S(1)}, bf16[128,256]{1,0:T(8,128)(2,1)S(1)}, u32[]{:S(2)}, u32[]{:S(2)}) collective-permute-start(bf16[128,256]{1,0:T(8,128)(2,1)S(1)} %get-tuple-element.30), channel_id=1, source_target_pairs={{0,4},{1,5},{2,6},{3,7},{4,0},{5,1},{6,2},{7,3},{8,12},{9,13},{10,... | collective-permute-start | bytes 196616 | tf_op jit(solution)/shard_map/ppermute | solution.py:353
  15.2 5.5 %collective-permute-start.3 = (bf16[128,256]{1,0:T(8,128)(2,1)S(1)}, bf16[128,256]{1,0:T(8,128)(2,1)S(1)}, u32[]{:S(2)}, u32[]{:S(2)}) collective-permute-start(bf16[128,256]{1,0:T(8,128)(2,1)S(1)} %get-tuple-element.31), channel_id=1, source_target_pairs={{0,5},{1,4},{2,7},{3,6},{4,1},{5,0},{6,3},{7,2},{8,13},{9,12},{10,... | collective-permute-start | bytes 196616 | tf_op jit(solution)/shard_map/ppermute | solution.py:353
  15.8 4.9 %collective-permute-start.4 = (bf16[128,256]{1,0:T(8,128)(2,1)S(1)}, bf16[128,256]{1,0:T(8,128)(2,1)S(1)}, u32[]{:S(2)}, u32[]{:S(2)}) collective-permute-start(bf16[128,256]{1,0:T(8,128)(2,1)S(1)} %get-tuple-element.32), channel_id=1, source_target_pairs={{0,2},{1,3},{2,0},{3,1},{4,6},{5,7},{6,4},{7,5},{8,10},{9,11},{10,... | collective-permute-start | bytes 196616 | tf_op jit(solution)/shard_map/ppermute | solution.py:353
  17.5 4.2 %collective-permute-start.5 = (bf16[128,256]{1,0:T(8,128)(2,1)S(1)}, bf16[128,256]{1,0:T(8,128)(2,1)S(1)}, u32[]{:S(2)}, u32[]{:S(2)}) collective-permute-start(bf16[128,256]{1,0:T(8,128)(2,1)S(1)} %get-tuple-element.33), channel_id=1, source_target_pairs={{0,3},{1,2},{2,1},{3,0},{4,7},{5,6},{6,5},{7,4},{8,11},{9,10},{10,... | collective-permute-start | bytes 196616 | tf_op jit(solution)/shard_map/ppermute | solution.py:353
  19.2 2.5 %collective-permute-start.6 = (bf16[128,256]{1,0:T(8,128)(2,1)S(1)}, bf16[128,256]{1,0:T(8,128)(2,1)S(1)}, u32[]{:S(2)}, u32[]{:S(2)}) collective-permute-start(bf16[128,256]{1,0:T(8,128)(2,1)S(1)} %get-tuple-element.34), channel_id=1, source_target_pairs={{0,1},{1,0},{2,3},{3,2},{4,5},{5,4},{6,7},{7,6},{8,9},{9,8},{10,11... | collective-permute-start | bytes 196616 | tf_op jit(solution)/shard_map/ppermute | solution.py:353
  22.5 3.7 %collective-permute-start.13 = (bf16[128,256]{1,0:T(8,128)(2,1)S(1)}, bf16[128,256]{1,0:T(8,128)(2,1)S(1)}, u32[]{:S(2)}, u32[]{:S(2)}) collective-permute-start(bf16[128,256]{1,0:T(8,128)(2,1)S(1)} %get-tuple-element.39.rest_7_), channel_id=1, source_target_pairs={{0,1},{1,0},{2,3},{3,2},{4,5},{5,4},{6,7},{7,6},{8,9},{9,8},{10,11... | collective-permute-start | bytes 196616 | tf_op jit(solution)/shard_map/ppermute | solution.py:353
  22.5 5.7 %collective-permute-start.12 = (bf16[128,256]{1,0:T(8,128)(2,1)S(1)}, bf16[128,256]{1,0:T(8,128)(2,1)S(1)}, u32[]{:S(2)}, u32[]{:S(2)}) collective-permute-start(bf16[128,256]{1,0:T(8,128)(2,1)S(1)} %get-tuple-element.39.rest_7_), channel_id=1, source_target_pairs={{0,3},{1,2},{2,1},{3,0},{4,7},{5,6},{6,5},{7,4},{8,11},{9,10},{10,... | collective-permute-start | bytes 196616 | tf_op jit(solution)/shard_map/ppermute | solution.py:353
  23.6 6.3 %collective-permute-start.11 = (bf16[128,256]{1,0:T(8,128)(2,1)S(1)}, bf16[128,256]{1,0:T(8,128)(2,1)S(1)}, u32[]{:S(2)}, u32[]{:S(2)}) collective-permute-start(bf16[128,256]{1,0:T(8,128)(2,1)S(1)} %get-tuple-element.39.rest_7_), channel_id=1, source_target_pairs={{0,2},{1,3},{2,0},{3,1},{4,6},{5,7},{6,4},{7,5},{8,10},{9,11},{10,... | collective-permute-start | bytes 196616 | tf_op jit(solution)/shard_map/ppermute | solution.py:353
  24.6 5.3 %collective-permute-start.10 = (bf16[128,256]{1,0:T(8,128)(2,1)S(1)}, bf16[128,256]{1,0:T(8,128)(2,1)S(1)}, u32[]{:S(2)}, u32[]{:S(2)}) collective-permute-start(bf16[128,256]{1,0:T(8,128)(2,1)S(1)} %get-tuple-element.39.rest_7_), channel_id=1, source_target_pairs={{0,5},{1,4},{2,7},{3,6},{4,1},{5,0},{6,3},{7,2},{8,13},{9,12},{10,... | collective-permute-start | bytes 196616 | tf_op jit(solution)/shard_map/ppermute | solution.py:353
  25.5 6.4 %collective-permute-start.9 = (bf16[128,256]{1,0:T(8,128)(2,1)S(1)}, bf16[128,256]{1,0:T(8,128)(2,1)S(1)}, u32[]{:S(2)}, u32[]{:S(2)}) collective-permute-start(bf16[128,256]{1,0:T(8,128)(2,1)S(1)} %get-tuple-element.39.rest_7_), channel_id=1, source_target_pairs={{0,4},{1,5},{2,6},{3,7},{4,0},{5,1},{6,2},{7,3},{8,12},{9,13},{10,... | collective-permute-start | bytes 196616 | tf_op jit(solution)/shard_map/ppermute | solution.py:353
  26.2 5.7 %collective-permute-start.8 = (bf16[128,256]{1,0:T(8,128)(2,1)S(1)}, bf16[128,256]{1,0:T(8,128)(2,1)S(1)}, u32[]{:S(2)}, u32[]{:S(2)}) collective-permute-start(bf16[128,256]{1,0:T(8,128)(2,1)S(1)} %get-tuple-element.39.rest_7_), channel_id=1, source_target_pairs={{0,7},{1,6},{2,5},{3,4},{4,3},{5,2},{6,1},{7,0},{8,15},{9,14},{10,... | collective-permute-start | bytes 196616 | tf_op jit(solution)/shard_map/ppermute | solution.py:353
  28.2 5.2 %collective-permute-start.7 = (bf16[128,256]{1,0:T(8,128)(2,1)S(1)}, bf16[128,256]{1,0:T(8,128)(2,1)S(1)}, u32[]{:S(2)}, u32[]{:S(2)}) collective-permute-start(bf16[128,256]{1,0:T(8,128)(2,1)S(1)} %get-tuple-element.39.rest_7_), channel_id=1, source_target_pairs={{0,6},{1,7},{2,4},{3,5},{4,2},{5,3},{6,0},{7,1},{8,14},{9,15},{10,... | collective-permute-start | bytes 196616 | tf_op jit(solution)/shard_map/ppermute | solution.py:353
  34.9 10.8 %collective-permute-start.15 = (bf16[256,256]{1,0:T(8,128)(2,1)S(1)}, bf16[256,256]{1,0:T(8,128)(2,1)S(1)}, u32[]{:S(2)}, u32[]{:S(2)}) collective-permute-start(bf16[256,256]{1,0:T(8,128)(2,1)S(1)} %get-tuple-element.41), channel_id=1, source_target_pairs={{0,8},{24,16},{1,9},{25,17},{2,10},{26,18},{3,11},{27,19},{4,12},{... | collective-permute-start | bytes 393224 | tf_op jit(solution)/shard_map/ppermute | solution.py:326
  38.7 7.7 %collective-permute-start.20 = (bf16[256,256]{1,0:T(8,128)(2,1)S(1)}, bf16[256,256]{1,0:T(8,128)(2,1)S(1)}, u32[]{:S(2)}, u32[]{:S(2)}) collective-permute-start(bf16[256,256]{1,0:T(8,128)(2,1)S(1)} %get-tuple-element.44), channel_id=1, source_target_pairs={{0,8},{24,16},{1,9},{25,17},{2,10},{26,18},{3,11},{27,19},{4,12},{... | collective-permute-start | bytes 393224 | tf_op jit(solution)/shard_map/ppermute | solution.py:326
  41.5 13.8 %collective-permute-start.14 = (bf16[512,256]{1,0:T(8,128)(2,1)S(1)}, bf16[512,256]{1,0:T(8,128)(2,1)S(1)}, u32[]{:S(2)}, u32[]{:S(2)}) collective-permute-start(bf16[512,256]{1,0:T(8,128)(2,1)S(1)} %gradient.3), channel_id=1, source_target_pairs={{0,8},{24,16},{1,9},{25,17},{2,10},{26,18},{3,11},{27,19},{4,12},{... | collective-permute-start | bytes 786440 | tf_op jit(solution)/shard_map/ppermute | solution.py:326
  44.4 10.2 %collective-permute-start.19 = (bf16[512,256]{1,0:T(8,128)(2,1)S(1)}, bf16[512,256]{1,0:T(8,128)(2,1)S(1)}, u32[]{:S(2)}, u32[]{:S(2)}) collective-permute-start(bf16[512,256]{1,0:T(8,128)(2,1)S(1)} %gradient.5), channel_id=1, source_target_pairs={{0,8},{24,16},{1,9},{25,17},{2,10},{26,18},{3,11},{27,19},{4,12},{... | collective-permute-start | bytes 786440 | tf_op jit(solution)/shard_map/ppermute | solution.py:326
  45.7 1.4 %collective-permute-start.16 = (bf16[256,256]{1,0:T(8,128)(2,1)S(1)}, bf16[256,256]{1,0:T(8,128)(2,1)S(1)}, u32[]{:S(2)}, u32[]{:S(2)}) collective-permute-start(bf16[256,256]{1,0:T(8,128)(2,1)S(1)} %reduce-precision_convert_fusion.7), channel_id=1, source_target_pairs={{8,16},{16,8},{9,17},{17,9},{10,18},{18,10},{11,19},{19,11},{12,20... | collective-permute-start | bytes 393224 | tf_op jit(solution)/shard_map/ppermute | solution.py:333
  46.5 2.0 %collective-permute-start.21 = (bf16[256,256]{1,0:T(8,128)(2,1)S(1)}, bf16[256,256]{1,0:T(8,128)(2,1)S(1)}, u32[]{:S(2)}, u32[]{:S(2)}) collective-permute-start(bf16[256,256]{1,0:T(8,128)(2,1)S(1)} %reduce-precision_convert_fusion.5), channel_id=1, source_target_pairs={{8,16},{16,8},{9,17},{17,9},{10,18},{18,10},{11,19},{19,11},{12,20... | collective-permute-start | bytes 393224 | tf_op jit(solution)/shard_map/ppermute | solution.py:333
  47.2 16.1 %collective-permute-start.24 = (bf16[256,256]{1,0:T(8,128)(2,1)S(1)}, bf16[256,256]{1,0:T(8,128)(2,1)S(1)}, u32[]{:S(2)}, u32[]{:S(2)}) collective-permute-start(bf16[256,256]{1,0:T(8,128)(2,1)S(1)} %reduce-precision_convert_fusion.6.sent_ref), channel_id=1, source_target_pairs={{8,0},{16,24},{9,1},{17,25},{10,2},{18,26},{11,3},{19,27},{12,4},{... | collective-permute-start | bytes 393224 | tf_op jit(solution)/shard_map/ppermute | solution.py:342
  48.5 11.2 %collective-permute-start.25 = (bf16[256,256]{1,0:T(8,128)(2,1)S(1)}, bf16[256,256]{1,0:T(8,128)(2,1)S(1)}, u32[]{:S(2)}, u32[]{:S(2)}) collective-permute-start(bf16[256,256]{1,0:T(8,128)(2,1)S(1)} %reduce-precision_convert_fusion.4.sent_ref), channel_id=1, source_target_pairs={{8,0},{16,24},{9,1},{17,25},{10,2},{18,26},{11,3},{19,27},{12,4},{... | collective-permute-start | bytes 393224 | tf_op jit(solution)/shard_map/ppermute | solution.py:342
  54.6 5.9 %collective-permute-start.22 = (bf16[512,256]{1,0:T(8,128)(2,1)S(1)}, bf16[512,256]{1,0:T(8,128)(2,1)S(1)}, u32[]{:S(2)}, u32[]{:S(2)}) collective-permute-start(bf16[512,256]{1,0:T(8,128)(2,1)S(1)} %reduce-precision_convert_fusion.1), channel_id=1, source_target_pairs={{8,16},{16,8},{9,17},{17,9},{10,18},{18,10},{11,19},{19,11},{12,20... | collective-permute-start | bytes 786440 | tf_op jit(solution)/shard_map/ppermute | solution.py:333
  55.4 6.5 %collective-permute-start.17 = (bf16[512,256]{1,0:T(8,128)(2,1)S(1)}, bf16[512,256]{1,0:T(8,128)(2,1)S(1)}, u32[]{:S(2)}, u32[]{:S(2)}) collective-permute-start(bf16[512,256]{1,0:T(8,128)(2,1)S(1)} %reduce-precision_convert_fusion.3), channel_id=1, source_target_pairs={{8,16},{16,8},{9,17},{17,9},{10,18},{18,10},{11,19},{19,11},{12,20... | collective-permute-start | bytes 786440 | tf_op jit(solution)/shard_map/ppermute | solution.py:333
  60.6 15.8 %collective-permute-start.23 = (bf16[512,256]{1,0:T(8,128)(2,1)S(1)}, bf16[512,256]{1,0:T(8,128)(2,1)S(1)}, u32[]{:S(2)}, u32[]{:S(2)}) collective-permute-start(bf16[512,256]{1,0:T(8,128)(2,1)S(1)} %reduce-precision_convert_fusion.sent_ref), channel_id=1, source_target_pairs={{8,0},{16,24},{9,1},{17,25},{10,2},{18,26},{11,3},{19,27},{12,4},{... | collective-permute-start | bytes 786440 | tf_op jit(solution)/shard_map/ppermute | solution.py:342
  61.9 17.6 %collective-permute-start.18 = (bf16[512,256]{1,0:T(8,128)(2,1)S(1)}, bf16[512,256]{1,0:T(8,128)(2,1)S(1)}, u32[]{:S(2)}, u32[]{:S(2)}) collective-permute-start(bf16[512,256]{1,0:T(8,128)(2,1)S(1)} %reduce-precision_convert_fusion.2.sent_ref), channel_id=1, source_target_pairs={{8,0},{16,24},{9,1},{17,25},{10,2},{18,26},{11,3},{19,27},{12,4},{... | collective-permute-start | bytes 786440 | tf_op jit(solution)/shard_map/ppermute | solution.py:342

commit v2 on v1

--- a/solution.py
+++ b/solution.py
@@ -177,7 +177,7 @@
     me = lax.axis_index("feat")
     for k, piece in enumerate(piece_refs):
         first = pl.multiple_of((me ^ k) * BLK, BLK)
-        piece[...] = pre_ref[:, pl.ds(first, BLK)].T.astype(BF16)
+        piece[...] = pre_ref[:, pl.ds(first, BLK)].T.astype(piece.dtype)
 
 
 def forward(inv_deg, adj, features, proj_weight, n_feat):
@@ -187,7 +187,10 @@
     return pl.pallas_call(
         functools.partial(forward_kernel, n_feat, relations),
         name="forward",
-        out_shape=[jax.ShapeDtypeStruct((nodes // n_feat, hidden), BF16)] * n_feat,
+        out_shape=[
+            jax.ShapeDtypeStruct((nodes // n_feat, hidden), BF16 if k % 2 else F32)
+            for k in range(n_feat)
+        ],
         in_specs=[vmem] * (3 + relations),
         out_specs=[vmem] * n_feat,
         scratch_shapes=[pltpu.VMEM((hidden, nodes), F32)],
@@ -344,14 +347,29 @@
     return out
 
 
-ORDER = (6, 7, 4, 5, 2, 3, 1, 0)
-
-
-def exchange(value_of, n_feat):
-    got = []
-    for k in ORDER[:-1]:
-        got.append(lax.ppermute(value_of(k), "feat", [(i, i ^ k) for i in range(n_feat)]))
-    return got + [value_of(0)]
+ORDER = (6, 4, 2, 0, 1, 3, 5, 7)
+
+
+def swap(value, k, n_feat):
+    return lax.ppermute(value, "feat", [(i, i ^ k) for i in range(n_feat)])
+
+
+def reduce_pieces(pieces, n_feat):
+    other = {k: swap(pieces[k + 1], 1, n_feat) for k in (6, 4, 2, 0)}
+    terms = []
+    for k in (6, 4, 2):
+        chip = (pieces[k] + other[k].astype(F32)).astype(BF16)
+        terms.append(swap(chip, k, n_feat))
+    return terms + [other[0], pieces[0]]
+
+
+def gather_pieces(piece, n_feat):
+    got = {0: piece}
+    for k in (6, 4, 2):
+        got[k] = swap(piece, k, n_feat)
+    for k in (0, 6, 4, 2):
+        got[k + 1] = swap(got[k], 1, n_feat)
+    return [got[k] for k in ORDER]
 
 
 def dense_body(
@@ -370,10 +388,10 @@
     slot_count = jnp.transpose(slot_count, (1, 0))
     inv_deg, adj = adjacency(source_block, slot_count, block_pattern)
     pieces = forward(inv_deg, adj, features, proj_weight, n_feat)
-    received = exchange(lambda k: pieces[k], n_feat)
+    received = reduce_pieces(pieces, n_feat)
     x_t, col = transposed(features, inv_deg)
     activations, slope = combine(received, node_type, type_gain, cotangent)
-    slopes = exchange(lambda k: slope, n_feat)
+    slopes = gather_pieces(slope, n_feat)
     chunks = []
     for relation in range(proj_weight.shape[0]):
         parts = 2 if relation == 0 else 1

time: 80.8 us -> 78.1 us (0.967)
  starting transfers between devices: 29.6 us -> 24.5 us
  waiting for transfers between devices: 30.7 us -> 32.9 us
    ppermute x14, starting transfers between devices: 14 us -> 9.23 us  [swap(): return lax.ppermute(value, 'feat', [(i, i ^ k) for i in range(n_feat)])]
    ppermute x4, waiting for transfers between devices: 4.69 us -> 5.99 us  [chain_sum(): got = lax.ppermute(sent, 'dom', perm)]
    ppermute x14, waiting for transfers between devices: 7.6 us -> 8.53 us  [swap(): return lax.ppermute(value, 'feat', [(i, i ^ k) for i in range(n_feat)])]
  transfers between devices with their start and end apart: 26 -> 26, of which waited for: 10 -> 12; matrix products, arithmetic and copies ran while one was open for 1% -> 1% of each run, Pallas kernels for 8% -> 8%
where the time goes in v2:
time: 78.1 us; the launch traced here: 77.6 us
  waiting for transfers between devices  32.9 us (42%)
  starting transfers between devices  24.5 us (31%)
  Pallas kernels  16.4 us (21%)
  local copies, waits for them, and re-layouts  2.39 us (3%)
  between operations  0.97 us (1%)
    ppermute x4, waiting for transfers between devices, chain_sum(): got = lax.ppermute(sent, 'dom', [(low, low - 1), (high, high + 1)])  18.4 us
    ppermute x14, starting transfers between devices, swap(): return lax.ppermute(value, 'feat', [(i, i ^ k) for i in range(n_feat)])  9.23 us
    ppermute x14, waiting for transfers between devices, swap(): return lax.ppermute(value, 'feat', [(i, i ^ k) for i in range(n_feat)])  8.53 us
    ppermute x4, starting transfers between devices, chain_sum(): got = lax.ppermute(sent, 'dom', perm)  7.4 us
    ppermute x4, waiting for transfers between devices, chain_sum(): got = lax.ppermute(sent, 'dom', perm)  5.99 us
    ppermute x4, starting transfers between devices, chain_sum(): got = lax.ppermute(sent, 'dom', [(low, low - 1), (high, high + 1)])  5.17 us
    pallas_call x3, Pallas kernels, gradient(): pl.pallas_call(functools.partial(gradient_kernel, len(slopes)), name='gra...  4.53 us
    pallas_call x1, Pallas kernels, adjacency(): pl.pallas_call(adjacency_kernel, name='adjacency', out_shape=[jax.ShapeDt...  4.11 us
  transfers between devices with their start and end apart: 26, of which 12 were waited for; matrix products, arithmetic and copies ran while one was open for 1% of the time, Pallas kernels for 8%

profile of v2, /device:TPU:0, one launch (start us, length us, event | category | flops | bytes accessed | tf_op | source)
XLA Modules:
  0.0 77.6 jit_solution(1286110574142237286)
XLA Ops:
  0.6 1.0 %copy-done.5 = s32[8,3,4,8,128]{4,3,2,1,0:T(8,128)S(1)} copy-done((s32[8,3,4,8,128]{4,3,2,1,0:T(8,128)S(1)}, s32[8,3,4,8,128]{4,3,2,1,0:T(8,128)}, u32[]{:S(2)}) %copy-start.5) | copy-done | bytes 393240
  1.6 0.7 copy-done.6
  2.3 0.7 copy-done.7
  3.0 4.1 %adjacency.1 = (f32[3,8,1024]{2,1,0:T(8,128)S(1)}, bf16[1024,1024]{1,0:T(8,128)(2,1)S(1)}, bf16[1024,1024]{1,0:T(8,128)(2,1)S(1)}, bf16[1024,1024]{1,0:T(8,128)(2,1)S(1)}) custom-call(s32[3,4,8]{2,1,0:T(4,128)S(1)} %bitcast.4, s32[3,8]{1,0:T(4,128)S(1)} %bitcast.5, s32[8,3,4,8,128]{4,3,2,1,0:T(8,128)S(1)} %copy-done.5), custom_call_target="tpu_custom_call" | custom-call | flops 3145728000 | bytes 6291456 | tf_op jit(solution)/shard_map/adjacency/pallas_call | solution.py:146
  7.2 3.0 %forward.1 = (f32[128,256]{1,0:T(8,128)S(1)}, bf16[128,256]{1,0:T(8,128)(2,1)S(1)}, f32[128,256]{1,0:T(8,128)S(1)}, bf16[128,256]{1,0:T(8,128)(2,1)S(1)}, f32[12...) custom-call(f32[3,8,1024]{2,1,0:T(8,128)S(1)} %get-tuple-element.24.inv_, ...), custom_call_target="tpu_custom_call" | custom-call | flops 2415919104 | bytes 6291456 | tf_op jit(solution)/shard_map/forward/pallas_call | solution.py:187
  10.2 0.5 collective-permute-start
  10.7 0.1 collective-permute-start.2
  10.8 0.4 collective-permute-start.4
  11.2 0.1 collective-permute-start.6
  11.3 0.3 collective-permute-done
  11.6 3.9 %collective-permute-start.1 = (bf16[128,256]{1,0:T(8,128)(2,1)S(1)}, bf16[128,256]{1,0:T(8,128)(2,1)S(1)}, u32[]{:S(2)}, u32[]{:S(2)}) collective-permute-start(bf16[128,256]{1,0:T(8,128)(2,1)S(1)} %add_convert_fusion.2), channel_id=1, source_target_pairs={{0,6},{1,7},{2,4},{3,5},{4,2},{5,3},{6,0},{7,1},{8,14},{9,15},{10,... | collective-permute-start | bytes 196616 | tf_op jit(solution)/shard_map/ppermute | solution.py:354
  15.5 0.6 collective-permute-start.3
  16.1 0.2 collective-permute-start.5
  16.3 1.6 %collective-permute-done.1.refs_0_ = bf16[128,256]{1,0:T(8,128)(2,1)S(1)} collective-permute-done((bf16[128,256]{1,0:T(8,128)(2,1)S(1)}, bf16[128,256]{1,0:T(8,128)(2,1)S(1)}, u32[]{:S(2)}, u32[]{:S(2)}) %collective-permute-start.1) | collective-permute-done | bytes 65568 | tf_op jit(solution)/shard_map/ppermute | solution.py:354
  17.9 1.9 %collective-permute-done.3.refs_1_ = bf16[128,256]{1,0:T(8,128)(2,1)S(1)} collective-permute-done((bf16[128,256]{1,0:T(8,128)(2,1)S(1)}, bf16[128,256]{1,0:T(8,128)(2,1)S(1)}, u32[]{:S(2)}, u32[]{:S(2)}) %collective-permute-start.3) | collective-permute-done | bytes 65568 | tf_op jit(solution)/shard_map/ppermute | solution.py:354
  19.8 0.6 collective-permute-done.5.refs_2_
  20.4 0.7 combine.1
  21.2 0.6 collective-permute-start.9
  21.8 1.4 %collective-permute-start.8 = (bf16[128,256]{1,0:T(8,128)(2,1)S(1)}, bf16[128,256]{1,0:T(8,128)(2,1)S(1)}, u32[]{:S(2)}, u32[]{:S(2)}) collective-permute-start(bf16[128,256]{1,0:T(8,128)(2,1)S(1)} %get-tuple-element.39.rest_3_), channel_id=1, source_target_pairs={{0,4},{1,5},{2,6},{3,7},{4,0},{5,1},{6,2},{7,3},{8,12},{9,13},{10,... | collective-permute-start | bytes 196616 | tf_op jit(solution)/shard_map/ppermute | solution.py:354
  23.2 1.4 %collective-permute-start.7 = (bf16[128,256]{1,0:T(8,128)(2,1)S(1)}, bf16[128,256]{1,0:T(8,128)(2,1)S(1)}, u32[]{:S(2)}, u32[]{:S(2)}) collective-permute-start(bf16[128,256]{1,0:T(8,128)(2,1)S(1)} %get-tuple-element.39.rest_3_), channel_id=1, source_target_pairs={{0,6},{1,7},{2,4},{3,5},{4,2},{5,3},{6,0},{7,1},{8,14},{9,15},{10,... | collective-permute-start | bytes 196616 | tf_op jit(solution)/shard_map/ppermute | solution.py:354
  24.7 1.1 %collective-permute-done.9.rest_2_ = bf16[128,256]{1,0:T(8,128)(2,1)S(1)} collective-permute-done((bf16[128,256]{1,0:T(8,128)(2,1)S(1)}, bf16[128,256]{1,0:T(8,128)(2,1)S(1)}, u32[]{:S(2)}, u32[]{:S(2)}) %collective-permute-start.9) | collective-permute-done | bytes 65568 | tf_op jit(solution)/shard_map/ppermute | solution.py:354
  25.8 0.6 collective-permute-done.8.rest_1_
  26.3 2.1 %collective-permute-done.7.rest_0_ = bf16[128,256]{1,0:T(8,128)(2,1)S(1)} collective-permute-done((bf16[128,256]{1,0:T(8,128)(2,1)S(1)}, bf16[128,256]{1,0:T(8,128)(2,1)S(1)}, u32[]{:S(2)}, u32[]{:S(2)}) %collective-permute-start.7) | collective-permute-done | bytes 65568 | tf_op jit(solution)/shard_map/ppermute | solution.py:354
  28.4 0.9 %transposed.1 = (bf16[512,1024]{1,0:T(8,128)(2,1)S(1)}, f32[1024,128]{1,0:T(8,128)S(1)}, f32[1024,128]{1,0:T(8,128)S(1)}, f32[1024,128]{1,0:T(8,128)S(1)}) custom-call(bf16[1024,512]{1,0:T(8,128)(2,1)S(1)} %copy-done, f32[3,8,1024]{2,1,0:T(8,128)S(1)} %get-tuple-element.24.inv_ref), custom_call_target="tpu_custom_call" | custom-call | flops 1048576 | bytes 3145728 | tf_op jit(solution)/shard_map/transposed/pallas_call | solution.py:219
  29.3 0.3 collective-permute-done.13.rest_7_
  29.6 1.5 %gradient.4 = (bf16[256,256]{1,0:T(8,128)(2,1)S(1)}, bf16[256,256]{1,0:T(8,128)(2,1)S(1)}) custom-call(bf16[512,1024]{1,0:T(8,128)(2,1)S(1)} %get-tuple-element.37.xt_ref, bf16[1024,1024]{1,0:T(8,128)(2,1)S(1)} %get-tuple-element.25.refs_0_.adj_ref, f32[1024,128]{1,0:T(8,128)S(1)} %get-tuple-element.40.col_ref, ...), custom_call_target="tpu_custom_call" | custom-call | flops 805306368 | bytes 2883584 | tf_op jit(solution)/shard_map/gradient/pallas_call | solution.py:276
  31.2 3.5 %collective-permute-start.15 = (bf16[256,256]{1,0:T(8,128)(2,1)S(1)}, bf16[256,256]{1,0:T(8,128)(2,1)S(1)}, u32[]{:S(2)}, u32[]{:S(2)}) collective-permute-start(bf16[256,256]{1,0:T(8,128)(2,1)S(1)} %get-tuple-element.41), channel_id=1, source_target_pairs={{0,8},{24,16},{1,9},{25,17},{2,10},{26,18},{3,11},{27,19},{4,12},{... | collective-permute-start | bytes 393224 | tf_op jit(solution)/shard_map/ppermute | solution.py:329
  34.7 1.3 %collective-permute-start.20 = (bf16[256,256]{1,0:T(8,128)(2,1)S(1)}, bf16[256,256]{1,0:T(8,128)(2,1)S(1)}, u32[]{:S(2)}, u32[]{:S(2)}) collective-permute-start(bf16[256,256]{1,0:T(8,128)(2,1)S(1)} %get-tuple-element.44), channel_id=1, source_target_pairs={{0,8},{24,16},{1,9},{25,17},{2,10},{26,18},{3,11},{27,19},{4,12},{... | collective-permute-start | bytes 393224 | tf_op jit(solution)/shard_map/ppermute | solution.py:329
  36.0 1.5 %gradient.3 = bf16[512,256]{1,0:T(8,128)(2,1)S(1)} custom-call(bf16[512,1024]{1,0:T(8,128)(2,1)S(1)} %get-tuple-element.37.xt_ref, bf16[1024,1024]{1,0:T(8,128)(2,1)S(1)} %get-tuple-element.27.refs_2_.adj_ref, f32[1024,128]{1,0:T(8,128)S(1)} %get-tuple-element.38.col_ref, bf16[128,256]{1,0:T(8,128)(2,1)S(1)} %collective-permute-done.7.rest_0_, ...), custom_call_target="tpu_custom_call" | custom-call | flops 805306368 | bytes 2883584 | tf_op jit(solution)/shard_map/gradient/pallas_call | solution.py:276
  37.5 1.3 %collective-permute-start.14 = (bf16[512,256]{1,0:T(8,128)(2,1)S(1)}, bf16[512,256]{1,0:T(8,128)(2,1)S(1)}, u32[]{:S(2)}, u32[]{:S(2)}) collective-permute-start(bf16[512,256]{1,0:T(8,128)(2,1)S(1)} %gradient.3), channel_id=1, source_target_pairs={{0,8},{24,16},{1,9},{25,17},{2,10},{26,18},{3,11},{27,19},{4,12},{... | collective-permute-start | bytes 786440 | tf_op jit(solution)/shard_map/ppermute | solution.py:329
  38.8 1.5 %gradient.5 = bf16[512,256]{1,0:T(8,128)(2,1)S(1)} custom-call(bf16[512,1024]{1,0:T(8,128)(2,1)S(1)} %get-tuple-element.37.xt_ref, bf16[1024,1024]{1,0:T(8,128)(2,1)S(1)} %get-tuple-element.26.refs_1_.adj_ref, f32[1024,128]{1,0:T(8,128)S(1)} %get-tuple-element.43.col_ref, bf16[128,256]{1,0:T(8,128)(2,1)S(1)} %collective-permute-done.7.rest_0_, ...), custom_call_target="tpu_custom_call" | custom-call | flops 805306368 | bytes 2883584 | tf_op jit(solution)/shard_map/gradient/pallas_call | solution.py:276
  40.3 1.3 %collective-permute-start.19 = (bf16[512,256]{1,0:T(8,128)(2,1)S(1)}, bf16[512,256]{1,0:T(8,128)(2,1)S(1)}, u32[]{:S(2)}, u32[]{:S(2)}) collective-permute-start(bf16[512,256]{1,0:T(8,128)(2,1)S(1)} %gradient.5), channel_id=1, source_target_pairs={{0,8},{24,16},{1,9},{25,17},{2,10},{26,18},{3,11},{27,19},{4,12},{... | collective-permute-start | bytes 786440 | tf_op jit(solution)/shard_map/ppermute | solution.py:329
  41.7 0.7 collective-permute-start.16
  42.4 0.7 collective-permute-start.21
  43.1 1.3 %collective-permute-start.24 = (bf16[256,256]{1,0:T(8,128)(2,1)S(1)}, bf16[256,256]{1,0:T(8,128)(2,1)S(1)}, u32[]{:S(2)}, u32[]{:S(2)}) collective-permute-start(bf16[256,256]{1,0:T(8,128)(2,1)S(1)} %reduce-precision_convert_fusion.6.sent_ref), channel_id=1, source_target_pairs={{8,0},{16,24},{9,1},{17,25},{10,2},{18,26},{11,3},{19,27},{12,4},{... | collective-permute-start | bytes 393224 | tf_op jit(solution)/shard_map/ppermute | solution.py:345
  44.5 1.3 %collective-permute-start.25 = (bf16[256,256]{1,0:T(8,128)(2,1)S(1)}, bf16[256,256]{1,0:T(8,128)(2,1)S(1)}, u32[]{:S(2)}, u32[]{:S(2)}) collective-permute-start(bf16[256,256]{1,0:T(8,128)(2,1)S(1)} %reduce-precision_convert_fusion.4.sent_ref), channel_id=1, source_target_pairs={{8,0},{16,24},{9,1},{17,25},{10,2},{18,26},{11,3},{19,27},{12,4},{... | collective-permute-start | bytes 393224 | tf_op jit(solution)/shard_map/ppermute | solution.py:345
  45.8 6.0 %collective-permute-done.19 = bf16[512,256]{1,0:T(8,128)(2,1)S(1)} collective-permute-done((bf16[512,256]{1,0:T(8,128)(2,1)S(1)}, bf16[512,256]{1,0:T(8,128)(2,1)S(1)}, u32[]{:S(2)}, u32[]{:S(2)}) %collective-permute-start.19) | collective-permute-done | bytes 262176 | tf_op jit(solution)/shard_map/ppermute | solution.py:329
  51.8 0.7 collective-permute-start.22
  52.6 0.7 collective-permute-start.17
  53.3 2.7 %collective-permute-done.25.got_ref = bf16[256,256]{1,0:T(8,128)(2,1)S(1)} collective-permute-done((bf16[256,256]{1,0:T(8,128)(2,1)S(1)}, bf16[256,256]{1,0:T(8,128)(2,1)S(1)}, u32[]{:S(2)}, u32[]{:S(2)}) %collective-permute-start.25) | collective-permute-done | bytes 131104 | tf_op jit(solution)/shard_map/ppermute | solution.py:345
  56.0 0.7 finish.4.rest_0_
  56.8 1.3 %collective-permute-start.23 = (bf16[512,256]{1,0:T(8,128)(2,1)S(1)}, bf16[512,256]{1,0:T(8,128)(2,1)S(1)}, u32[]{:S(2)}, u32[]{:S(2)}) collective-permute-start(bf16[512,256]{1,0:T(8,128)(2,1)S(1)} %reduce-precision_convert_fusion.sent_ref), channel_id=1, source_target_pairs={{8,0},{16,24},{9,1},{17,25},{10,2},{18,26},{11,3},{19,27},{12,4},{... | collective-permute-start | bytes 786440 | tf_op jit(solution)/shard_map/ppermute | solution.py:345
  58.2 1.3 %collective-permute-start.18 = (bf16[512,256]{1,0:T(8,128)(2,1)S(1)}, bf16[512,256]{1,0:T(8,128)(2,1)S(1)}, u32[]{:S(2)}, u32[]{:S(2)}) collective-permute-start(bf16[512,256]{1,0:T(8,128)(2,1)S(1)} %reduce-precision_convert_fusion.2.sent_ref), channel_id=1, source_target_pairs={{8,0},{16,24},{9,1},{17,25},{10,2},{18,26},{11,3},{19,27},{12,4},{... | collective-permute-start | bytes 786440 | tf_op jit(solution)/shard_map/ppermute | solution.py:345
  59.5 0.7 finish.5.rest_0_
  60.3 12.0 %collective-permute-done.23.got_ref = bf16[512,256]{1,0:T(8,128)(2,1)S(1)} collective-permute-done((bf16[512,256]{1,0:T(8,128)(2,1)S(1)}, bf16[512,256]{1,0:T(8,128)(2,1)S(1)}, u32[]{:S(2)}, u32[]{:S(2)}) %collective-permute-start.23) | collective-permute-done | bytes 262176 | tf_op jit(solution)/shard_map/ppermute | solution.py:345
  72.2 0.9 %finish.6.rest_0_ = f32[3,512,256]{2,1,0:T(8,128)} custom-call(bf16[512,256]{1,0:T(8,128)(2,1)S(1)} %collective-permute-done.23.got_ref, bf16[512,256]{1,0:T(8,128)(2,1)S(1)} %reduce-precision_convert_fusion.sent_ref, f32[3,512,256]{2,1,0:T(8,128)} %finish.5.rest_0_), custom_call_target="tpu_custom_call", output_to_operand_aliasing={{}: (2, {})} | custom-call | flops 2000000000 | bytes 1048576 | tf_op jit(solution)/shard_map/finish/pallas_call | solution.py:303
  73.1 3.7 %collective-permute-done.18.got_ref = bf16[512,256]{1,0:T(8,128)(2,1)S(1)} collective-permute-done((bf16[512,256]{1,0:T(8,128)(2,1)S(1)}, bf16[512,256]{1,0:T(8,128)(2,1)S(1)}, u32[]{:S(2)}, u32[]{:S(2)}) %collective-permute-start.18) | collective-permute-done | bytes 262176 | tf_op jit(solution)/shard_map/ppermute | solution.py:345
  76.8 0.9 %finish.7 = f32[3,512,256]{2,1,0:T(8,128)} custom-call(bf16[512,256]{1,0:T(8,128)(2,1)S(1)} %collective-permute-done.18.got_ref, bf16[512,256]{1,0:T(8,128)(2,1)S(1)} %reduce-precision_convert_fusion.2.sent_ref, f32[3,512,256]{2,1,0:T(8,128)} %finish.6.rest_0_), custom_call_target="tpu_custom_call", output_to_operand_aliasing={{}: (2, {})} | custom-call | flops 2000000000 | bytes 1048576 | tf_op jit(solution)/shard_map/finish/pallas_call | solution.py:303
  (42 shorter events, 0.5 us)
Async XLA Ops:
  0.6 1.0 %copy-start.5 = (s32[8,3,4,8,128]{4,3,2,1,0:T(8,128)S(1)}, s32[8,3,4,8,128]{4,3,2,1,0:T(8,128)}, u32[]{:S(2)}) copy-start(s32[8,3,4,8,128]{4,3,2,1,0:T(8,128)} %pat_ref.1) | copy-start | bytes 1179652
  1.6 0.7 copy-start.6
  2.3 0.7 copy-start.7
  3.0 4.1 %copy-start = (bf16[1024,512]{1,0:T(8,128)(2,1)S(1)}, bf16[1024,512]{1,0:T(8,128)(2,1)}, u32[]{:S(2)}) copy-start(bf16[1024,512]{1,0:T(8,128)(2,1)} %x_ref.1) | copy-start | bytes 3145732
  3.0 4.1 %copy-start.4 = (bf16[3,512,256]{2,1,0:T(8,128)(2,1)S(1)}, bf16[3,512,256]{2,1,0:T(8,128)(2,1)}, u32[]{:S(2)}) copy-start(bf16[3,512,256]{2,1,0:T(8,128)(2,1)} %refs_4_.1) | copy-start | bytes 2359300
  7.1 13.3 %copy-start.1 = (bf16[128,256]{1,0:T(8,128)(2,1)S(1)}, bf16[128,256]{1,0:T(8,128)(2,1)}, u32[]{:S(2)}) copy-start(bf16[128,256]{1,0:T(8,128)(2,1)} %refs_7_.1) | copy-start | bytes 196612
  7.2 13.3 %copy-start.2 = (f32[3,256]{1,0:T(4,128)S(1)}, f32[3,256]{1,0:T(4,128)}, u32[]{:S(2)}) copy-start(f32[3,256]{1,0:T(4,128)} %refs_6_.1) | copy-start | bytes 9220
  7.2 13.2 %copy-start.3 = (s32[128]{0:T(128)S(1)}, s32[128]{0:T(128)}, u32[]{:S(2)}) copy-start(s32[128]{0:T(128)} %param.13) | copy-start | bytes 1540
  10.2 1.4 %collective-permute-start = (bf16[128,256]{1,0:T(8,128)(2,1)S(1)}, bf16[128,256]{1,0:T(8,128)(2,1)S(1)}, u32[]{:S(2)}, u32[]{:S(2)}) collective-permute-start(bf16[128,256]{1,0:T(8,128)(2,1)S(1)} %get-tuple-element.29), channel_id=1, source_target_pairs={{0,1},{1,0},{2,3},{3,2},{4,5},{5,4},{6,7},{7,6},{8,9},{9,8},{10,11... | collective-permute-start | bytes 196616 | tf_op jit(solution)/shard_map/ppermute | solution.py:354
  10.7 4.8 %collective-permute-start.2 = (bf16[128,256]{1,0:T(8,128)(2,1)S(1)}, bf16[128,256]{1,0:T(8,128)(2,1)S(1)}, u32[]{:S(2)}, u32[]{:S(2)}) collective-permute-start(bf16[128,256]{1,0:T(8,128)(2,1)S(1)} %get-tuple-element.31), channel_id=1, source_target_pairs={{0,1},{1,0},{2,3},{3,2},{4,5},{5,4},{6,7},{7,6},{8,9},{9,8},{10,11... | collective-permute-start | bytes 196616 | tf_op jit(solution)/shard_map/ppermute | solution.py:354
  10.8 5.3 %collective-permute-start.4 = (bf16[128,256]{1,0:T(8,128)(2,1)S(1)}, bf16[128,256]{1,0:T(8,128)(2,1)S(1)}, u32[]{:S(2)}, u32[]{:S(2)}) collective-permute-start(bf16[128,256]{1,0:T(8,128)(2,1)S(1)} %get-tuple-element.33), channel_id=1, source_target_pairs={{0,1},{1,0},{2,3},{3,2},{4,5},{5,4},{6,7},{7,6},{8,9},{9,8},{10,11... | collective-permute-start | bytes 196616 | tf_op jit(solution)/shard_map/ppermute | solution.py:354
  11.2 5.1 %collective-permute-start.6 = (bf16[128,256]{1,0:T(8,128)(2,1)S(1)}, bf16[128,256]{1,0:T(8,128)(2,1)S(1)}, u32[]{:S(2)}, u32[]{:S(2)}) collective-permute-start(bf16[128,256]{1,0:T(8,128)(2,1)S(1)} %get-tuple-element.34), channel_id=1, source_target_pairs={{0,1},{1,0},{2,3},{3,2},{4,5},{5,4},{6,7},{7,6},{8,9},{9,8},{10,11... | collective-permute-start | bytes 196616 | tf_op jit(solution)/shard_map/ppermute | solution.py:354
  11.6 6.3 %collective-permute-start.1 = (bf16[128,256]{1,0:T(8,128)(2,1)S(1)}, bf16[128,256]{1,0:T(8,128)(2,1)S(1)}, u32[]{:S(2)}, u32[]{:S(2)}) collective-permute-start(bf16[128,256]{1,0:T(8,128)(2,1)S(1)} %add_convert_fusion.2), channel_id=1, source_target_pairs={{0,6},{1,7},{2,4},{3,5},{4,2},{5,3},{6,0},{7,1},{8,14},{9,15},{10,... | collective-permute-start | bytes 196616 | tf_op jit(solution)/shard_map/ppermute | solution.py:354
  15.5 4.3 %collective-permute-start.3 = (bf16[128,256]{1,0:T(8,128)(2,1)S(1)}, bf16[128,256]{1,0:T(8,128)(2,1)S(1)}, u32[]{:S(2)}, u32[]{:S(2)}) collective-permute-start(bf16[128,256]{1,0:T(8,128)(2,1)S(1)} %add_convert_fusion.1), channel_id=1, source_target_pairs={{0,4},{1,5},{2,6},{3,7},{4,0},{5,1},{6,2},{7,3},{8,12},{9,13},{10,... | collective-permute-start | bytes 196616 | tf_op jit(solution)/shard_map/ppermute | solution.py:354
  16.1 4.3 %collective-permute-start.5 = (bf16[128,256]{1,0:T(8,128)(2,1)S(1)}, bf16[128,256]{1,0:T(8,128)(2,1)S(1)}, u32[]{:S(2)}, u32[]{:S(2)}) collective-permute-start(bf16[128,256]{1,0:T(8,128)(2,1)S(1)} %add_convert_fusion), channel_id=1, source_target_pairs={{0,2},{1,3},{2,0},{3,1},{4,6},{5,7},{6,4},{7,5},{8,10},{9,11},{10,... | collective-permute-start | bytes 196616 | tf_op jit(solution)/shard_map/ppermute | solution.py:354
  21.2 4.6 %collective-permute-start.9 = (bf16[128,256]{1,0:T(8,128)(2,1)S(1)}, bf16[128,256]{1,0:T(8,128)(2,1)S(1)}, u32[]{:S(2)}, u32[]{:S(2)}) collective-permute-start(bf16[128,256]{1,0:T(8,128)(2,1)S(1)} %get-tuple-element.39.rest_3_), channel_id=1, source_target_pairs={{0,2},{1,3},{2,0},{3,1},{4,6},{5,7},{6,4},{7,5},{8,10},{9,11},{10,... | collective-permute-start | bytes 196616 | tf_op jit(solution)/shard_map/ppermute | solution.py:354
  21.8 4.5 %collective-permute-start.8 = (bf16[128,256]{1,0:T(8,128)(2,1)S(1)}, bf16[128,256]{1,0:T(8,128)(2,1)S(1)}, u32[]{:S(2)}, u32[]{:S(2)}) collective-permute-start(bf16[128,256]{1,0:T(8,128)(2,1)S(1)} %get-tuple-element.39.rest_3_), channel_id=1, source_target_pairs={{0,4},{1,5},{2,6},{3,7},{4,0},{5,1},{6,2},{7,3},{8,12},{9,13},{10,... | collective-permute-start | bytes 196616 | tf_op jit(solution)/shard_map/ppermute | solution.py:354
  23.2 5.2 %collective-permute-start.7 = (bf16[128,256]{1,0:T(8,128)(2,1)S(1)}, bf16[128,256]{1,0:T(8,128)(2,1)S(1)}, u32[]{:S(2)}, u32[]{:S(2)}) collective-permute-start(bf16[128,256]{1,0:T(8,128)(2,1)S(1)} %get-tuple-element.39.rest_3_), channel_id=1, source_target_pairs={{0,6},{1,7},{2,4},{3,5},{4,2},{5,3},{6,0},{7,1},{8,14},{9,15},{10,... | collective-permute-start | bytes 196616 | tf_op jit(solution)/shard_map/ppermute | solution.py:354
  24.7 4.6 %collective-permute-start.10 = (bf16[128,256]{1,0:T(8,128)(2,1)S(1)}, bf16[128,256]{1,0:T(8,128)(2,1)S(1)}, u32[]{:S(2)}, u32[]{:S(2)}) collective-permute-start(bf16[128,256]{1,0:T(8,128)(2,1)S(1)} %get-tuple-element.39.rest_3_), channel_id=1, source_target_pairs={{0,1},{1,0},{2,3},{3,2},{4,5},{5,4},{6,7},{7,6},{8,9},{9,8},{10,11... | collective-permute-start | bytes 196616 | tf_op jit(solution)/shard_map/ppermute | solution.py:354
  25.8 3.5 %collective-permute-start.11 = (bf16[128,256]{1,0:T(8,128)(2,1)S(1)}, bf16[128,256]{1,0:T(8,128)(2,1)S(1)}, u32[]{:S(2)}, u32[]{:S(2)}) collective-permute-start(bf16[128,256]{1,0:T(8,128)(2,1)S(1)} %collective-permute-done.9.rest_2_), channel_id=1, source_target_pairs={{0,1},{1,0},{2,3},{3,2},{4,5},{5,4},{6,7},{7,6},{8,9},{9,8},{10,11... | collective-permute-start | bytes 196616 | tf_op jit(solution)/shard_map/ppermute | solution.py:354
  26.3 3.0 %collective-permute-start.12 = (bf16[128,256]{1,0:T(8,128)(2,1)S(1)}, bf16[128,256]{1,0:T(8,128)(2,1)S(1)}, u32[]{:S(2)}, u32[]{:S(2)}) collective-permute-start(bf16[128,256]{1,0:T(8,128)(2,1)S(1)} %collective-permute-done.8.rest_1_), channel_id=1, source_target_pairs={{0,1},{1,0},{2,3},{3,2},{4,5},{5,4},{6,7},{7,6},{8,9},{9,8},{10,11... | collective-permute-start | bytes 196616 | tf_op jit(solution)/shard_map/ppermute | solution.py:354
  28.4 1.3 %collective-permute-start.13 = (bf16[128,256]{1,0:T(8,128)(2,1)S(1)}, bf16[128,256]{1,0:T(8,128)(2,1)S(1)}, u32[]{:S(2)}, u32[]{:S(2)}) collective-permute-start(bf16[128,256]{1,0:T(8,128)(2,1)S(1)} %collective-permute-done.7.rest_0_), channel_id=1, source_target_pairs={{0,1},{1,0},{2,3},{3,2},{4,5},{5,4},{6,7},{7,6},{8,9},{9,8},{10,11... | collective-permute-start | bytes 196616 | tf_op jit(solution)/shard_map/ppermute | solution.py:354
  31.2 10.5 %collective-permute-start.15 = (bf16[256,256]{1,0:T(8,128)(2,1)S(1)}, bf16[256,256]{1,0:T(8,128)(2,1)S(1)}, u32[]{:S(2)}, u32[]{:S(2)}) collective-permute-start(bf16[256,256]{1,0:T(8,128)(2,1)S(1)} %get-tuple-element.41), channel_id=1, source_target_pairs={{0,8},{24,16},{1,9},{25,17},{2,10},{26,18},{3,11},{27,19},{4,12},{... | collective-permute-start | bytes 393224 | tf_op jit(solution)/shard_map/ppermute | solution.py:329
  34.7 7.7 %collective-permute-start.20 = (bf16[256,256]{1,0:T(8,128)(2,1)S(1)}, bf16[256,256]{1,0:T(8,128)(2,1)S(1)}, u32[]{:S(2)}, u32[]{:S(2)}) collective-permute-start(bf16[256,256]{1,0:T(8,128)(2,1)S(1)} %get-tuple-element.44), channel_id=1, source_target_pairs={{0,8},{24,16},{1,9},{25,17},{2,10},{26,18},{3,11},{27,19},{4,12},{... | collective-permute-start | bytes 393224 | tf_op jit(solution)/shard_map/ppermute | solution.py:329
  37.5 15.1 %collective-permute-start.14 = (bf16[512,256]{1,0:T(8,128)(2,1)S(1)}, bf16[512,256]{1,0:T(8,128)(2,1)S(1)}, u32[]{:S(2)}, u32[]{:S(2)}) collective-permute-start(bf16[512,256]{1,0:T(8,128)(2,1)S(1)} %gradient.3), channel_id=1, source_target_pairs={{0,8},{24,16},{1,9},{25,17},{2,10},{26,18},{3,11},{27,19},{4,12},{... | collective-permute-start | bytes 786440 | tf_op jit(solution)/shard_map/ppermute | solution.py:329
  40.3 11.5 %collective-permute-start.19 = (bf16[512,256]{1,0:T(8,128)(2,1)S(1)}, bf16[512,256]{1,0:T(8,128)(2,1)S(1)}, u32[]{:S(2)}, u32[]{:S(2)}) collective-permute-start(bf16[512,256]{1,0:T(8,128)(2,1)S(1)} %gradient.5), channel_id=1, source_target_pairs={{0,8},{24,16},{1,9},{25,17},{2,10},{26,18},{3,11},{27,19},{4,12},{... | collective-permute-start | bytes 786440 | tf_op jit(solution)/shard_map/ppermute | solution.py:329
  41.7 1.4 %collective-permute-start.16 = (bf16[256,256]{1,0:T(8,128)(2,1)S(1)}, bf16[256,256]{1,0:T(8,128)(2,1)S(1)}, u32[]{:S(2)}, u32[]{:S(2)}) collective-permute-start(bf16[256,256]{1,0:T(8,128)(2,1)S(1)} %reduce-precision_convert_fusion.7), channel_id=1, source_target_pairs={{8,16},{16,8},{9,17},{17,9},{10,18},{18,10},{11,19},{19,11},{12,20... | collective-permute-start | bytes 393224 | tf_op jit(solution)/shard_map/ppermute | solution.py:336
  42.4 2.0 %collective-permute-start.21 = (bf16[256,256]{1,0:T(8,128)(2,1)S(1)}, bf16[256,256]{1,0:T(8,128)(2,1)S(1)}, u32[]{:S(2)}, u32[]{:S(2)}) collective-permute-start(bf16[256,256]{1,0:T(8,128)(2,1)S(1)} %reduce-precision_convert_fusion.5), channel_id=1, source_target_pairs={{8,16},{16,8},{9,17},{17,9},{10,18},{18,10},{11,19},{19,11},{12,20... | collective-permute-start | bytes 393224 | tf_op jit(solution)/shard_map/ppermute | solution.py:336
  43.1 16.4 %collective-permute-start.24 = (bf16[256,256]{1,0:T(8,128)(2,1)S(1)}, bf16[256,256]{1,0:T(8,128)(2,1)S(1)}, u32[]{:S(2)}, u32[]{:S(2)}) collective-permute-start(bf16[256,256]{1,0:T(8,128)(2,1)S(1)} %reduce-precision_convert_fusion.6.sent_ref), channel_id=1, source_target_pairs={{8,0},{16,24},{9,1},{17,25},{10,2},{18,26},{11,3},{19,27},{12,4},{... | collective-permute-start | bytes 393224 | tf_op jit(solution)/shard_map/ppermute | solution.py:345
  44.5 11.5 %collective-permute-start.25 = (bf16[256,256]{1,0:T(8,128)(2,1)S(1)}, bf16[256,256]{1,0:T(8,128)(2,1)S(1)}, u32[]{:S(2)}, u32[]{:S(2)}) collective-permute-start(bf16[256,256]{1,0:T(8,128)(2,1)S(1)} %reduce-precision_convert_fusion.4.sent_ref), channel_id=1, source_target_pairs={{8,0},{16,24},{9,1},{17,25},{10,2},{18,26},{11,3},{19,27},{12,4},{... | collective-permute-start | bytes 393224 | tf_op jit(solution)/shard_map/ppermute | solution.py:345
  51.8 4.9 %collective-permute-start.22 = (bf16[512,256]{1,0:T(8,128)(2,1)S(1)}, bf16[512,256]{1,0:T(8,128)(2,1)S(1)}, u32[]{:S(2)}, u32[]{:S(2)}) collective-permute-start(bf16[512,256]{1,0:T(8,128)(2,1)S(1)} %reduce-precision_convert_fusion.1), channel_id=1, source_target_pairs={{8,16},{16,8},{9,17},{17,9},{10,18},{18,10},{11,19},{19,11},{12,20... | collective-permute-start | bytes 786440 | tf_op jit(solution)/shard_map/ppermute | solution.py:336
  52.6 5.5 %collective-permute-start.17 = (bf16[512,256]{1,0:T(8,128)(2,1)S(1)}, bf16[512,256]{1,0:T(8,128)(2,1)S(1)}, u32[]{:S(2)}, u32[]{:S(2)}) collective-permute-start(bf16[512,256]{1,0:T(8,128)(2,1)S(1)} %reduce-precision_convert_fusion.3), channel_id=1, source_target_pairs={{8,16},{16,8},{9,17},{17,9},{10,18},{18,10},{11,19},{19,11},{12,20... | collective-permute-start | bytes 786440 | tf_op jit(solution)/shard_map/ppermute | solution.py:336
  56.8 15.4 %collective-permute-start.23 = (bf16[512,256]{1,0:T(8,128)(2,1)S(1)}, bf16[512,256]{1,0:T(8,128)(2,1)S(1)}, u32[]{:S(2)}, u32[]{:S(2)}) collective-permute-start(bf16[512,256]{1,0:T(8,128)(2,1)S(1)} %reduce-precision_convert_fusion.sent_ref), channel_id=1, source_target_pairs={{8,0},{16,24},{9,1},{17,25},{10,2},{18,26},{11,3},{19,27},{12,4},{... | collective-permute-start | bytes 786440 | tf_op jit(solution)/shard_map/ppermute | solution.py:345
  58.2 18.6 %collective-permute-start.18 = (bf16[512,256]{1,0:T(8,128)(2,1)S(1)}, bf16[512,256]{1,0:T(8,128)(2,1)S(1)}, u32[]{:S(2)}, u32[]{:S(2)}) collective-permute-start(bf16[512,256]{1,0:T(8,128)(2,1)S(1)} %reduce-precision_convert_fusion.2.sent_ref), channel_id=1, source_target_pairs={{8,0},{16,24},{9,1},{17,25},{10,2},{18,26},{11,3},{19,27},{12,4},{... | collective-permute-start | bytes 786440 | tf_op jit(solution)/shard_map/ppermute | solution.py:345

commit v3 on v2

--- a/solution.py
+++ b/solution.py
@@ -105,15 +105,21 @@
 
 def add_edges(relation, places, src_ref, cnt_ref, pat_ref):
     bit = jnp.left_shift(1, lax.broadcasted_iota(jnp.int32, (16, BLK), 0))
+    group = 4
     for s in range(src_ref.shape[1]):
-        for b, (ref, lanes) in enumerate(places):
-            words = live_words(relation, s, b, cnt_ref, pat_ref)
-            row0 = pl.multiple_of(src_ref[relation, s, b] * BLK, BLK)
-            parts = [
-                jnp.where((words[w : w + 1, :] & bit) != 0, 1.0, 0.0)
-                for w in range(words.shape[0])
-            ]
-            ref[pl.ds(row0, BLK), lanes] += jnp.concatenate(parts, axis=0).astype(BF16)
+        for b0 in range(0, len(places), group):
+            held = []
+            for b in range(b0, min(b0 + group, len(places))):
+                ref, lanes = places[b]
+                row0 = pl.multiple_of(src_ref[relation, s, b] * BLK, BLK)
+                held.append((ref, pl.ds(row0, BLK), lanes, ref[pl.ds(row0, BLK), lanes]))
+            for b, (ref, rows, lanes, tile) in enumerate(held, b0):
+                words = live_words(relation, s, b, cnt_ref, pat_ref)
+                parts = [
+                    jnp.where((words[w : w + 1, :] & bit) != 0, 1.0, 0.0)
+                    for w in range(words.shape[0])
+                ]
+                ref[rows, lanes] = tile + jnp.concatenate(parts, axis=0).astype(BF16)
 
 
 def inverse_degrees(relation, inv_ref, src_ref, cnt_ref, pat_ref):
@@ -390,6 +396,7 @@
     pieces = forward(inv_deg, adj, features, proj_weight, n_feat)
     received = reduce_pieces(pieces, n_feat)
     x_t, col = transposed(features, inv_deg)
+    received, x_t, col = lax.optimization_barrier((received, x_t, col))
     activations, slope = combine(received, node_type, type_gain, cotangent)
     slopes = gather_pieces(slope, n_feat)
     chunks = []

time: 78.1 us -> 78.2 us (level)
  no operation moved by 1% of the time
where the time goes in v3:
time: 78.2 us; the launch traced here: 77.8 us
  waiting for transfers between devices  32.9 us (42%)
  starting transfers between devices  24.5 us (31%)
  Pallas kernels  16.6 us (21%)
  local copies, waits for them, and re-layouts  2.39 us (3%)
  between operations  0.97 us (1%)
    ppermute x4, waiting for transfers between devices, chain_sum(): got = lax.ppermute(sent, 'dom', [(low, low - 1), (high, high + 1)])  18.4 us
    ppermute x14, starting transfers between devices, swap(): return lax.ppermute(value, 'feat', [(i, i ^ k) for i in range(n_feat)])  9.23 us
    ppermute x14, waiting for transfers between devices, swap(): return lax.ppermute(value, 'feat', [(i, i ^ k) for i in range(n_feat)])  8.53 us
    ppermute x4, starting transfers between devices, chain_sum(): got = lax.ppermute(sent, 'dom', perm)  7.4 us
    ppermute x4, waiting for transfers between devices, chain_sum(): got = lax.ppermute(sent, 'dom', perm)  5.97 us
    ppermute x4, starting transfers between devices, chain_sum(): got = lax.ppermute(sent, 'dom', [(low, low - 1), (high, high + 1)])  5.17 us
    pallas_call x3, Pallas kernels, gradient(): pl.pallas_call(functools.partial(gradient_kernel, len(slopes)), name='gra...  4.53 us
    pallas_call x1, Pallas kernels, adjacency(): pl.pallas_call(adjacency_kernel, name='adjacency', out_shape=[jax.ShapeDt...  4.25 us
  transfers between devices with their start and end apart: 26, of which 12 were waited for; matrix products, arithmetic and copies ran while one was open for 1% of the time, Pallas kernels for 8%

profile of v3, /device:TPU:0, one launch (start us, length us, event | category | flops | bytes accessed | tf_op | source)
XLA Modules:
  0.0 77.8 jit_solution(1145525263458225583)
XLA Ops:
  0.6 1.0 %copy-done.5 = s32[8,3,4,8,128]{4,3,2,1,0:T(8,128)S(1)} copy-done((s32[8,3,4,8,128]{4,3,2,1,0:T(8,128)S(1)}, s32[8,3,4,8,128]{4,3,2,1,0:T(8,128)}, u32[]{:S(2)}) %copy-start.5) | copy-done | bytes 393240
  1.6 0.7 copy-done.6
  2.3 0.7 copy-done.7
  3.0 4.2 %adjacency.1 = (f32[3,8,1024]{2,1,0:T(8,128)S(1)}, bf16[1024,1024]{1,0:T(8,128)(2,1)S(1)}, bf16[1024,1024]{1,0:T(8,128)(2,1)S(1)}, bf16[1024,1024]{1,0:T(8,128)(2,1)S(1)}) custom-call(s32[3,4,8]{2,1,0:T(4,128)S(1)} %bitcast.4, s32[3,8]{1,0:T(4,128)S(1)} %bitcast.5, s32[8,3,4,8,128]{4,3,2,1,0:T(8,128)S(1)} %copy-done.5), custom_call_target="tpu_custom_call" | custom-call | flops 3145728000 | bytes 6291456 | tf_op jit(solution)/shard_map/adjacency/pallas_call | solution.py:152
  7.3 3.0 %forward.1 = (f32[128,256]{1,0:T(8,128)S(1)}, bf16[128,256]{1,0:T(8,128)(2,1)S(1)}, f32[128,256]{1,0:T(8,128)S(1)}, bf16[128,256]{1,0:T(8,128)(2,1)S(1)}, f32[12...) custom-call(f32[3,8,1024]{2,1,0:T(8,128)S(1)} %get-tuple-element.33.inv_, ...), custom_call_target="tpu_custom_call" | custom-call | flops 2415919104 | bytes 6291456 | tf_op jit(solution)/shard_map/forward/pallas_call | solution.py:193
  10.3 0.5 collective-permute-start
  10.8 0.1 collective-permute-start.2
  10.9 0.4 collective-permute-start.4
  11.3 0.1 collective-permute-start.6
  11.4 0.3 collective-permute-done
  11.7 3.9 %collective-permute-start.1 = (bf16[128,256]{1,0:T(8,128)(2,1)S(1)}, bf16[128,256]{1,0:T(8,128)(2,1)S(1)}, u32[]{:S(2)}, u32[]{:S(2)}) collective-permute-start(bf16[128,256]{1,0:T(8,128)(2,1)S(1)} %add_convert_fusion.2), channel_id=1, source_target_pairs={{0,6},{1,7},{2,4},{3,5},{4,2},{5,3},{6,0},{7,1},{8,14},{9,15},{10,... | collective-permute-start | bytes 196616 | tf_op jit(solution)/shard_map/ppermute | solution.py:360
  15.6 0.6 collective-permute-start.3
  16.2 0.2 collective-permute-start.5
  16.4 0.9 %transposed.1 = (bf16[512,1024]{1,0:T(8,128)(2,1)S(1)}, f32[1024,128]{1,0:T(8,128)S(1)}, f32[1024,128]{1,0:T(8,128)S(1)}, f32[1024,128]{1,0:T(8,128)S(1)}) custom-call(bf16[1024,512]{1,0:T(8,128)(2,1)S(1)} %copy-done, f32[3,8,1024]{2,1,0:T(8,128)S(1)} %get-tuple-element.33.inv_ref), custom_call_target="tpu_custom_call" | custom-call | flops 1048576 | bytes 3145728 | tf_op jit(solution)/shard_map/transposed/pallas_call | solution.py:225
  17.3 0.7 collective-permute-done.1.refs_0_
  18.0 1.9 %collective-permute-done.3.refs_1_ = bf16[128,256]{1,0:T(8,128)(2,1)S(1)} collective-permute-done((bf16[128,256]{1,0:T(8,128)(2,1)S(1)}, bf16[128,256]{1,0:T(8,128)(2,1)S(1)}, u32[]{:S(2)}, u32[]{:S(2)}) %collective-permute-start.3) | collective-permute-done | bytes 65568 | tf_op jit(solution)/shard_map/ppermute | solution.py:360
  19.9 0.6 collective-permute-done.5.refs_2_
  20.5 0.7 combine.1
  21.3 0.6 collective-permute-start.9
  21.9 1.4 %collective-permute-start.8 = (bf16[128,256]{1,0:T(8,128)(2,1)S(1)}, bf16[128,256]{1,0:T(8,128)(2,1)S(1)}, u32[]{:S(2)}, u32[]{:S(2)}) collective-permute-start(bf16[128,256]{1,0:T(8,128)(2,1)S(1)} %get-tuple-element.57.rest_3_), channel_id=1, source_target_pairs={{0,4},{1,5},{2,6},{3,7},{4,0},{5,1},{6,2},{7,3},{8,12},{9,13},{10,... | collective-permute-start | bytes 196616 | tf_op jit(solution)/shard_map/ppermute | solution.py:360
  23.4 1.4 %collective-permute-start.7 = (bf16[128,256]{1,0:T(8,128)(2,1)S(1)}, bf16[128,256]{1,0:T(8,128)(2,1)S(1)}, u32[]{:S(2)}, u32[]{:S(2)}) collective-permute-start(bf16[128,256]{1,0:T(8,128)(2,1)S(1)} %get-tuple-element.57.rest_3_), channel_id=1, source_target_pairs={{0,6},{1,7},{2,4},{3,5},{4,2},{5,3},{6,0},{7,1},{8,14},{9,15},{10,... | collective-permute-start | bytes 196616 | tf_op jit(solution)/shard_map/ppermute | solution.py:360
  24.8 1.1 %collective-permute-done.9.rest_2_ = bf16[128,256]{1,0:T(8,128)(2,1)S(1)} collective-permute-done((bf16[128,256]{1,0:T(8,128)(2,1)S(1)}, bf16[128,256]{1,0:T(8,128)(2,1)S(1)}, u32[]{:S(2)}, u32[]{:S(2)}) %collective-permute-start.9) | collective-permute-done | bytes 65568 | tf_op jit(solution)/shard_map/ppermute | solution.py:360
  25.9 0.6 collective-permute-done.8.rest_1_
  26.5 2.0 %collective-permute-done.7.rest_0_ = bf16[128,256]{1,0:T(8,128)(2,1)S(1)} collective-permute-done((bf16[128,256]{1,0:T(8,128)(2,1)S(1)}, bf16[128,256]{1,0:T(8,128)(2,1)S(1)}, u32[]{:S(2)}, u32[]{:S(2)}) %collective-permute-start.7) | collective-permute-done | bytes 65568 | tf_op jit(solution)/shard_map/ppermute | solution.py:360
  28.5 1.2 %collective-permute-done.13.rest_7_ = bf16[128,256]{1,0:T(8,128)(2,1)S(1)} collective-permute-done((bf16[128,256]{1,0:T(8,128)(2,1)S(1)}, bf16[128,256]{1,0:T(8,128)(2,1)S(1)}, u32[]{:S(2)}, u32[]{:S(2)}) %collective-permute-start.13) | collective-permute-done | bytes 65568 | tf_op jit(solution)/shard_map/ppermute | solution.py:360
  29.8 1.5 %gradient.4 = (bf16[256,256]{1,0:T(8,128)(2,1)S(1)}, bf16[256,256]{1,0:T(8,128)(2,1)S(1)}) custom-call(bf16[512,1024]{1,0:T(8,128)(2,1)S(1)} %get-tuple-element.55.xt_ref, bf16[1024,1024]{1,0:T(8,128)(2,1)S(1)} %get-tuple-element.34.refs_0_.adj_ref, f32[1024,128]{1,0:T(8,128)S(1)} %get-tuple-element.58.col_ref, ...), custom_call_target="tpu_custom_call" | custom-call | flops 805306368 | bytes 2883584 | tf_op jit(solution)/shard_map/gradient/pallas_call | solution.py:282
  31.3 3.5 %collective-permute-start.15 = (bf16[256,256]{1,0:T(8,128)(2,1)S(1)}, bf16[256,256]{1,0:T(8,128)(2,1)S(1)}, u32[]{:S(2)}, u32[]{:S(2)}) collective-permute-start(bf16[256,256]{1,0:T(8,128)(2,1)S(1)} %get-tuple-element.59), channel_id=1, source_target_pairs={{0,8},{24,16},{1,9},{25,17},{2,10},{26,18},{3,11},{27,19},{4,12},{... | collective-permute-start | bytes 393224 | tf_op jit(solution)/shard_map/ppermute | solution.py:335
  34.8 1.3 %collective-permute-start.20 = (bf16[256,256]{1,0:T(8,128)(2,1)S(1)}, bf16[256,256]{1,0:T(8,128)(2,1)S(1)}, u32[]{:S(2)}, u32[]{:S(2)}) collective-permute-start(bf16[256,256]{1,0:T(8,128)(2,1)S(1)} %get-tuple-element.62), channel_id=1, source_target_pairs={{0,8},{24,16},{1,9},{25,17},{2,10},{26,18},{3,11},{27,19},{4,12},{... | collective-permute-start | bytes 393224 | tf_op jit(solution)/shard_map/ppermute | solution.py:335
  36.1 1.5 %gradient.3 = bf16[512,256]{1,0:T(8,128)(2,1)S(1)} custom-call(bf16[512,1024]{1,0:T(8,128)(2,1)S(1)} %get-tuple-element.55.xt_ref, bf16[1024,1024]{1,0:T(8,128)(2,1)S(1)} %get-tuple-element.36.refs_2_.adj_ref, f32[1024,128]{1,0:T(8,128)S(1)} %get-tuple-element.56.col_ref, bf16[128,256]{1,0:T(8,128)(2,1)S(1)} %collective-permute-done.7.rest_0_, ...), custom_call_target="tpu_custom_call" | custom-call | flops 805306368 | bytes 2883584 | tf_op jit(solution)/shard_map/gradient/pallas_call | solution.py:282
  37.6 1.3 %collective-permute-start.14 = (bf16[512,256]{1,0:T(8,128)(2,1)S(1)}, bf16[512,256]{1,0:T(8,128)(2,1)S(1)}, u32[]{:S(2)}, u32[]{:S(2)}) collective-permute-start(bf16[512,256]{1,0:T(8,128)(2,1)S(1)} %gradient.3), channel_id=1, source_target_pairs={{0,8},{24,16},{1,9},{25,17},{2,10},{26,18},{3,11},{27,19},{4,12},{... | collective-permute-start | bytes 786440 | tf_op jit(solution)/shard_map/ppermute | solution.py:335
  38.9 1.5 %gradient.5 = bf16[512,256]{1,0:T(8,128)(2,1)S(1)} custom-call(bf16[512,1024]{1,0:T(8,128)(2,1)S(1)} %get-tuple-element.55.xt_ref, bf16[1024,1024]{1,0:T(8,128)(2,1)S(1)} %get-tuple-element.35.refs_1_.adj_ref, f32[1024,128]{1,0:T(8,128)S(1)} %get-tuple-element.61.col_ref, bf16[128,256]{1,0:T(8,128)(2,1)S(1)} %collective-permute-done.7.rest_0_, ...), custom_call_target="tpu_custom_call" | custom-call | flops 805306368 | bytes 2883584 | tf_op jit(solution)/shard_map/gradient/pallas_call | solution.py:282
  40.4 1.3 %collective-permute-start.19 = (bf16[512,256]{1,0:T(8,128)(2,1)S(1)}, bf16[512,256]{1,0:T(8,128)(2,1)S(1)}, u32[]{:S(2)}, u32[]{:S(2)}) collective-permute-start(bf16[512,256]{1,0:T(8,128)(2,1)S(1)} %gradient.5), channel_id=1, source_target_pairs={{0,8},{24,16},{1,9},{25,17},{2,10},{26,18},{3,11},{27,19},{4,12},{... | collective-permute-start | bytes 786440 | tf_op jit(solution)/shard_map/ppermute | solution.py:335
  41.8 0.7 collective-permute-start.16
  42.5 0.7 collective-permute-start.21
  43.3 1.3 %collective-permute-start.24 = (bf16[256,256]{1,0:T(8,128)(2,1)S(1)}, bf16[256,256]{1,0:T(8,128)(2,1)S(1)}, u32[]{:S(2)}, u32[]{:S(2)}) collective-permute-start(bf16[256,256]{1,0:T(8,128)(2,1)S(1)} %reduce-precision_convert_fusion.6.sent_ref), channel_id=1, source_target_pairs={{8,0},{16,24},{9,1},{17,25},{10,2},{18,26},{11,3},{19,27},{12,4},{... | collective-permute-start | bytes 393224 | tf_op jit(solution)/shard_map/ppermute | solution.py:351
  44.6 1.3 %collective-permute-start.25 = (bf16[256,256]{1,0:T(8,128)(2,1)S(1)}, bf16[256,256]{1,0:T(8,128)(2,1)S(1)}, u32[]{:S(2)}, u32[]{:S(2)}) collective-permute-start(bf16[256,256]{1,0:T(8,128)(2,1)S(1)} %reduce-precision_convert_fusion.4.sent_ref), channel_id=1, source_target_pairs={{8,0},{16,24},{9,1},{17,25},{10,2},{18,26},{11,3},{19,27},{12,4},{... | collective-permute-start | bytes 393224 | tf_op jit(solution)/shard_map/ppermute | solution.py:351
  45.9 6.0 %collective-permute-done.19 = bf16[512,256]{1,0:T(8,128)(2,1)S(1)} collective-permute-done((bf16[512,256]{1,0:T(8,128)(2,1)S(1)}, bf16[512,256]{1,0:T(8,128)(2,1)S(1)}, u32[]{:S(2)}, u32[]{:S(2)}) %collective-permute-start.19) | collective-permute-done | bytes 262176 | tf_op jit(solution)/shard_map/ppermute | solution.py:335
  52.0 0.7 collective-permute-start.22
  52.7 0.7 collective-permute-start.17
  53.4 2.7 %collective-permute-done.25.got_ref = bf16[256,256]{1,0:T(8,128)(2,1)S(1)} collective-permute-done((bf16[256,256]{1,0:T(8,128)(2,1)S(1)}, bf16[256,256]{1,0:T(8,128)(2,1)S(1)}, u32[]{:S(2)}, u32[]{:S(2)}) %collective-permute-start.25) | collective-permute-done | bytes 131104 | tf_op jit(solution)/shard_map/ppermute | solution.py:351
  56.1 0.7 finish.4.rest_0_
  57.0 1.3 %collective-permute-start.23 = (bf16[512,256]{1,0:T(8,128)(2,1)S(1)}, bf16[512,256]{1,0:T(8,128)(2,1)S(1)}, u32[]{:S(2)}, u32[]{:S(2)}) collective-permute-start(bf16[512,256]{1,0:T(8,128)(2,1)S(1)} %reduce-precision_convert_fusion.sent_ref), channel_id=1, source_target_pairs={{8,0},{16,24},{9,1},{17,25},{10,2},{18,26},{11,3},{19,27},{12,4},{... | collective-permute-start | bytes 786440 | tf_op jit(solution)/shard_map/ppermute | solution.py:351
  58.3 1.3 %collective-permute-start.18 = (bf16[512,256]{1,0:T(8,128)(2,1)S(1)}, bf16[512,256]{1,0:T(8,128)(2,1)S(1)}, u32[]{:S(2)}, u32[]{:S(2)}) collective-permute-start(bf16[512,256]{1,0:T(8,128)(2,1)S(1)} %reduce-precision_convert_fusion.2.sent_ref), channel_id=1, source_target_pairs={{8,0},{16,24},{9,1},{17,25},{10,2},{18,26},{11,3},{19,27},{12,4},{... | collective-permute-start | bytes 786440 | tf_op jit(solution)/shard_map/ppermute | solution.py:351
  59.7 0.7 finish.5.rest_0_
  60.4 12.0 %collective-permute-done.23.got_ref = bf16[512,256]{1,0:T(8,128)(2,1)S(1)} collective-permute-done((bf16[512,256]{1,0:T(8,128)(2,1)S(1)}, bf16[512,256]{1,0:T(8,128)(2,1)S(1)}, u32[]{:S(2)}, u32[]{:S(2)}) %collective-permute-start.23) | collective-permute-done | bytes 262176 | tf_op jit(solution)/shard_map/ppermute | solution.py:351
  72.4 0.9 %finish.6.rest_0_ = f32[3,512,256]{2,1,0:T(8,128)} custom-call(bf16[512,256]{1,0:T(8,128)(2,1)S(1)} %collective-permute-done.23.got_ref, bf16[512,256]{1,0:T(8,128)(2,1)S(1)} %reduce-precision_convert_fusion.sent_ref, f32[3,512,256]{2,1,0:T(8,128)} %finish.5.rest_0_), custom_call_target="tpu_custom_call", output_to_operand_aliasing={{}: (2, {})} | custom-call | flops 2000000000 | bytes 1048576 | tf_op jit(solution)/shard_map/finish/pallas_call | solution.py:309
  73.3 3.6 %collective-permute-done.18.got_ref = bf16[512,256]{1,0:T(8,128)(2,1)S(1)} collective-permute-done((bf16[512,256]{1,0:T(8,128)(2,1)S(1)}, bf16[512,256]{1,0:T(8,128)(2,1)S(1)}, u32[]{:S(2)}, u32[]{:S(2)}) %collective-permute-start.18) | collective-permute-done | bytes 262176 | tf_op jit(solution)/shard_map/ppermute | solution.py:351
  76.9 0.9 %finish.7 = f32[3,512,256]{2,1,0:T(8,128)} custom-call(bf16[512,256]{1,0:T(8,128)(2,1)S(1)} %collective-permute-done.18.got_ref, bf16[512,256]{1,0:T(8,128)(2,1)S(1)} %reduce-precision_convert_fusion.2.sent_ref, f32[3,512,256]{2,1,0:T(8,128)} %finish.6.rest_0_), custom_call_target="tpu_custom_call", output_to_operand_aliasing={{}: (2, {})} | custom-call | flops 2000000000 | bytes 1048576 | tf_op jit(solution)/shard_map/finish/pallas_call | solution.py:309
  (42 shorter events, 0.5 us)
Async XLA Ops:
  0.6 1.0 %copy-start.5 = (s32[8,3,4,8,128]{4,3,2,1,0:T(8,128)S(1)}, s32[8,3,4,8,128]{4,3,2,1,0:T(8,128)}, u32[]{:S(2)}) copy-start(s32[8,3,4,8,128]{4,3,2,1,0:T(8,128)} %pat_ref.1) | copy-start | bytes 1179652
  1.6 0.7 copy-start.6
  2.3 0.7 copy-start.7
  3.0 4.3 %copy-start = (bf16[1024,512]{1,0:T(8,128)(2,1)S(1)}, bf16[1024,512]{1,0:T(8,128)(2,1)}, u32[]{:S(2)}) copy-start(bf16[1024,512]{1,0:T(8,128)(2,1)} %x_ref.1) | copy-start | bytes 3145732
  3.0 4.3 %copy-start.4 = (bf16[3,512,256]{2,1,0:T(8,128)(2,1)S(1)}, bf16[3,512,256]{2,1,0:T(8,128)(2,1)}, u32[]{:S(2)}) copy-start(bf16[3,512,256]{2,1,0:T(8,128)(2,1)} %refs_4_.1) | copy-start | bytes 2359300
  10.3 10.3 %copy-start.1 = (bf16[128,256]{1,0:T(8,128)(2,1)S(1)}, bf16[128,256]{1,0:T(8,128)(2,1)}, u32[]{:S(2)}) copy-start(bf16[128,256]{1,0:T(8,128)(2,1)} %refs_7_.1) | copy-start | bytes 196612
  10.3 10.3 %copy-start.2 = (f32[3,256]{1,0:T(4,128)S(1)}, f32[3,256]{1,0:T(4,128)}, u32[]{:S(2)}) copy-start(f32[3,256]{1,0:T(4,128)} %refs_6_.1) | copy-start | bytes 9220
  10.3 10.3 %copy-start.3 = (s32[128]{0:T(128)S(1)}, s32[128]{0:T(128)}, u32[]{:S(2)}) copy-start(s32[128]{0:T(128)} %param.13) | copy-start | bytes 1540
  10.3 1.4 %collective-permute-start = (bf16[128,256]{1,0:T(8,128)(2,1)S(1)}, bf16[128,256]{1,0:T(8,128)(2,1)S(1)}, u32[]{:S(2)}, u32[]{:S(2)}) collective-permute-start(bf16[128,256]{1,0:T(8,128)(2,1)S(1)} %get-tuple-element.38), channel_id=1, source_target_pairs={{0,1},{1,0},{2,3},{3,2},{4,5},{5,4},{6,7},{7,6},{8,9},{9,8},{10,11... | collective-permute-start | bytes 196616 | tf_op jit(solution)/shard_map/ppermute | solution.py:360
  10.8 4.8 %collective-permute-start.2 = (bf16[128,256]{1,0:T(8,128)(2,1)S(1)}, bf16[128,256]{1,0:T(8,128)(2,1)S(1)}, u32[]{:S(2)}, u32[]{:S(2)}) collective-permute-start(bf16[128,256]{1,0:T(8,128)(2,1)S(1)} %get-tuple-element.40), channel_id=1, source_target_pairs={{0,1},{1,0},{2,3},{3,2},{4,5},{5,4},{6,7},{7,6},{8,9},{9,8},{10,11... | collective-permute-start | bytes 196616 | tf_op jit(solution)/shard_map/ppermute | solution.py:360
  10.9 5.3 %collective-permute-start.4 = (bf16[128,256]{1,0:T(8,128)(2,1)S(1)}, bf16[128,256]{1,0:T(8,128)(2,1)S(1)}, u32[]{:S(2)}, u32[]{:S(2)}) collective-permute-start(bf16[128,256]{1,0:T(8,128)(2,1)S(1)} %get-tuple-element.42), channel_id=1, source_target_pairs={{0,1},{1,0},{2,3},{3,2},{4,5},{5,4},{6,7},{7,6},{8,9},{9,8},{10,11... | collective-permute-start | bytes 196616 | tf_op jit(solution)/shard_map/ppermute | solution.py:360
  11.3 6.0 %collective-permute-start.6 = (bf16[128,256]{1,0:T(8,128)(2,1)S(1)}, bf16[128,256]{1,0:T(8,128)(2,1)S(1)}, u32[]{:S(2)}, u32[]{:S(2)}) collective-permute-start(bf16[128,256]{1,0:T(8,128)(2,1)S(1)} %get-tuple-element.43), channel_id=1, source_target_pairs={{0,1},{1,0},{2,3},{3,2},{4,5},{5,4},{6,7},{7,6},{8,9},{9,8},{10,11... | collective-permute-start | bytes 196616 | tf_op jit(solution)/shard_map/ppermute | solution.py:360
  11.7 6.3 %collective-permute-start.1 = (bf16[128,256]{1,0:T(8,128)(2,1)S(1)}, bf16[128,256]{1,0:T(8,128)(2,1)S(1)}, u32[]{:S(2)}, u32[]{:S(2)}) collective-permute-start(bf16[128,256]{1,0:T(8,128)(2,1)S(1)} %add_convert_fusion.2), channel_id=1, source_target_pairs={{0,6},{1,7},{2,4},{3,5},{4,2},{5,3},{6,0},{7,1},{8,14},{9,15},{10,... | collective-permute-start | bytes 196616 | tf_op jit(solution)/shard_map/ppermute | solution.py:360
  15.6 4.3 %collective-permute-start.3 = (bf16[128,256]{1,0:T(8,128)(2,1)S(1)}, bf16[128,256]{1,0:T(8,128)(2,1)S(1)}, u32[]{:S(2)}, u32[]{:S(2)}) collective-permute-start(bf16[128,256]{1,0:T(8,128)(2,1)S(1)} %add_convert_fusion.1), channel_id=1, source_target_pairs={{0,4},{1,5},{2,6},{3,7},{4,0},{5,1},{6,2},{7,3},{8,12},{9,13},{10,... | collective-permute-start | bytes 196616 | tf_op jit(solution)/shard_map/ppermute | solution.py:360
  16.2 4.3 %collective-permute-start.5 = (bf16[128,256]{1,0:T(8,128)(2,1)S(1)}, bf16[128,256]{1,0:T(8,128)(2,1)S(1)}, u32[]{:S(2)}, u32[]{:S(2)}) collective-permute-start(bf16[128,256]{1,0:T(8,128)(2,1)S(1)} %add_convert_fusion), channel_id=1, source_target_pairs={{0,2},{1,3},{2,0},{3,1},{4,6},{5,7},{6,4},{7,5},{8,10},{9,11},{10,... | collective-permute-start | bytes 196616 | tf_op jit(solution)/shard_map/ppermute | solution.py:360
  21.3 4.6 %collective-permute-start.9 = (bf16[128,256]{1,0:T(8,128)(2,1)S(1)}, bf16[128,256]{1,0:T(8,128)(2,1)S(1)}, u32[]{:S(2)}, u32[]{:S(2)}) collective-permute-start(bf16[128,256]{1,0:T(8,128)(2,1)S(1)} %get-tuple-element.57.rest_3_), channel_id=1, source_target_pairs={{0,2},{1,3},{2,0},{3,1},{4,6},{5,7},{6,4},{7,5},{8,10},{9,11},{10,... | collective-permute-start | bytes 196616 | tf_op jit(solution)/shard_map/ppermute | solution.py:360
  21.9 4.5 %collective-permute-start.8 = (bf16[128,256]{1,0:T(8,128)(2,1)S(1)}, bf16[128,256]{1,0:T(8,128)(2,1)S(1)}, u32[]{:S(2)}, u32[]{:S(2)}) collective-permute-start(bf16[128,256]{1,0:T(8,128)(2,1)S(1)} %get-tuple-element.57.rest_3_), channel_id=1, source_target_pairs={{0,4},{1,5},{2,6},{3,7},{4,0},{5,1},{6,2},{7,3},{8,12},{9,13},{10,... | collective-permute-start | bytes 196616 | tf_op jit(solution)/shard_map/ppermute | solution.py:360
  23.4 5.2 %collective-permute-start.7 = (bf16[128,256]{1,0:T(8,128)(2,1)S(1)}, bf16[128,256]{1,0:T(8,128)(2,1)S(1)}, u32[]{:S(2)}, u32[]{:S(2)}) collective-permute-start(bf16[128,256]{1,0:T(8,128)(2,1)S(1)} %get-tuple-element.57.rest_3_), channel_id=1, source_target_pairs={{0,6},{1,7},{2,4},{3,5},{4,2},{5,3},{6,0},{7,1},{8,14},{9,15},{10,... | collective-permute-start | bytes 196616 | tf_op jit(solution)/shard_map/ppermute | solution.py:360
  24.8 3.7 %collective-permute-start.10 = (bf16[128,256]{1,0:T(8,128)(2,1)S(1)}, bf16[128,256]{1,0:T(8,128)(2,1)S(1)}, u32[]{:S(2)}, u32[]{:S(2)}) collective-permute-start(bf16[128,256]{1,0:T(8,128)(2,1)S(1)} %get-tuple-element.57.rest_3_), channel_id=1, source_target_pairs={{0,1},{1,0},{2,3},{3,2},{4,5},{5,4},{6,7},{7,6},{8,9},{9,8},{10,11... | collective-permute-start | bytes 196616 | tf_op jit(solution)/shard_map/ppermute | solution.py:360
  25.9 2.6 %collective-permute-start.11 = (bf16[128,256]{1,0:T(8,128)(2,1)S(1)}, bf16[128,256]{1,0:T(8,128)(2,1)S(1)}, u32[]{:S(2)}, u32[]{:S(2)}) collective-permute-start(bf16[128,256]{1,0:T(8,128)(2,1)S(1)} %collective-permute-done.9.rest_2_), channel_id=1, source_target_pairs={{0,1},{1,0},{2,3},{3,2},{4,5},{5,4},{6,7},{7,6},{8,9},{9,8},{10,11... | collective-permute-start | bytes 196616 | tf_op jit(solution)/shard_map/ppermute | solution.py:360
  26.5 2.1 %collective-permute-start.12 = (bf16[128,256]{1,0:T(8,128)(2,1)S(1)}, bf16[128,256]{1,0:T(8,128)(2,1)S(1)}, u32[]{:S(2)}, u32[]{:S(2)}) collective-permute-start(bf16[128,256]{1,0:T(8,128)(2,1)S(1)} %collective-permute-done.8.rest_1_), channel_id=1, source_target_pairs={{0,1},{1,0},{2,3},{3,2},{4,5},{5,4},{6,7},{7,6},{8,9},{9,8},{10,11... | collective-permute-start | bytes 196616 | tf_op jit(solution)/shard_map/ppermute | solution.py:360
  28.5 1.3 %collective-permute-start.13 = (bf16[128,256]{1,0:T(8,128)(2,1)S(1)}, bf16[128,256]{1,0:T(8,128)(2,1)S(1)}, u32[]{:S(2)}, u32[]{:S(2)}) collective-permute-start(bf16[128,256]{1,0:T(8,128)(2,1)S(1)} %collective-permute-done.7.rest_0_), channel_id=1, source_target_pairs={{0,1},{1,0},{2,3},{3,2},{4,5},{5,4},{6,7},{7,6},{8,9},{9,8},{10,11... | collective-permute-start | bytes 196616 | tf_op jit(solution)/shard_map/ppermute | solution.py:360
  31.3 10.5 %collective-permute-start.15 = (bf16[256,256]{1,0:T(8,128)(2,1)S(1)}, bf16[256,256]{1,0:T(8,128)(2,1)S(1)}, u32[]{:S(2)}, u32[]{:S(2)}) collective-permute-start(bf16[256,256]{1,0:T(8,128)(2,1)S(1)} %get-tuple-element.59), channel_id=1, source_target_pairs={{0,8},{24,16},{1,9},{25,17},{2,10},{26,18},{3,11},{27,19},{4,12},{... | collective-permute-start | bytes 393224 | tf_op jit(solution)/shard_map/ppermute | solution.py:335
  34.8 7.7 %collective-permute-start.20 = (bf16[256,256]{1,0:T(8,128)(2,1)S(1)}, bf16[256,256]{1,0:T(8,128)(2,1)S(1)}, u32[]{:S(2)}, u32[]{:S(2)}) collective-permute-start(bf16[256,256]{1,0:T(8,128)(2,1)S(1)} %get-tuple-element.62), channel_id=1, source_target_pairs={{0,8},{24,16},{1,9},{25,17},{2,10},{26,18},{3,11},{27,19},{4,12},{... | collective-permute-start | bytes 393224 | tf_op jit(solution)/shard_map/ppermute | solution.py:335
  37.6 15.0 %collective-permute-start.14 = (bf16[512,256]{1,0:T(8,128)(2,1)S(1)}, bf16[512,256]{1,0:T(8,128)(2,1)S(1)}, u32[]{:S(2)}, u32[]{:S(2)}) collective-permute-start(bf16[512,256]{1,0:T(8,128)(2,1)S(1)} %gradient.3), channel_id=1, source_target_pairs={{0,8},{24,16},{1,9},{25,17},{2,10},{26,18},{3,11},{27,19},{4,12},{... | collective-permute-start | bytes 786440 | tf_op jit(solution)/shard_map/ppermute | solution.py:335
  40.4 11.4 %collective-permute-start.19 = (bf16[512,256]{1,0:T(8,128)(2,1)S(1)}, bf16[512,256]{1,0:T(8,128)(2,1)S(1)}, u32[]{:S(2)}, u32[]{:S(2)}) collective-permute-start(bf16[512,256]{1,0:T(8,128)(2,1)S(1)} %gradient.5), channel_id=1, source_target_pairs={{0,8},{24,16},{1,9},{25,17},{2,10},{26,18},{3,11},{27,19},{4,12},{... | collective-permute-start | bytes 786440 | tf_op jit(solution)/shard_map/ppermute | solution.py:335
  41.8 1.4 %collective-permute-start.16 = (bf16[256,256]{1,0:T(8,128)(2,1)S(1)}, bf16[256,256]{1,0:T(8,128)(2,1)S(1)}, u32[]{:S(2)}, u32[]{:S(2)}) collective-permute-start(bf16[256,256]{1,0:T(8,128)(2,1)S(1)} %reduce-precision_convert_fusion.7), channel_id=1, source_target_pairs={{8,16},{16,8},{9,17},{17,9},{10,18},{18,10},{11,19},{19,11},{12,20... | collective-permute-start | bytes 393224 | tf_op jit(solution)/shard_map/ppermute | solution.py:342
  42.5 2.0 %collective-permute-start.21 = (bf16[256,256]{1,0:T(8,128)(2,1)S(1)}, bf16[256,256]{1,0:T(8,128)(2,1)S(1)}, u32[]{:S(2)}, u32[]{:S(2)}) collective-permute-start(bf16[256,256]{1,0:T(8,128)(2,1)S(1)} %reduce-precision_convert_fusion.5), channel_id=1, source_target_pairs={{8,16},{16,8},{9,17},{17,9},{10,18},{18,10},{11,19},{19,11},{12,20... | collective-permute-start | bytes 393224 | tf_op jit(solution)/shard_map/ppermute | solution.py:342
  43.3 16.4 %collective-permute-start.24 = (bf16[256,256]{1,0:T(8,128)(2,1)S(1)}, bf16[256,256]{1,0:T(8,128)(2,1)S(1)}, u32[]{:S(2)}, u32[]{:S(2)}) collective-permute-start(bf16[256,256]{1,0:T(8,128)(2,1)S(1)} %reduce-precision_convert_fusion.6.sent_ref), channel_id=1, source_target_pairs={{8,0},{16,24},{9,1},{17,25},{10,2},{18,26},{11,3},{19,27},{12,4},{... | collective-permute-start | bytes 393224 | tf_op jit(solution)/shard_map/ppermute | solution.py:351
  44.6 11.5 %collective-permute-start.25 = (bf16[256,256]{1,0:T(8,128)(2,1)S(1)}, bf16[256,256]{1,0:T(8,128)(2,1)S(1)}, u32[]{:S(2)}, u32[]{:S(2)}) collective-permute-start(bf16[256,256]{1,0:T(8,128)(2,1)S(1)} %reduce-precision_convert_fusion.4.sent_ref), channel_id=1, source_target_pairs={{8,0},{16,24},{9,1},{17,25},{10,2},{18,26},{11,3},{19,27},{12,4},{... | collective-permute-start | bytes 393224 | tf_op jit(solution)/shard_map/ppermute | solution.py:351
  52.0 4.9 %collective-permute-start.22 = (bf16[512,256]{1,0:T(8,128)(2,1)S(1)}, bf16[512,256]{1,0:T(8,128)(2,1)S(1)}, u32[]{:S(2)}, u32[]{:S(2)}) collective-permute-start(bf16[512,256]{1,0:T(8,128)(2,1)S(1)} %reduce-precision_convert_fusion.1), channel_id=1, source_target_pairs={{8,16},{16,8},{9,17},{17,9},{10,18},{18,10},{11,19},{19,11},{12,20... | collective-permute-start | bytes 786440 | tf_op jit(solution)/shard_map/ppermute | solution.py:342
  52.7 5.5 %collective-permute-start.17 = (bf16[512,256]{1,0:T(8,128)(2,1)S(1)}, bf16[512,256]{1,0:T(8,128)(2,1)S(1)}, u32[]{:S(2)}, u32[]{:S(2)}) collective-permute-start(bf16[512,256]{1,0:T(8,128)(2,1)S(1)} %reduce-precision_convert_fusion.3), channel_id=1, source_target_pairs={{8,16},{16,8},{9,17},{17,9},{10,18},{18,10},{11,19},{19,11},{12,20... | collective-permute-start | bytes 786440 | tf_op jit(solution)/shard_map/ppermute | solution.py:342
  57.0 15.4 %collective-permute-start.23 = (bf16[512,256]{1,0:T(8,128)(2,1)S(1)}, bf16[512,256]{1,0:T(8,128)(2,1)S(1)}, u32[]{:S(2)}, u32[]{:S(2)}) collective-permute-start(bf16[512,256]{1,0:T(8,128)(2,1)S(1)} %reduce-precision_convert_fusion.sent_ref), channel_id=1, source_target_pairs={{8,0},{16,24},{9,1},{17,25},{10,2},{18,26},{11,3},{19,27},{12,4},{... | collective-permute-start | bytes 786440 | tf_op jit(solution)/shard_map/ppermute | solution.py:351
  58.3 18.6 %collective-permute-start.18 = (bf16[512,256]{1,0:T(8,128)(2,1)S(1)}, bf16[512,256]{1,0:T(8,128)(2,1)S(1)}, u32[]{:S(2)}, u32[]{:S(2)}) collective-permute-start(bf16[512,256]{1,0:T(8,128)(2,1)S(1)} %reduce-precision_convert_fusion.2.sent_ref), channel_id=1, source_target_pairs={{8,0},{16,24},{9,1},{17,25},{10,2},{18,26},{11,3},{19,27},{12,4},{... | collective-permute-start | bytes 786440 | tf_op jit(solution)/shard_map/ppermute | solution.py:351

commit v4 on v2

--- a/solution.py
+++ b/solution.py
@@ -396,7 +396,9 @@
     for relation in range(proj_weight.shape[0]):
         parts = 2 if relation == 0 else 1
         made = gradient(parts, x_t, adj[relation], col[relation], slopes)
+        x_t, *made = lax.optimization_barrier((x_t, *made))
         chunks += [((relation, i), chunk) for i, chunk in enumerate(made)]
+    chunks = chunks[:2] + chunks[:1:-1]
     shape = (proj_weight.shape[0], features.shape[1], proj_weight.shape[2])
     return activations, chain_sum(chunks, n_dom, shape)
 

time: 78.1 us -> 77 us (0.986)
  waiting for transfers between devices: 32.9 us -> 31.8 us
    ppermute x4, waiting for transfers between devices: 18.4 us -> 16.5 us  [chain_sum(): got = lax.ppermute(sent, 'dom', [(low, low - 1), (high, high + 1)])]
    ppermute x4, waiting for transfers between devices: 5.99 us -> 6.77 us  [chain_sum(): got = lax.ppermute(sent, 'dom', perm)]
  transfers between devices with their start and end apart: 26 -> 26, of which waited for: 12 -> 14; matrix products, arithmetic and copies ran while one was open for 1% -> 1% of each run, Pallas kernels for 8% -> 8%
where the time goes in v4:
time: 77 us; the launch traced here: 76.5 us
  waiting for transfers between devices  31.8 us (41%)
  starting transfers between devices  24.5 us (32%)
  Pallas kernels  16.4 us (21%)
  local copies, waits for them, and re-layouts  2.39 us (3%)
  between operations  0.95 us (1%)
    ppermute x4, waiting for transfers between devices, chain_sum(): got = lax.ppermute(sent, 'dom', [(low, low - 1), (high, high + 1)])  16.5 us
    ppermute x14, starting transfers between devices, swap(): return lax.ppermute(value, 'feat', [(i, i ^ k) for i in range(n_feat)])  9.23 us
    ppermute x14, waiting for transfers between devices, swap(): return lax.ppermute(value, 'feat', [(i, i ^ k) for i in range(n_feat)])  8.53 us
    ppermute x4, starting transfers between devices, chain_sum(): got = lax.ppermute(sent, 'dom', perm)  7.4 us
    ppermute x4, waiting for transfers between devices, chain_sum(): got = lax.ppermute(sent, 'dom', perm)  6.77 us
    ppermute x4, starting transfers between devices, chain_sum(): got = lax.ppermute(sent, 'dom', [(low, low - 1), (high, high + 1)])  5.17 us
    pallas_call x3, Pallas kernels, gradient(): pl.pallas_call(functools.partial(gradient_kernel, len(slopes)), name='gra...  4.53 us
    pallas_call x1, Pallas kernels, adjacency(): pl.pallas_call(adjacency_kernel, name='adjacency', out_shape=[jax.ShapeDt...  4.11 us
  transfers between devices with their start and end apart: 26, of which 14 were waited for; matrix products, arithmetic and copies ran while one was open for 1% of the time, Pallas kernels for 8%

profile of v4, /device:TPU:0, one launch (start us, length us, event | category | flops | bytes accessed | tf_op | source)
XLA Modules:
  0.0 76.5 jit_solution(17163449979108337942)
XLA Ops:
  0.6 1.0 %copy-done.5 = s32[8,3,4,8,128]{4,3,2,1,0:T(8,128)S(1)} copy-done((s32[8,3,4,8,128]{4,3,2,1,0:T(8,128)S(1)}, s32[8,3,4,8,128]{4,3,2,1,0:T(8,128)}, u32[]{:S(2)}) %copy-start.5) | copy-done | bytes 393240
  1.6 0.7 copy-done.6
  2.3 0.7 copy-done.7
  3.0 4.1 %adjacency.1 = (f32[3,8,1024]{2,1,0:T(8,128)S(1)}, bf16[1024,1024]{1,0:T(8,128)(2,1)S(1)}, bf16[1024,1024]{1,0:T(8,128)(2,1)S(1)}, bf16[1024,1024]{1,0:T(8,128)(2,1)S(1)}) custom-call(s32[3,4,8]{2,1,0:T(4,128)S(1)} %bitcast.4, s32[3,8]{1,0:T(4,128)S(1)} %bitcast.5, s32[8,3,4,8,128]{4,3,2,1,0:T(8,128)S(1)} %copy-done.5), custom_call_target="tpu_custom_call" | custom-call | flops 3145728000 | bytes 6291456 | tf_op jit(solution)/shard_map/adjacency/pallas_call | solution.py:146
  7.2 3.0 %forward.1 = (f32[128,256]{1,0:T(8,128)S(1)}, bf16[128,256]{1,0:T(8,128)(2,1)S(1)}, f32[128,256]{1,0:T(8,128)S(1)}, bf16[128,256]{1,0:T(8,128)(2,1)S(1)}, f32[12...) custom-call(f32[3,8,1024]{2,1,0:T(8,128)S(1)} %get-tuple-element.30.inv_, ...), custom_call_target="tpu_custom_call" | custom-call | flops 2415919104 | bytes 6291456 | tf_op jit(solution)/shard_map/forward/pallas_call | solution.py:187
  10.2 0.5 collective-permute-start
  10.8 0.4 collective-permute-start.4
  11.3 0.3 collective-permute-done
  11.6 3.9 %collective-permute-start.1 = (bf16[128,256]{1,0:T(8,128)(2,1)S(1)}, bf16[128,256]{1,0:T(8,128)(2,1)S(1)}, u32[]{:S(2)}, u32[]{:S(2)}) collective-permute-start(bf16[128,256]{1,0:T(8,128)(2,1)S(1)} %add_convert_fusion.2), channel_id=1, source_target_pairs={{0,6},{1,7},{2,4},{3,5},{4,2},{5,3},{6,0},{7,1},{8,14},{9,15},{10,... | collective-permute-start | bytes 196616 | tf_op jit(solution)/shard_map/ppermute | solution.py:354
  15.5 0.6 collective-permute-start.3
  16.1 0.2 collective-permute-start.5
  16.3 1.6 %collective-permute-done.1.refs_0_ = bf16[128,256]{1,0:T(8,128)(2,1)S(1)} collective-permute-done((bf16[128,256]{1,0:T(8,128)(2,1)S(1)}, bf16[128,256]{1,0:T(8,128)(2,1)S(1)}, u32[]{:S(2)}, u32[]{:S(2)}) %collective-permute-start.1) | collective-permute-done | bytes 65568 | tf_op jit(solution)/shard_map/ppermute | solution.py:354
  17.9 1.9 %collective-permute-done.3.refs_1_ = bf16[128,256]{1,0:T(8,128)(2,1)S(1)} collective-permute-done((bf16[128,256]{1,0:T(8,128)(2,1)S(1)}, bf16[128,256]{1,0:T(8,128)(2,1)S(1)}, u32[]{:S(2)}, u32[]{:S(2)}) %collective-permute-start.3) | collective-permute-done | bytes 65568 | tf_op jit(solution)/shard_map/ppermute | solution.py:354
  19.8 0.6 collective-permute-done.5.refs_2_
  20.4 0.7 combine.1
  21.2 0.6 collective-permute-start.9
  21.8 1.4 %collective-permute-start.8 = (bf16[128,256]{1,0:T(8,128)(2,1)S(1)}, bf16[128,256]{1,0:T(8,128)(2,1)S(1)}, u32[]{:S(2)}, u32[]{:S(2)}) collective-permute-start(bf16[128,256]{1,0:T(8,128)(2,1)S(1)} %get-tuple-element.45.rest_3_), channel_id=1, source_target_pairs={{0,4},{1,5},{2,6},{3,7},{4,0},{5,1},{6,2},{7,3},{8,12},{9,13},{10,... | collective-permute-start | bytes 196616 | tf_op jit(solution)/shard_map/ppermute | solution.py:354
  23.2 1.4 %collective-permute-start.7 = (bf16[128,256]{1,0:T(8,128)(2,1)S(1)}, bf16[128,256]{1,0:T(8,128)(2,1)S(1)}, u32[]{:S(2)}, u32[]{:S(2)}) collective-permute-start(bf16[128,256]{1,0:T(8,128)(2,1)S(1)} %get-tuple-element.45.rest_3_), channel_id=1, source_target_pairs={{0,6},{1,7},{2,4},{3,5},{4,2},{5,3},{6,0},{7,1},{8,14},{9,15},{10,... | collective-permute-start | bytes 196616 | tf_op jit(solution)/shard_map/ppermute | solution.py:354
  24.7 1.1 %collective-permute-done.9.rest_2_ = bf16[128,256]{1,0:T(8,128)(2,1)S(1)} collective-permute-done((bf16[128,256]{1,0:T(8,128)(2,1)S(1)}, bf16[128,256]{1,0:T(8,128)(2,1)S(1)}, u32[]{:S(2)}, u32[]{:S(2)}) %collective-permute-start.9) | collective-permute-done | bytes 65568 | tf_op jit(solution)/shard_map/ppermute | solution.py:354
  25.8 0.6 collective-permute-done.8.rest_1_
  26.3 2.1 %collective-permute-done.7.rest_0_ = bf16[128,256]{1,0:T(8,128)(2,1)S(1)} collective-permute-done((bf16[128,256]{1,0:T(8,128)(2,1)S(1)}, bf16[128,256]{1,0:T(8,128)(2,1)S(1)}, u32[]{:S(2)}, u32[]{:S(2)}) %collective-permute-start.7) | collective-permute-done | bytes 65568 | tf_op jit(solution)/shard_map/ppermute | solution.py:354
  28.4 0.9 %transposed.1 = (bf16[512,1024]{1,0:T(8,128)(2,1)S(1)}, f32[1024,128]{1,0:T(8,128)S(1)}, f32[1024,128]{1,0:T(8,128)S(1)}, f32[1024,128]{1,0:T(8,128)S(1)}) custom-call(bf16[1024,512]{1,0:T(8,128)(2,1)S(1)} %copy-done, f32[3,8,1024]{2,1,0:T(8,128)S(1)} %get-tuple-element.30.inv_ref), custom_call_target="tpu_custom_call" | custom-call | flops 1048576 | bytes 3145728 | tf_op jit(solution)/shard_map/transposed/pallas_call | solution.py:219
  29.3 0.3 collective-permute-done.13.rest_7_
  29.6 1.5 %gradient.3 = (bf16[256,256]{1,0:T(8,128)(2,1)S(1)}, bf16[256,256]{1,0:T(8,128)(2,1)S(1)}) custom-call(bf16[512,1024]{1,0:T(8,128)(2,1)S(1)} %get-tuple-element.53.xt_ref, bf16[1024,1024]{1,0:T(8,128)(2,1)S(1)} %get-tuple-element.31.refs_0_.adj_ref, f32[1024,128]{1,0:T(8,128)S(1)} %get-tuple-element.44.col_ref, ...), custom_call_target="tpu_custom_call" | custom-call | flops 805306368 | bytes 2883584 | tf_op jit(solution)/shard_map/gradient/pallas_call | solution.py:276
  31.2 3.5 %collective-permute-start.15 = (bf16[256,256]{1,0:T(8,128)(2,1)S(1)}, bf16[256,256]{1,0:T(8,128)(2,1)S(1)}, u32[]{:S(2)}, u32[]{:S(2)}) collective-permute-start(bf16[256,256]{1,0:T(8,128)(2,1)S(1)} %get-tuple-element.51), channel_id=1, source_target_pairs={{0,8},{24,16},{1,9},{25,17},{2,10},{26,18},{3,11},{27,19},{4,12},{... | collective-permute-start | bytes 393224 | tf_op jit(solution)/shard_map/ppermute | solution.py:329
  34.6 1.5 %gradient.4 = bf16[512,256]{1,0:T(8,128)(2,1)S(1)} custom-call(bf16[512,1024]{1,0:T(8,128)(2,1)S(1)} %get-tuple-element.53.xt_ref, bf16[1024,1024]{1,0:T(8,128)(2,1)S(1)} %get-tuple-element.32.refs_1_.adj_ref, f32[1024,128]{1,0:T(8,128)S(1)} %get-tuple-element.49.col_ref, bf16[128,256]{1,0:T(8,128)(2,1)S(1)} %collective-permute-done.7.rest_0_, ...), custom_call_target="tpu_custom_call" | custom-call | flops 805306368 | bytes 2883584 | tf_op jit(solution)/shard_map/gradient/pallas_call | solution.py:276
  36.2 1.5 %gradient.5 = bf16[512,256]{1,0:T(8,128)(2,1)S(1)} custom-call(bf16[512,1024]{1,0:T(8,128)(2,1)S(1)} %get-tuple-element.53.xt_ref, bf16[1024,1024]{1,0:T(8,128)(2,1)S(1)} %get-tuple-element.33.refs_2_.adj_ref, f32[1024,128]{1,0:T(8,128)S(1)} %get-tuple-element.54.col_ref, bf16[128,256]{1,0:T(8,128)(2,1)S(1)} %collective-permute-done.7.rest_0_, ...), custom_call_target="tpu_custom_call" | custom-call | flops 805306368 | bytes 2883584 | tf_op jit(solution)/shard_map/gradient/pallas_call | solution.py:276
  37.7 1.3 %collective-permute-start.20 = (bf16[256,256]{1,0:T(8,128)(2,1)S(1)}, bf16[256,256]{1,0:T(8,128)(2,1)S(1)}, u32[]{:S(2)}, u32[]{:S(2)}) collective-permute-start(bf16[256,256]{1,0:T(8,128)(2,1)S(1)} %get-tuple-element.56), channel_id=1, source_target_pairs={{0,8},{24,16},{1,9},{25,17},{2,10},{26,18},{3,11},{27,19},{4,12},{... | collective-permute-start | bytes 393224 | tf_op jit(solution)/shard_map/ppermute | solution.py:329
  39.0 1.3 %collective-permute-start.19 = (bf16[512,256]{1,0:T(8,128)(2,1)S(1)}, bf16[512,256]{1,0:T(8,128)(2,1)S(1)}, u32[]{:S(2)}, u32[]{:S(2)}) collective-permute-start(bf16[512,256]{1,0:T(8,128)(2,1)S(1)} %gradient.5), channel_id=1, source_target_pairs={{0,8},{24,16},{1,9},{25,17},{2,10},{26,18},{3,11},{27,19},{4,12},{... | collective-permute-start | bytes 786440 | tf_op jit(solution)/shard_map/ppermute | solution.py:329
  40.3 1.3 %collective-permute-start.14 = (bf16[512,256]{1,0:T(8,128)(2,1)S(1)}, bf16[512,256]{1,0:T(8,128)(2,1)S(1)}, u32[]{:S(2)}, u32[]{:S(2)}) collective-permute-start(bf16[512,256]{1,0:T(8,128)(2,1)S(1)} %gradient.4), channel_id=1, source_target_pairs={{0,8},{24,16},{1,9},{25,17},{2,10},{26,18},{3,11},{27,19},{4,12},{... | collective-permute-start | bytes 786440 | tf_op jit(solution)/shard_map/ppermute | solution.py:329
  41.7 0.7 collective-permute-start.16
  42.4 0.5 collective-permute-done.20
  42.9 0.7 collective-permute-start.21
  43.6 1.3 %collective-permute-start.24 = (bf16[256,256]{1,0:T(8,128)(2,1)S(1)}, bf16[256,256]{1,0:T(8,128)(2,1)S(1)}, u32[]{:S(2)}, u32[]{:S(2)}) collective-permute-start(bf16[256,256]{1,0:T(8,128)(2,1)S(1)} %reduce-precision_convert_fusion.6.sent_ref), channel_id=1, source_target_pairs={{8,0},{16,24},{9,1},{17,25},{10,2},{18,26},{11,3},{19,27},{12,4},{... | collective-permute-start | bytes 393224 | tf_op jit(solution)/shard_map/ppermute | solution.py:345
  44.9 1.3 %collective-permute-start.25 = (bf16[256,256]{1,0:T(8,128)(2,1)S(1)}, bf16[256,256]{1,0:T(8,128)(2,1)S(1)}, u32[]{:S(2)}, u32[]{:S(2)}) collective-permute-start(bf16[256,256]{1,0:T(8,128)(2,1)S(1)} %reduce-precision_convert_fusion.4.sent_ref), channel_id=1, source_target_pairs={{8,0},{16,24},{9,1},{17,25},{10,2},{18,26},{11,3},{19,27},{12,4},{... | collective-permute-start | bytes 393224 | tf_op jit(solution)/shard_map/ppermute | solution.py:345
  46.2 2.2 %collective-permute-done.19 = bf16[512,256]{1,0:T(8,128)(2,1)S(1)} collective-permute-done((bf16[512,256]{1,0:T(8,128)(2,1)S(1)}, bf16[512,256]{1,0:T(8,128)(2,1)S(1)}, u32[]{:S(2)}, u32[]{:S(2)}) %collective-permute-start.19) | collective-permute-done | bytes 262176 | tf_op jit(solution)/shard_map/ppermute | solution.py:329
  48.5 0.7 collective-permute-start.22
  49.2 4.1 %collective-permute-done.14 = bf16[512,256]{1,0:T(8,128)(2,1)S(1)} collective-permute-done((bf16[512,256]{1,0:T(8,128)(2,1)S(1)}, bf16[512,256]{1,0:T(8,128)(2,1)S(1)}, u32[]{:S(2)}, u32[]{:S(2)}) %collective-permute-start.14) | collective-permute-done | bytes 262176 | tf_op jit(solution)/shard_map/ppermute | solution.py:329
  53.4 0.7 collective-permute-start.17
  54.1 2.4 %collective-permute-done.25.got_ref = bf16[256,256]{1,0:T(8,128)(2,1)S(1)} collective-permute-done((bf16[256,256]{1,0:T(8,128)(2,1)S(1)}, bf16[256,256]{1,0:T(8,128)(2,1)S(1)}, u32[]{:S(2)}, u32[]{:S(2)}) %collective-permute-start.25) | collective-permute-done | bytes 131104 | tf_op jit(solution)/shard_map/ppermute | solution.py:345
  56.5 0.7 finish.4.rest_0_
  57.3 1.3 %collective-permute-start.23 = (bf16[512,256]{1,0:T(8,128)(2,1)S(1)}, bf16[512,256]{1,0:T(8,128)(2,1)S(1)}, u32[]{:S(2)}, u32[]{:S(2)}) collective-permute-start(bf16[512,256]{1,0:T(8,128)(2,1)S(1)} %reduce-precision_convert_fusion.sent_ref), channel_id=1, source_target_pairs={{8,0},{16,24},{9,1},{17,25},{10,2},{18,26},{11,3},{19,27},{12,4},{... | collective-permute-start | bytes 786440 | tf_op jit(solution)/shard_map/ppermute | solution.py:345
  58.7 1.3 %collective-permute-start.18 = (bf16[512,256]{1,0:T(8,128)(2,1)S(1)}, bf16[512,256]{1,0:T(8,128)(2,1)S(1)}, u32[]{:S(2)}, u32[]{:S(2)}) collective-permute-start(bf16[512,256]{1,0:T(8,128)(2,1)S(1)} %reduce-precision_convert_fusion.2.sent_ref), channel_id=1, source_target_pairs={{8,0},{16,24},{9,1},{17,25},{10,2},{18,26},{11,3},{19,27},{12,4},{... | collective-permute-start | bytes 786440 | tf_op jit(solution)/shard_map/ppermute | solution.py:345
  60.0 0.7 finish.5.rest_0_
  60.7 11.8 %collective-permute-done.23.got_ref = bf16[512,256]{1,0:T(8,128)(2,1)S(1)} collective-permute-done((bf16[512,256]{1,0:T(8,128)(2,1)S(1)}, bf16[512,256]{1,0:T(8,128)(2,1)S(1)}, u32[]{:S(2)}, u32[]{:S(2)}) %collective-permute-start.23) | collective-permute-done | bytes 262176 | tf_op jit(solution)/shard_map/ppermute | solution.py:345
  72.5 0.9 %finish.6.rest_0_ = f32[3,512,256]{2,1,0:T(8,128)} custom-call(bf16[512,256]{1,0:T(8,128)(2,1)S(1)} %collective-permute-done.23.got_ref, bf16[512,256]{1,0:T(8,128)(2,1)S(1)} %reduce-precision_convert_fusion.sent_ref, f32[3,512,256]{2,1,0:T(8,128)} %finish.5.rest_0_), custom_call_target="tpu_custom_call", output_to_operand_aliasing={{}: (2, {})} | custom-call | flops 2000000000 | bytes 1048576 | tf_op jit(solution)/shard_map/finish/pallas_call | solution.py:303
  73.4 2.3 %collective-permute-done.18.got_ref = bf16[512,256]{1,0:T(8,128)(2,1)S(1)} collective-permute-done((bf16[512,256]{1,0:T(8,128)(2,1)S(1)}, bf16[512,256]{1,0:T(8,128)(2,1)S(1)}, u32[]{:S(2)}, u32[]{:S(2)}) %collective-permute-start.18) | collective-permute-done | bytes 262176 | tf_op jit(solution)/shard_map/ppermute | solution.py:345
  75.7 0.9 %finish.7 = f32[3,512,256]{2,1,0:T(8,128)} custom-call(bf16[512,256]{1,0:T(8,128)(2,1)S(1)} %collective-permute-done.18.got_ref, bf16[512,256]{1,0:T(8,128)(2,1)S(1)} %reduce-precision_convert_fusion.2.sent_ref, f32[3,512,256]{2,1,0:T(8,128)} %finish.6.rest_0_), custom_call_target="tpu_custom_call", output_to_operand_aliasing={{}: (2, {})} | custom-call | flops 2000000000 | bytes 1048576 | tf_op jit(solution)/shard_map/finish/pallas_call | solution.py:303
  (42 shorter events, 0.7 us)
Async XLA Ops:
  0.6 1.0 %copy-start.5 = (s32[8,3,4,8,128]{4,3,2,1,0:T(8,128)S(1)}, s32[8,3,4,8,128]{4,3,2,1,0:T(8,128)}, u32[]{:S(2)}) copy-start(s32[8,3,4,8,128]{4,3,2,1,0:T(8,128)} %pat_ref.1) | copy-start | bytes 1179652
  1.6 0.7 copy-start.6
  2.3 0.7 copy-start.7
  3.0 4.1 %copy-start = (bf16[1024,512]{1,0:T(8,128)(2,1)S(1)}, bf16[1024,512]{1,0:T(8,128)(2,1)}, u32[]{:S(2)}) copy-start(bf16[1024,512]{1,0:T(8,128)(2,1)} %x_ref.1) | copy-start | bytes 3145732
  3.0 4.1 %copy-start.4 = (bf16[3,512,256]{2,1,0:T(8,128)(2,1)S(1)}, bf16[3,512,256]{2,1,0:T(8,128)(2,1)}, u32[]{:S(2)}) copy-start(bf16[3,512,256]{2,1,0:T(8,128)(2,1)} %refs_4_.1) | copy-start | bytes 2359300
  7.1 13.3 %copy-start.1 = (bf16[128,256]{1,0:T(8,128)(2,1)S(1)}, bf16[128,256]{1,0:T(8,128)(2,1)}, u32[]{:S(2)}) copy-start(bf16[128,256]{1,0:T(8,128)(2,1)} %refs_7_.1) | copy-start | bytes 196612
  7.2 13.2 %copy-start.2 = (f32[3,256]{1,0:T(4,128)S(1)}, f32[3,256]{1,0:T(4,128)}, u32[]{:S(2)}) copy-start(f32[3,256]{1,0:T(4,128)} %refs_6_.1) | copy-start | bytes 9220
  7.2 13.2 %copy-start.3 = (s32[128]{0:T(128)S(1)}, s32[128]{0:T(128)}, u32[]{:S(2)}) copy-start(s32[128]{0:T(128)} %param.13) | copy-start | bytes 1540
  10.2 1.4 %collective-permute-start = (bf16[128,256]{1,0:T(8,128)(2,1)S(1)}, bf16[128,256]{1,0:T(8,128)(2,1)S(1)}, u32[]{:S(2)}, u32[]{:S(2)}) collective-permute-start(bf16[128,256]{1,0:T(8,128)(2,1)S(1)} %get-tuple-element.35), channel_id=1, source_target_pairs={{0,1},{1,0},{2,3},{3,2},{4,5},{5,4},{6,7},{7,6},{8,9},{9,8},{10,11... | collective-permute-start | bytes 196616 | tf_op jit(solution)/shard_map/ppermute | solution.py:354
  10.7 4.8 %collective-permute-start.2 = (bf16[128,256]{1,0:T(8,128)(2,1)S(1)}, bf16[128,256]{1,0:T(8,128)(2,1)S(1)}, u32[]{:S(2)}, u32[]{:S(2)}) collective-permute-start(bf16[128,256]{1,0:T(8,128)(2,1)S(1)} %get-tuple-element.37), channel_id=1, source_target_pairs={{0,1},{1,0},{2,3},{3,2},{4,5},{5,4},{6,7},{7,6},{8,9},{9,8},{10,11... | collective-permute-start | bytes 196616 | tf_op jit(solution)/shard_map/ppermute | solution.py:354
  10.8 5.3 %collective-permute-start.4 = (bf16[128,256]{1,0:T(8,128)(2,1)S(1)}, bf16[128,256]{1,0:T(8,128)(2,1)S(1)}, u32[]{:S(2)}, u32[]{:S(2)}) collective-permute-start(bf16[128,256]{1,0:T(8,128)(2,1)S(1)} %get-tuple-element.39), channel_id=1, source_target_pairs={{0,1},{1,0},{2,3},{3,2},{4,5},{5,4},{6,7},{7,6},{8,9},{9,8},{10,11... | collective-permute-start | bytes 196616 | tf_op jit(solution)/shard_map/ppermute | solution.py:354
  11.2 5.1 %collective-permute-start.6 = (bf16[128,256]{1,0:T(8,128)(2,1)S(1)}, bf16[128,256]{1,0:T(8,128)(2,1)S(1)}, u32[]{:S(2)}, u32[]{:S(2)}) collective-permute-start(bf16[128,256]{1,0:T(8,128)(2,1)S(1)} %get-tuple-element.40), channel_id=1, source_target_pairs={{0,1},{1,0},{2,3},{3,2},{4,5},{5,4},{6,7},{7,6},{8,9},{9,8},{10,11... | collective-permute-start | bytes 196616 | tf_op jit(solution)/shard_map/ppermute | solution.py:354
  11.6 6.3 %collective-permute-start.1 = (bf16[128,256]{1,0:T(8,128)(2,1)S(1)}, bf16[128,256]{1,0:T(8,128)(2,1)S(1)}, u32[]{:S(2)}, u32[]{:S(2)}) collective-permute-start(bf16[128,256]{1,0:T(8,128)(2,1)S(1)} %add_convert_fusion.2), channel_id=1, source_target_pairs={{0,6},{1,7},{2,4},{3,5},{4,2},{5,3},{6,0},{7,1},{8,14},{9,15},{10,... | collective-permute-start | bytes 196616 | tf_op jit(solution)/shard_map/ppermute | solution.py:354
  15.5 4.3 %collective-permute-start.3 = (bf16[128,256]{1,0:T(8,128)(2,1)S(1)}, bf16[128,256]{1,0:T(8,128)(2,1)S(1)}, u32[]{:S(2)}, u32[]{:S(2)}) collective-permute-start(bf16[128,256]{1,0:T(8,128)(2,1)S(1)} %add_convert_fusion.1), channel_id=1, source_target_pairs={{0,4},{1,5},{2,6},{3,7},{4,0},{5,1},{6,2},{7,3},{8,12},{9,13},{10,... | collective-permute-start | bytes 196616 | tf_op jit(solution)/shard_map/ppermute | solution.py:354
  16.1 4.3 %collective-permute-start.5 = (bf16[128,256]{1,0:T(8,128)(2,1)S(1)}, bf16[128,256]{1,0:T(8,128)(2,1)S(1)}, u32[]{:S(2)}, u32[]{:S(2)}) collective-permute-start(bf16[128,256]{1,0:T(8,128)(2,1)S(1)} %add_convert_fusion), channel_id=1, source_target_pairs={{0,2},{1,3},{2,0},{3,1},{4,6},{5,7},{6,4},{7,5},{8,10},{9,11},{10,... | collective-permute-start | bytes 196616 | tf_op jit(solution)/shard_map/ppermute | solution.py:354
  21.2 4.6 %collective-permute-start.9 = (bf16[128,256]{1,0:T(8,128)(2,1)S(1)}, bf16[128,256]{1,0:T(8,128)(2,1)S(1)}, u32[]{:S(2)}, u32[]{:S(2)}) collective-permute-start(bf16[128,256]{1,0:T(8,128)(2,1)S(1)} %get-tuple-element.45.rest_3_), channel_id=1, source_target_pairs={{0,2},{1,3},{2,0},{3,1},{4,6},{5,7},{6,4},{7,5},{8,10},{9,11},{10,... | collective-permute-start | bytes 196616 | tf_op jit(solution)/shard_map/ppermute | solution.py:354
  21.8 4.5 %collective-permute-start.8 = (bf16[128,256]{1,0:T(8,128)(2,1)S(1)}, bf16[128,256]{1,0:T(8,128)(2,1)S(1)}, u32[]{:S(2)}, u32[]{:S(2)}) collective-permute-start(bf16[128,256]{1,0:T(8,128)(2,1)S(1)} %get-tuple-element.45.rest_3_), channel_id=1, source_target_pairs={{0,4},{1,5},{2,6},{3,7},{4,0},{5,1},{6,2},{7,3},{8,12},{9,13},{10,... | collective-permute-start | bytes 196616 | tf_op jit(solution)/shard_map/ppermute | solution.py:354
  23.2 5.2 %collective-permute-start.7 = (bf16[128,256]{1,0:T(8,128)(2,1)S(1)}, bf16[128,256]{1,0:T(8,128)(2,1)S(1)}, u32[]{:S(2)}, u32[]{:S(2)}) collective-permute-start(bf16[128,256]{1,0:T(8,128)(2,1)S(1)} %get-tuple-element.45.rest_3_), channel_id=1, source_target_pairs={{0,6},{1,7},{2,4},{3,5},{4,2},{5,3},{6,0},{7,1},{8,14},{9,15},{10,... | collective-permute-start | bytes 196616 | tf_op jit(solution)/shard_map/ppermute | solution.py:354
  24.6 4.6 %collective-permute-start.10 = (bf16[128,256]{1,0:T(8,128)(2,1)S(1)}, bf16[128,256]{1,0:T(8,128)(2,1)S(1)}, u32[]{:S(2)}, u32[]{:S(2)}) collective-permute-start(bf16[128,256]{1,0:T(8,128)(2,1)S(1)} %get-tuple-element.45.rest_3_), channel_id=1, source_target_pairs={{0,1},{1,0},{2,3},{3,2},{4,5},{5,4},{6,7},{7,6},{8,9},{9,8},{10,11... | collective-permute-start | bytes 196616 | tf_op jit(solution)/shard_map/ppermute | solution.py:354
  25.8 3.5 %collective-permute-start.11 = (bf16[128,256]{1,0:T(8,128)(2,1)S(1)}, bf16[128,256]{1,0:T(8,128)(2,1)S(1)}, u32[]{:S(2)}, u32[]{:S(2)}) collective-permute-start(bf16[128,256]{1,0:T(8,128)(2,1)S(1)} %collective-permute-done.9.rest_2_), channel_id=1, source_target_pairs={{0,1},{1,0},{2,3},{3,2},{4,5},{5,4},{6,7},{7,6},{8,9},{9,8},{10,11... | collective-permute-start | bytes 196616 | tf_op jit(solution)/shard_map/ppermute | solution.py:354
  26.3 3.0 %collective-permute-start.12 = (bf16[128,256]{1,0:T(8,128)(2,1)S(1)}, bf16[128,256]{1,0:T(8,128)(2,1)S(1)}, u32[]{:S(2)}, u32[]{:S(2)}) collective-permute-start(bf16[128,256]{1,0:T(8,128)(2,1)S(1)} %collective-permute-done.8.rest_1_), channel_id=1, source_target_pairs={{0,1},{1,0},{2,3},{3,2},{4,5},{5,4},{6,7},{7,6},{8,9},{9,8},{10,11... | collective-permute-start | bytes 196616 | tf_op jit(solution)/shard_map/ppermute | solution.py:354
  28.4 1.3 %collective-permute-start.13 = (bf16[128,256]{1,0:T(8,128)(2,1)S(1)}, bf16[128,256]{1,0:T(8,128)(2,1)S(1)}, u32[]{:S(2)}, u32[]{:S(2)}) collective-permute-start(bf16[128,256]{1,0:T(8,128)(2,1)S(1)} %collective-permute-done.7.rest_0_), channel_id=1, source_target_pairs={{0,1},{1,0},{2,3},{3,2},{4,5},{5,4},{6,7},{7,6},{8,9},{9,8},{10,11... | collective-permute-start | bytes 196616 | tf_op jit(solution)/shard_map/ppermute | solution.py:354
  31.2 10.5 %collective-permute-start.15 = (bf16[256,256]{1,0:T(8,128)(2,1)S(1)}, bf16[256,256]{1,0:T(8,128)(2,1)S(1)}, u32[]{:S(2)}, u32[]{:S(2)}) collective-permute-start(bf16[256,256]{1,0:T(8,128)(2,1)S(1)} %get-tuple-element.51), channel_id=1, source_target_pairs={{0,8},{24,16},{1,9},{25,17},{2,10},{26,18},{3,11},{27,19},{4,12},{... | collective-permute-start | bytes 393224 | tf_op jit(solution)/shard_map/ppermute | solution.py:329
  37.7 5.1 %collective-permute-start.20 = (bf16[256,256]{1,0:T(8,128)(2,1)S(1)}, bf16[256,256]{1,0:T(8,128)(2,1)S(1)}, u32[]{:S(2)}, u32[]{:S(2)}) collective-permute-start(bf16[256,256]{1,0:T(8,128)(2,1)S(1)} %get-tuple-element.56), channel_id=1, source_target_pairs={{0,8},{24,16},{1,9},{25,17},{2,10},{26,18},{3,11},{27,19},{4,12},{... | collective-permute-start | bytes 393224 | tf_op jit(solution)/shard_map/ppermute | solution.py:329
  39.0 9.4 %collective-permute-start.19 = (bf16[512,256]{1,0:T(8,128)(2,1)S(1)}, bf16[512,256]{1,0:T(8,128)(2,1)S(1)}, u32[]{:S(2)}, u32[]{:S(2)}) collective-permute-start(bf16[512,256]{1,0:T(8,128)(2,1)S(1)} %gradient.5), channel_id=1, source_target_pairs={{0,8},{24,16},{1,9},{25,17},{2,10},{26,18},{3,11},{27,19},{4,12},{... | collective-permute-start | bytes 786440 | tf_op jit(solution)/shard_map/ppermute | solution.py:329
  40.3 13.0 %collective-permute-start.14 = (bf16[512,256]{1,0:T(8,128)(2,1)S(1)}, bf16[512,256]{1,0:T(8,128)(2,1)S(1)}, u32[]{:S(2)}, u32[]{:S(2)}) collective-permute-start(bf16[512,256]{1,0:T(8,128)(2,1)S(1)} %gradient.4), channel_id=1, source_target_pairs={{0,8},{24,16},{1,9},{25,17},{2,10},{26,18},{3,11},{27,19},{4,12},{... | collective-permute-start | bytes 786440 | tf_op jit(solution)/shard_map/ppermute | solution.py:329
  41.7 1.9 %collective-permute-start.16 = (bf16[256,256]{1,0:T(8,128)(2,1)S(1)}, bf16[256,256]{1,0:T(8,128)(2,1)S(1)}, u32[]{:S(2)}, u32[]{:S(2)}) collective-permute-start(bf16[256,256]{1,0:T(8,128)(2,1)S(1)} %reduce-precision_convert_fusion.7), channel_id=1, source_target_pairs={{8,16},{16,8},{9,17},{17,9},{10,18},{18,10},{11,19},{19,11},{12,20... | collective-permute-start | bytes 393224 | tf_op jit(solution)/shard_map/ppermute | solution.py:336
  42.9 2.0 %collective-permute-start.21 = (bf16[256,256]{1,0:T(8,128)(2,1)S(1)}, bf16[256,256]{1,0:T(8,128)(2,1)S(1)}, u32[]{:S(2)}, u32[]{:S(2)}) collective-permute-start(bf16[256,256]{1,0:T(8,128)(2,1)S(1)} %reduce-precision_convert_fusion.5), channel_id=1, source_target_pairs={{8,16},{16,8},{9,17},{17,9},{10,18},{18,10},{11,19},{19,11},{12,20... | collective-permute-start | bytes 393224 | tf_op jit(solution)/shard_map/ppermute | solution.py:336
  43.6 16.4 %collective-permute-start.24 = (bf16[256,256]{1,0:T(8,128)(2,1)S(1)}, bf16[256,256]{1,0:T(8,128)(2,1)S(1)}, u32[]{:S(2)}, u32[]{:S(2)}) collective-permute-start(bf16[256,256]{1,0:T(8,128)(2,1)S(1)} %reduce-precision_convert_fusion.6.sent_ref), channel_id=1, source_target_pairs={{8,0},{16,24},{9,1},{17,25},{10,2},{18,26},{11,3},{19,27},{12,4},{... | collective-permute-start | bytes 393224 | tf_op jit(solution)/shard_map/ppermute | solution.py:345
  44.9 11.5 %collective-permute-start.25 = (bf16[256,256]{1,0:T(8,128)(2,1)S(1)}, bf16[256,256]{1,0:T(8,128)(2,1)S(1)}, u32[]{:S(2)}, u32[]{:S(2)}) collective-permute-start(bf16[256,256]{1,0:T(8,128)(2,1)S(1)} %reduce-precision_convert_fusion.4.sent_ref), channel_id=1, source_target_pairs={{8,0},{16,24},{9,1},{17,25},{10,2},{18,26},{11,3},{19,27},{12,4},{... | collective-permute-start | bytes 393224 | tf_op jit(solution)/shard_map/ppermute | solution.py:345
  48.5 8.7 %collective-permute-start.22 = (bf16[512,256]{1,0:T(8,128)(2,1)S(1)}, bf16[512,256]{1,0:T(8,128)(2,1)S(1)}, u32[]{:S(2)}, u32[]{:S(2)}) collective-permute-start(bf16[512,256]{1,0:T(8,128)(2,1)S(1)} %reduce-precision_convert_fusion.1), channel_id=1, source_target_pairs={{8,16},{16,8},{9,17},{17,9},{10,18},{18,10},{11,19},{19,11},{12,20... | collective-permute-start | bytes 786440 | tf_op jit(solution)/shard_map/ppermute | solution.py:336
  53.4 5.2 %collective-permute-start.17 = (bf16[512,256]{1,0:T(8,128)(2,1)S(1)}, bf16[512,256]{1,0:T(8,128)(2,1)S(1)}, u32[]{:S(2)}, u32[]{:S(2)}) collective-permute-start(bf16[512,256]{1,0:T(8,128)(2,1)S(1)} %reduce-precision_convert_fusion.3), channel_id=1, source_target_pairs={{8,16},{16,8},{9,17},{17,9},{10,18},{18,10},{11,19},{19,11},{12,20... | collective-permute-start | bytes 786440 | tf_op jit(solution)/shard_map/ppermute | solution.py:336
  57.3 15.3 %collective-permute-start.23 = (bf16[512,256]{1,0:T(8,128)(2,1)S(1)}, bf16[512,256]{1,0:T(8,128)(2,1)S(1)}, u32[]{:S(2)}, u32[]{:S(2)}) collective-permute-start(bf16[512,256]{1,0:T(8,128)(2,1)S(1)} %reduce-precision_convert_fusion.sent_ref), channel_id=1, source_target_pairs={{8,0},{16,24},{9,1},{17,25},{10,2},{18,26},{11,3},{19,27},{12,4},{... | collective-permute-start | bytes 786440 | tf_op jit(solution)/shard_map/ppermute | solution.py:345
  58.7 17.0 %collective-permute-start.18 = (bf16[512,256]{1,0:T(8,128)(2,1)S(1)}, bf16[512,256]{1,0:T(8,128)(2,1)S(1)}, u32[]{:S(2)}, u32[]{:S(2)}) collective-permute-start(bf16[512,256]{1,0:T(8,128)(2,1)S(1)} %reduce-precision_convert_fusion.2.sent_ref), channel_id=1, source_target_pairs={{8,0},{16,24},{9,1},{17,25},{10,2},{18,26},{11,3},{19,27},{12,4},{... | collective-permute-start | bytes 786440 | tf_op jit(solution)/shard_map/ppermute | solution.py:345

commit v5 on v4

--- a/solution.py
+++ b/solution.py
@@ -331,9 +331,11 @@
         inner.append(sent)
     middle = []
     for i, sent in enumerate(inner):
-        if i >= 2:
+        if i == 3:
             sent, _ = lax.optimization_barrier((sent, middle[i - 2]))
         got = lax.ppermute(sent, "dom", [(half - 1, half), (half, half - 1)])
+        if i == 1 and len(inner) > 2:
+            got, _ = lax.optimization_barrier((got, inner[2]))
         middle.append(rounded(sent.astype(F32) + got.astype(F32)).astype(BF16))
     out = None
     for i, sent in enumerate(middle):

time: 77 us -> 73.9 us (0.960)
  waiting for transfers between devices: 31.8 us -> 28.8 us
    ppermute x4, waiting for transfers between devices: 16.5 us -> 13.4 us  [chain_sum(): got = lax.ppermute(sent, 'dom', [(low, low - 1), (high, high + 1)])]
where the time goes in v5:
time: 73.9 us; the launch traced here: 73.5 us
  waiting for transfers between devices  28.8 us (39%)
  starting transfers between devices  24.5 us (33%)
  Pallas kernels  16.4 us (22%)
  local copies, waits for them, and re-layouts  2.39 us (3%)
  between operations  0.95 us (1%)
    ppermute x4, waiting for transfers between devices, chain_sum(): got = lax.ppermute(sent, 'dom', [(low, low - 1), (high, high + 1)])  13.4 us
    ppermute x14, starting transfers between devices, swap(): return lax.ppermute(value, 'feat', [(i, i ^ k) for i in range(n_feat)])  9.23 us
    ppermute x14, waiting for transfers between devices, swap(): return lax.ppermute(value, 'feat', [(i, i ^ k) for i in range(n_feat)])  8.53 us
    ppermute x4, starting transfers between devices, chain_sum(): got = lax.ppermute(sent, 'dom', perm)  7.4 us
    ppermute x4, waiting for transfers between devices, chain_sum(): got = lax.ppermute(sent, 'dom', perm)  6.77 us
    ppermute x4, starting transfers between devices, chain_sum(): got = lax.ppermute(sent, 'dom', [(low, low - 1), (high, high + 1)])  5.17 us
    pallas_call x3, Pallas kernels, gradient(): pl.pallas_call(functools.partial(gradient_kernel, len(slopes)), name='gra...  4.53 us
    pallas_call x1, Pallas kernels, adjacency(): pl.pallas_call(adjacency_kernel, name='adjacency', out_shape=[jax.ShapeDt...  4.11 us
  transfers between devices with their start and end apart: 26, of which 14 were waited for; matrix products, arithmetic and copies ran while one was open for 1% of the time, Pallas kernels for 8%

profile of v5, /device:TPU:0, one launch (start us, length us, event | category | flops | bytes accessed | tf_op | source)
XLA Modules:
  0.0 73.5 jit_solution(1362453016815085286)
XLA Ops:
  0.6 1.0 %copy-done.5 = s32[8,3,4,8,128]{4,3,2,1,0:T(8,128)S(1)} copy-done((s32[8,3,4,8,128]{4,3,2,1,0:T(8,128)S(1)}, s32[8,3,4,8,128]{4,3,2,1,0:T(8,128)}, u32[]{:S(2)}) %copy-start.5) | copy-done | bytes 393240
  1.6 0.7 copy-done.6
  2.3 0.7 copy-done.7
  3.0 4.1 %adjacency.1 = (f32[3,8,1024]{2,1,0:T(8,128)S(1)}, bf16[1024,1024]{1,0:T(8,128)(2,1)S(1)}, bf16[1024,1024]{1,0:T(8,128)(2,1)S(1)}, bf16[1024,1024]{1,0:T(8,128)(2,1)S(1)}) custom-call(s32[3,4,8]{2,1,0:T(4,128)S(1)} %bitcast.4, s32[3,8]{1,0:T(4,128)S(1)} %bitcast.5, s32[8,3,4,8,128]{4,3,2,1,0:T(8,128)S(1)} %copy-done.5), custom_call_target="tpu_custom_call" | custom-call | flops 3145728000 | bytes 6291456 | tf_op jit(solution)/shard_map/adjacency/pallas_call | solution.py:146
  7.2 3.0 %forward.1 = (f32[128,256]{1,0:T(8,128)S(1)}, bf16[128,256]{1,0:T(8,128)(2,1)S(1)}, f32[128,256]{1,0:T(8,128)S(1)}, bf16[128,256]{1,0:T(8,128)(2,1)S(1)}, f32[12...) custom-call(f32[3,8,1024]{2,1,0:T(8,128)S(1)} %get-tuple-element.30.inv_, ...), custom_call_target="tpu_custom_call" | custom-call | flops 2415919104 | bytes 6291456 | tf_op jit(solution)/shard_map/forward/pallas_call | solution.py:187
  10.2 0.5 collective-permute-start
  10.8 0.4 collective-permute-start.4
  11.3 0.3 collective-permute-done
  11.6 3.9 %collective-permute-start.1 = (bf16[128,256]{1,0:T(8,128)(2,1)S(1)}, bf16[128,256]{1,0:T(8,128)(2,1)S(1)}, u32[]{:S(2)}, u32[]{:S(2)}) collective-permute-start(bf16[128,256]{1,0:T(8,128)(2,1)S(1)} %add_convert_fusion.2), channel_id=1, source_target_pairs={{0,6},{1,7},{2,4},{3,5},{4,2},{5,3},{6,0},{7,1},{8,14},{9,15},{10,... | collective-permute-start | bytes 196616 | tf_op jit(solution)/shard_map/ppermute | solution.py:356
  15.5 0.6 collective-permute-start.3
  16.1 0.2 collective-permute-start.5
  16.3 1.6 %collective-permute-done.1.refs_0_ = bf16[128,256]{1,0:T(8,128)(2,1)S(1)} collective-permute-done((bf16[128,256]{1,0:T(8,128)(2,1)S(1)}, bf16[128,256]{1,0:T(8,128)(2,1)S(1)}, u32[]{:S(2)}, u32[]{:S(2)}) %collective-permute-start.1) | collective-permute-done | bytes 65568 | tf_op jit(solution)/shard_map/ppermute | solution.py:356
  17.9 1.9 %collective-permute-done.3.refs_1_ = bf16[128,256]{1,0:T(8,128)(2,1)S(1)} collective-permute-done((bf16[128,256]{1,0:T(8,128)(2,1)S(1)}, bf16[128,256]{1,0:T(8,128)(2,1)S(1)}, u32[]{:S(2)}, u32[]{:S(2)}) %collective-permute-start.3) | collective-permute-done | bytes 65568 | tf_op jit(solution)/shard_map/ppermute | solution.py:356
  19.8 0.6 collective-permute-done.5.refs_2_
  20.4 0.7 %combine.1 = (bf16[128,256]{1,0:T(8,128)(2,1)}, bf16[128,256]{1,0:T(8,128)(2,1)S(1)}) custom-call(bf16[128,256]{1,0:T(8,128)(2,1)S(1)} %collective-permute-done.1.refs_0_, bf16[128,256]{1,0:T(8,128)(2,1)S(1)} %collective-permute-done.3.refs_1_, bf16[128,256]{1,0:T(8,128)(2,1)S(1)} %collective-permute-done.5.refs_2_, ...), custom_call_target="tpu_custom_call" | custom-call | tf_op jit(solution)/shard_map/combine/pallas_call | solution.py:250
  21.2 0.6 collective-permute-start.9
  21.8 1.4 %collective-permute-start.8 = (bf16[128,256]{1,0:T(8,128)(2,1)S(1)}, bf16[128,256]{1,0:T(8,128)(2,1)S(1)}, u32[]{:S(2)}, u32[]{:S(2)}) collective-permute-start(bf16[128,256]{1,0:T(8,128)(2,1)S(1)} %get-tuple-element.45.rest_3_), channel_id=1, source_target_pairs={{0,4},{1,5},{2,6},{3,7},{4,0},{5,1},{6,2},{7,3},{8,12},{9,13},{10,... | collective-permute-start | bytes 196616 | tf_op jit(solution)/shard_map/ppermute | solution.py:356
  23.2 1.4 %collective-permute-start.7 = (bf16[128,256]{1,0:T(8,128)(2,1)S(1)}, bf16[128,256]{1,0:T(8,128)(2,1)S(1)}, u32[]{:S(2)}, u32[]{:S(2)}) collective-permute-start(bf16[128,256]{1,0:T(8,128)(2,1)S(1)} %get-tuple-element.45.rest_3_), channel_id=1, source_target_pairs={{0,6},{1,7},{2,4},{3,5},{4,2},{5,3},{6,0},{7,1},{8,14},{9,15},{10,... | collective-permute-start | bytes 196616 | tf_op jit(solution)/shard_map/ppermute | solution.py:356
  24.7 1.1 %collective-permute-done.9.rest_2_ = bf16[128,256]{1,0:T(8,128)(2,1)S(1)} collective-permute-done((bf16[128,256]{1,0:T(8,128)(2,1)S(1)}, bf16[128,256]{1,0:T(8,128)(2,1)S(1)}, u32[]{:S(2)}, u32[]{:S(2)}) %collective-permute-start.9) | collective-permute-done | bytes 65568 | tf_op jit(solution)/shard_map/ppermute | solution.py:356
  25.8 0.6 collective-permute-done.8.rest_1_
  26.3 2.1 %collective-permute-done.7.rest_0_ = bf16[128,256]{1,0:T(8,128)(2,1)S(1)} collective-permute-done((bf16[128,256]{1,0:T(8,128)(2,1)S(1)}, bf16[128,256]{1,0:T(8,128)(2,1)S(1)}, u32[]{:S(2)}, u32[]{:S(2)}) %collective-permute-start.7) | collective-permute-done | bytes 65568 | tf_op jit(solution)/shard_map/ppermute | solution.py:356
  28.4 0.9 %transposed.1 = (bf16[512,1024]{1,0:T(8,128)(2,1)S(1)}, f32[1024,128]{1,0:T(8,128)S(1)}, f32[1024,128]{1,0:T(8,128)S(1)}, f32[1024,128]{1,0:T(8,128)S(1)}) custom-call(bf16[1024,512]{1,0:T(8,128)(2,1)S(1)} %copy-done, f32[3,8,1024]{2,1,0:T(8,128)S(1)} %get-tuple-element.30.inv_ref), custom_call_target="tpu_custom_call" | custom-call | flops 1048576 | bytes 3145728 | tf_op jit(solution)/shard_map/transposed/pallas_call | solution.py:219
  29.3 0.3 collective-permute-done.13.rest_7_
  29.6 1.5 %gradient.3 = (bf16[256,256]{1,0:T(8,128)(2,1)S(1)}, bf16[256,256]{1,0:T(8,128)(2,1)S(1)}) custom-call(bf16[512,1024]{1,0:T(8,128)(2,1)S(1)} %get-tuple-element.52.xt_ref, bf16[1024,1024]{1,0:T(8,128)(2,1)S(1)} %get-tuple-element.31.refs_0_.adj_ref, f32[1024,128]{1,0:T(8,128)S(1)} %get-tuple-element.44.col_ref, ...), custom_call_target="tpu_custom_call" | custom-call | flops 805306368 | bytes 2883584 | tf_op jit(solution)/shard_map/gradient/pallas_call | solution.py:276
  31.2 3.5 %collective-permute-start.23 = (bf16[256,256]{1,0:T(8,128)(2,1)S(1)}, bf16[256,256]{1,0:T(8,128)(2,1)S(1)}, u32[]{:S(2)}, u32[]{:S(2)}) collective-permute-start(bf16[256,256]{1,0:T(8,128)(2,1)S(1)} %get-tuple-element.57), channel_id=1, source_target_pairs={{0,8},{24,16},{1,9},{25,17},{2,10},{26,18},{3,11},{27,19},{4,12},{... | collective-permute-start | bytes 393224 | tf_op jit(solution)/shard_map/ppermute | solution.py:329
  34.6 1.5 %gradient.4 = bf16[512,256]{1,0:T(8,128)(2,1)S(1)} custom-call(bf16[512,1024]{1,0:T(8,128)(2,1)S(1)} %get-tuple-element.52.xt_ref, bf16[1024,1024]{1,0:T(8,128)(2,1)S(1)} %get-tuple-element.32.refs_1_.adj_ref, f32[1024,128]{1,0:T(8,128)S(1)} %get-tuple-element.49.col_ref, bf16[128,256]{1,0:T(8,128)(2,1)S(1)} %collective-permute-done.7.rest_0_, ...), custom_call_target="tpu_custom_call" | custom-call | flops 805306368 | bytes 2883584 | tf_op jit(solution)/shard_map/gradient/pallas_call | solution.py:276
  36.2 1.5 %gradient.5 = bf16[512,256]{1,0:T(8,128)(2,1)S(1)} custom-call(bf16[512,1024]{1,0:T(8,128)(2,1)S(1)} %get-tuple-element.52.xt_ref, bf16[1024,1024]{1,0:T(8,128)(2,1)S(1)} %get-tuple-element.33.refs_2_.adj_ref, f32[1024,128]{1,0:T(8,128)S(1)} %get-tuple-element.53.col_ref, bf16[128,256]{1,0:T(8,128)(2,1)S(1)} %collective-permute-done.7.rest_0_, ...), custom_call_target="tpu_custom_call" | custom-call | flops 805306368 | bytes 2883584 | tf_op jit(solution)/shard_map/gradient/pallas_call | solution.py:276
  37.7 1.3 %collective-permute-start.15 = (bf16[256,256]{1,0:T(8,128)(2,1)S(1)}, bf16[256,256]{1,0:T(8,128)(2,1)S(1)}, u32[]{:S(2)}, u32[]{:S(2)}) collective-permute-start(bf16[256,256]{1,0:T(8,128)(2,1)S(1)} %get-tuple-element.51), channel_id=1, source_target_pairs={{0,8},{24,16},{1,9},{25,17},{2,10},{26,18},{3,11},{27,19},{4,12},{... | collective-permute-start | bytes 393224 | tf_op jit(solution)/shard_map/ppermute | solution.py:329
  39.0 1.3 %collective-permute-start.17 = (bf16[512,256]{1,0:T(8,128)(2,1)S(1)}, bf16[512,256]{1,0:T(8,128)(2,1)S(1)}, u32[]{:S(2)}, u32[]{:S(2)}) collective-permute-start(bf16[512,256]{1,0:T(8,128)(2,1)S(1)} %gradient.5), channel_id=1, source_target_pairs={{0,8},{24,16},{1,9},{25,17},{2,10},{26,18},{3,11},{27,19},{4,12},{... | collective-permute-start | bytes 786440 | tf_op jit(solution)/shard_map/ppermute | solution.py:329
  40.3 1.3 %collective-permute-start.14 = (bf16[512,256]{1,0:T(8,128)(2,1)S(1)}, bf16[512,256]{1,0:T(8,128)(2,1)S(1)}, u32[]{:S(2)}, u32[]{:S(2)}) collective-permute-start(bf16[512,256]{1,0:T(8,128)(2,1)S(1)} %gradient.4), channel_id=1, source_target_pairs={{0,8},{24,16},{1,9},{25,17},{2,10},{26,18},{3,11},{27,19},{4,12},{... | collective-permute-start | bytes 786440 | tf_op jit(solution)/shard_map/ppermute | solution.py:329
  41.7 0.7 collective-permute-start.24
  42.4 0.5 collective-permute-done.15
  42.9 0.7 collective-permute-start.16
  43.6 1.3 %collective-permute-start.25 = (bf16[256,256]{1,0:T(8,128)(2,1)S(1)}, bf16[256,256]{1,0:T(8,128)(2,1)S(1)}, u32[]{:S(2)}, u32[]{:S(2)}) collective-permute-start(bf16[256,256]{1,0:T(8,128)(2,1)S(1)} %reduce-precision_convert_fusion.4.sent_ref), channel_id=1, source_target_pairs={{8,0},{16,24},{9,1},{17,25},{10,2},{18,26},{11,3},{19,27},{12,4},{... | collective-permute-start | bytes 393224 | tf_op jit(solution)/shard_map/ppermute | solution.py:347
  44.9 3.5 %collective-permute-done.17 = bf16[512,256]{1,0:T(8,128)(2,1)S(1)} collective-permute-done((bf16[512,256]{1,0:T(8,128)(2,1)S(1)}, bf16[512,256]{1,0:T(8,128)(2,1)S(1)}, u32[]{:S(2)}, u32[]{:S(2)}) %collective-permute-start.17) | collective-permute-done | bytes 262176 | tf_op jit(solution)/shard_map/ppermute | solution.py:329
  48.5 0.7 collective-permute-start.20
  49.3 1.3 %collective-permute-start.22 = (bf16[256,256]{1,0:T(8,128)(2,1)S(1)}, bf16[256,256]{1,0:T(8,128)(2,1)S(1)}, u32[]{:S(2)}, u32[]{:S(2)}) collective-permute-start(bf16[256,256]{1,0:T(8,128)(2,1)S(1)} %reduce-precision_convert_fusion.6.sent_ref), channel_id=1, source_target_pairs={{8,0},{16,24},{9,1},{17,25},{10,2},{18,26},{11,3},{19,27},{12,4},{... | collective-permute-start | bytes 393224 | tf_op jit(solution)/shard_map/ppermute | solution.py:347
  50.6 2.7 %collective-permute-done.14 = bf16[512,256]{1,0:T(8,128)(2,1)S(1)} collective-permute-done((bf16[512,256]{1,0:T(8,128)(2,1)S(1)}, bf16[512,256]{1,0:T(8,128)(2,1)S(1)}, u32[]{:S(2)}, u32[]{:S(2)}) %collective-permute-start.14) | collective-permute-done | bytes 262176 | tf_op jit(solution)/shard_map/ppermute | solution.py:329
  53.4 0.7 collective-permute-start.18
  54.1 0.7 %finish.4.rest_0_ = f32[3,512,256]{2,1,0:T(8,128)} custom-call(bf16[256,256]{1,0:T(8,128)(2,1)S(1)} %collective-permute-done.25.got_ref, bf16[256,256]{1,0:T(8,128)(2,1)S(1)} %reduce-precision_convert_fusion.4.sent_ref), custom_call_target="tpu_custom_call" | custom-call | flops 2000000000 | bytes 524288 | tf_op jit(solution)/shard_map/finish/pallas_call | solution.py:303
  54.9 1.3 %collective-permute-start.21 = (bf16[512,256]{1,0:T(8,128)(2,1)S(1)}, bf16[512,256]{1,0:T(8,128)(2,1)S(1)}, u32[]{:S(2)}, u32[]{:S(2)}) collective-permute-start(bf16[512,256]{1,0:T(8,128)(2,1)S(1)} %reduce-precision_convert_fusion.sent_ref), channel_id=1, source_target_pairs={{8,0},{16,24},{9,1},{17,25},{10,2},{18,26},{11,3},{19,27},{12,4},{... | collective-permute-start | bytes 786440 | tf_op jit(solution)/shard_map/ppermute | solution.py:347
  56.3 1.3 %collective-permute-start.19 = (bf16[512,256]{1,0:T(8,128)(2,1)S(1)}, bf16[512,256]{1,0:T(8,128)(2,1)S(1)}, u32[]{:S(2)}, u32[]{:S(2)}) collective-permute-start(bf16[512,256]{1,0:T(8,128)(2,1)S(1)} %reduce-precision_convert_fusion.1.sent_ref), channel_id=1, source_target_pairs={{8,0},{16,24},{9,1},{17,25},{10,2},{18,26},{11,3},{19,27},{12,4},{... | collective-permute-start | bytes 786440 | tf_op jit(solution)/shard_map/ppermute | solution.py:347
  57.6 1.2 %collective-permute-done.22.got_ref = bf16[256,256]{1,0:T(8,128)(2,1)S(1)} collective-permute-done((bf16[256,256]{1,0:T(8,128)(2,1)S(1)}, bf16[256,256]{1,0:T(8,128)(2,1)S(1)}, u32[]{:S(2)}, u32[]{:S(2)}) %collective-permute-start.22) | collective-permute-done | bytes 131104 | tf_op jit(solution)/shard_map/ppermute | solution.py:347
  58.8 0.7 %finish.5.rest_0_ = f32[3,512,256]{2,1,0:T(8,128)} custom-call(bf16[256,256]{1,0:T(8,128)(2,1)S(1)} %collective-permute-done.22.got_ref, bf16[256,256]{1,0:T(8,128)(2,1)S(1)} %reduce-precision_convert_fusion.6.sent_ref, f32[3,512,256]{2,1,0:T(8,128)} %finish.4.rest_0_), custom_call_target="tpu_custom_call", output_to_operand_aliasing={{}: (2, {})} | custom-call | flops 2000000000 | bytes 524288 | tf_op jit(solution)/shard_map/finish/pallas_call | solution.py:303
  59.5 8.5 %collective-permute-done.21.got_ref = bf16[512,256]{1,0:T(8,128)(2,1)S(1)} collective-permute-done((bf16[512,256]{1,0:T(8,128)(2,1)S(1)}, bf16[512,256]{1,0:T(8,128)(2,1)S(1)}, u32[]{:S(2)}, u32[]{:S(2)}) %collective-permute-start.21) | collective-permute-done | bytes 262176 | tf_op jit(solution)/shard_map/ppermute | solution.py:347
  68.1 0.9 %finish.6.rest_0_ = f32[3,512,256]{2,1,0:T(8,128)} custom-call(bf16[512,256]{1,0:T(8,128)(2,1)S(1)} %collective-permute-done.21.got_ref, bf16[512,256]{1,0:T(8,128)(2,1)S(1)} %reduce-precision_convert_fusion.sent_ref, f32[3,512,256]{2,1,0:T(8,128)} %finish.5.rest_0_), custom_call_target="tpu_custom_call", output_to_operand_aliasing={{}: (2, {})} | custom-call | flops 2000000000 | bytes 1048576 | tf_op jit(solution)/shard_map/finish/pallas_call | solution.py:303
  68.9 3.7 %collective-permute-done.19.got_ref = bf16[512,256]{1,0:T(8,128)(2,1)S(1)} collective-permute-done((bf16[512,256]{1,0:T(8,128)(2,1)S(1)}, bf16[512,256]{1,0:T(8,128)(2,1)S(1)}, u32[]{:S(2)}, u32[]{:S(2)}) %collective-permute-start.19) | collective-permute-done | bytes 262176 | tf_op jit(solution)/shard_map/ppermute | solution.py:347
  72.6 0.9 %finish.7 = f32[3,512,256]{2,1,0:T(8,128)} custom-call(bf16[512,256]{1,0:T(8,128)(2,1)S(1)} %collective-permute-done.19.got_ref, bf16[512,256]{1,0:T(8,128)(2,1)S(1)} %reduce-precision_convert_fusion.1.sent_ref, f32[3,512,256]{2,1,0:T(8,128)} %finish.6.rest_0_), custom_call_target="tpu_custom_call", output_to_operand_aliasing={{}: (2, {})} | custom-call | flops 2000000000 | bytes 1048576 | tf_op jit(solution)/shard_map/finish/pallas_call | solution.py:303
  (42 shorter events, 0.7 us)
Async XLA Ops:
  0.6 1.0 %copy-start.5 = (s32[8,3,4,8,128]{4,3,2,1,0:T(8,128)S(1)}, s32[8,3,4,8,128]{4,3,2,1,0:T(8,128)}, u32[]{:S(2)}) copy-start(s32[8,3,4,8,128]{4,3,2,1,0:T(8,128)} %pat_ref.1) | copy-start | bytes 1179652
  1.6 0.7 copy-start.6
  2.3 0.7 copy-start.7
  3.0 4.1 %copy-start = (bf16[1024,512]{1,0:T(8,128)(2,1)S(1)}, bf16[1024,512]{1,0:T(8,128)(2,1)}, u32[]{:S(2)}) copy-start(bf16[1024,512]{1,0:T(8,128)(2,1)} %x_ref.1) | copy-start | bytes 3145732
  3.0 4.1 %copy-start.4 = (bf16[3,512,256]{2,1,0:T(8,128)(2,1)S(1)}, bf16[3,512,256]{2,1,0:T(8,128)(2,1)}, u32[]{:S(2)}) copy-start(bf16[3,512,256]{2,1,0:T(8,128)(2,1)} %refs_4_.1) | copy-start | bytes 2359300
  7.1 13.3 %copy-start.1 = (bf16[128,256]{1,0:T(8,128)(2,1)S(1)}, bf16[128,256]{1,0:T(8,128)(2,1)}, u32[]{:S(2)}) copy-start(bf16[128,256]{1,0:T(8,128)(2,1)} %refs_7_.1) | copy-start | bytes 196612
  7.2 13.2 %copy-start.2 = (f32[3,256]{1,0:T(4,128)S(1)}, f32[3,256]{1,0:T(4,128)}, u32[]{:S(2)}) copy-start(f32[3,256]{1,0:T(4,128)} %refs_6_.1) | copy-start | bytes 9220
  7.2 13.2 %copy-start.3 = (s32[128]{0:T(128)S(1)}, s32[128]{0:T(128)}, u32[]{:S(2)}) copy-start(s32[128]{0:T(128)} %param.13) | copy-start | bytes 1540
  10.2 1.4 %collective-permute-start = (bf16[128,256]{1,0:T(8,128)(2,1)S(1)}, bf16[128,256]{1,0:T(8,128)(2,1)S(1)}, u32[]{:S(2)}, u32[]{:S(2)}) collective-permute-start(bf16[128,256]{1,0:T(8,128)(2,1)S(1)} %get-tuple-element.35), channel_id=1, source_target_pairs={{0,1},{1,0},{2,3},{3,2},{4,5},{5,4},{6,7},{7,6},{8,9},{9,8},{10,11... | collective-permute-start | bytes 196616 | tf_op jit(solution)/shard_map/ppermute | solution.py:356
  10.7 4.8 %collective-permute-start.2 = (bf16[128,256]{1,0:T(8,128)(2,1)S(1)}, bf16[128,256]{1,0:T(8,128)(2,1)S(1)}, u32[]{:S(2)}, u32[]{:S(2)}) collective-permute-start(bf16[128,256]{1,0:T(8,128)(2,1)S(1)} %get-tuple-element.37), channel_id=1, source_target_pairs={{0,1},{1,0},{2,3},{3,2},{4,5},{5,4},{6,7},{7,6},{8,9},{9,8},{10,11... | collective-permute-start | bytes 196616 | tf_op jit(solution)/shard_map/ppermute | solution.py:356
  10.8 5.3 %collective-permute-start.4 = (bf16[128,256]{1,0:T(8,128)(2,1)S(1)}, bf16[128,256]{1,0:T(8,128)(2,1)S(1)}, u32[]{:S(2)}, u32[]{:S(2)}) collective-permute-start(bf16[128,256]{1,0:T(8,128)(2,1)S(1)} %get-tuple-element.39), channel_id=1, source_target_pairs={{0,1},{1,0},{2,3},{3,2},{4,5},{5,4},{6,7},{7,6},{8,9},{9,8},{10,11... | collective-permute-start | bytes 196616 | tf_op jit(solution)/shard_map/ppermute | solution.py:356
  11.2 5.1 %collective-permute-start.6 = (bf16[128,256]{1,0:T(8,128)(2,1)S(1)}, bf16[128,256]{1,0:T(8,128)(2,1)S(1)}, u32[]{:S(2)}, u32[]{:S(2)}) collective-permute-start(bf16[128,256]{1,0:T(8,128)(2,1)S(1)} %get-tuple-element.40), channel_id=1, source_target_pairs={{0,1},{1,0},{2,3},{3,2},{4,5},{5,4},{6,7},{7,6},{8,9},{9,8},{10,11... | collective-permute-start | bytes 196616 | tf_op jit(solution)/shard_map/ppermute | solution.py:356
  11.6 6.3 %collective-permute-start.1 = (bf16[128,256]{1,0:T(8,128)(2,1)S(1)}, bf16[128,256]{1,0:T(8,128)(2,1)S(1)}, u32[]{:S(2)}, u32[]{:S(2)}) collective-permute-start(bf16[128,256]{1,0:T(8,128)(2,1)S(1)} %add_convert_fusion.2), channel_id=1, source_target_pairs={{0,6},{1,7},{2,4},{3,5},{4,2},{5,3},{6,0},{7,1},{8,14},{9,15},{10,... | collective-permute-start | bytes 196616 | tf_op jit(solution)/shard_map/ppermute | solution.py:356
  15.5 4.3 %collective-permute-start.3 = (bf16[128,256]{1,0:T(8,128)(2,1)S(1)}, bf16[128,256]{1,0:T(8,128)(2,1)S(1)}, u32[]{:S(2)}, u32[]{:S(2)}) collective-permute-start(bf16[128,256]{1,0:T(8,128)(2,1)S(1)} %add_convert_fusion.1), channel_id=1, source_target_pairs={{0,4},{1,5},{2,6},{3,7},{4,0},{5,1},{6,2},{7,3},{8,12},{9,13},{10,... | collective-permute-start | bytes 196616 | tf_op jit(solution)/shard_map/ppermute | solution.py:356
  16.1 4.3 %collective-permute-start.5 = (bf16[128,256]{1,0:T(8,128)(2,1)S(1)}, bf16[128,256]{1,0:T(8,128)(2,1)S(1)}, u32[]{:S(2)}, u32[]{:S(2)}) collective-permute-start(bf16[128,256]{1,0:T(8,128)(2,1)S(1)} %add_convert_fusion), channel_id=1, source_target_pairs={{0,2},{1,3},{2,0},{3,1},{4,6},{5,7},{6,4},{7,5},{8,10},{9,11},{10,... | collective-permute-start | bytes 196616 | tf_op jit(solution)/shard_map/ppermute | solution.py:356
  21.2 4.6 %collective-permute-start.9 = (bf16[128,256]{1,0:T(8,128)(2,1)S(1)}, bf16[128,256]{1,0:T(8,128)(2,1)S(1)}, u32[]{:S(2)}, u32[]{:S(2)}) collective-permute-start(bf16[128,256]{1,0:T(8,128)(2,1)S(1)} %get-tuple-element.45.rest_3_), channel_id=1, source_target_pairs={{0,2},{1,3},{2,0},{3,1},{4,6},{5,7},{6,4},{7,5},{8,10},{9,11},{10,... | collective-permute-start | bytes 196616 | tf_op jit(solution)/shard_map/ppermute | solution.py:356
  21.8 4.5 %collective-permute-start.8 = (bf16[128,256]{1,0:T(8,128)(2,1)S(1)}, bf16[128,256]{1,0:T(8,128)(2,1)S(1)}, u32[]{:S(2)}, u32[]{:S(2)}) collective-permute-start(bf16[128,256]{1,0:T(8,128)(2,1)S(1)} %get-tuple-element.45.rest_3_), channel_id=1, source_target_pairs={{0,4},{1,5},{2,6},{3,7},{4,0},{5,1},{6,2},{7,3},{8,12},{9,13},{10,... | collective-permute-start | bytes 196616 | tf_op jit(solution)/shard_map/ppermute | solution.py:356
  23.2 5.2 %collective-permute-start.7 = (bf16[128,256]{1,0:T(8,128)(2,1)S(1)}, bf16[128,256]{1,0:T(8,128)(2,1)S(1)}, u32[]{:S(2)}, u32[]{:S(2)}) collective-permute-start(bf16[128,256]{1,0:T(8,128)(2,1)S(1)} %get-tuple-element.45.rest_3_), channel_id=1, source_target_pairs={{0,6},{1,7},{2,4},{3,5},{4,2},{5,3},{6,0},{7,1},{8,14},{9,15},{10,... | collective-permute-start | bytes 196616 | tf_op jit(solution)/shard_map/ppermute | solution.py:356
  24.6 4.6 %collective-permute-start.10 = (bf16[128,256]{1,0:T(8,128)(2,1)S(1)}, bf16[128,256]{1,0:T(8,128)(2,1)S(1)}, u32[]{:S(2)}, u32[]{:S(2)}) collective-permute-start(bf16[128,256]{1,0:T(8,128)(2,1)S(1)} %get-tuple-element.45.rest_3_), channel_id=1, source_target_pairs={{0,1},{1,0},{2,3},{3,2},{4,5},{5,4},{6,7},{7,6},{8,9},{9,8},{10,11... | collective-permute-start | bytes 196616 | tf_op jit(solution)/shard_map/ppermute | solution.py:356
  25.8 3.5 %collective-permute-start.11 = (bf16[128,256]{1,0:T(8,128)(2,1)S(1)}, bf16[128,256]{1,0:T(8,128)(2,1)S(1)}, u32[]{:S(2)}, u32[]{:S(2)}) collective-permute-start(bf16[128,256]{1,0:T(8,128)(2,1)S(1)} %collective-permute-done.9.rest_2_), channel_id=1, source_target_pairs={{0,1},{1,0},{2,3},{3,2},{4,5},{5,4},{6,7},{7,6},{8,9},{9,8},{10,11... | collective-permute-start | bytes 196616 | tf_op jit(solution)/shard_map/ppermute | solution.py:356
  26.3 3.0 %collective-permute-start.12 = (bf16[128,256]{1,0:T(8,128)(2,1)S(1)}, bf16[128,256]{1,0:T(8,128)(2,1)S(1)}, u32[]{:S(2)}, u32[]{:S(2)}) collective-permute-start(bf16[128,256]{1,0:T(8,128)(2,1)S(1)} %collective-permute-done.8.rest_1_), channel_id=1, source_target_pairs={{0,1},{1,0},{2,3},{3,2},{4,5},{5,4},{6,7},{7,6},{8,9},{9,8},{10,11... | collective-permute-start | bytes 196616 | tf_op jit(solution)/shard_map/ppermute | solution.py:356
  28.4 1.3 %collective-permute-start.13 = (bf16[128,256]{1,0:T(8,128)(2,1)S(1)}, bf16[128,256]{1,0:T(8,128)(2,1)S(1)}, u32[]{:S(2)}, u32[]{:S(2)}) collective-permute-start(bf16[128,256]{1,0:T(8,128)(2,1)S(1)} %collective-permute-done.7.rest_0_), channel_id=1, source_target_pairs={{0,1},{1,0},{2,3},{3,2},{4,5},{5,4},{6,7},{7,6},{8,9},{9,8},{10,11... | collective-permute-start | bytes 196616 | tf_op jit(solution)/shard_map/ppermute | solution.py:356
  31.2 10.5 %collective-permute-start.23 = (bf16[256,256]{1,0:T(8,128)(2,1)S(1)}, bf16[256,256]{1,0:T(8,128)(2,1)S(1)}, u32[]{:S(2)}, u32[]{:S(2)}) collective-permute-start(bf16[256,256]{1,0:T(8,128)(2,1)S(1)} %get-tuple-element.57), channel_id=1, source_target_pairs={{0,8},{24,16},{1,9},{25,17},{2,10},{26,18},{3,11},{27,19},{4,12},{... | collective-permute-start | bytes 393224 | tf_op jit(solution)/shard_map/ppermute | solution.py:329
  37.7 5.1 %collective-permute-start.15 = (bf16[256,256]{1,0:T(8,128)(2,1)S(1)}, bf16[256,256]{1,0:T(8,128)(2,1)S(1)}, u32[]{:S(2)}, u32[]{:S(2)}) collective-permute-start(bf16[256,256]{1,0:T(8,128)(2,1)S(1)} %get-tuple-element.51), channel_id=1, source_target_pairs={{0,8},{24,16},{1,9},{25,17},{2,10},{26,18},{3,11},{27,19},{4,12},{... | collective-permute-start | bytes 393224 | tf_op jit(solution)/shard_map/ppermute | solution.py:329
  39.0 9.4 %collective-permute-start.17 = (bf16[512,256]{1,0:T(8,128)(2,1)S(1)}, bf16[512,256]{1,0:T(8,128)(2,1)S(1)}, u32[]{:S(2)}, u32[]{:S(2)}) collective-permute-start(bf16[512,256]{1,0:T(8,128)(2,1)S(1)} %gradient.5), channel_id=1, source_target_pairs={{0,8},{24,16},{1,9},{25,17},{2,10},{26,18},{3,11},{27,19},{4,12},{... | collective-permute-start | bytes 786440 | tf_op jit(solution)/shard_map/ppermute | solution.py:329
  40.3 13.0 %collective-permute-start.14 = (bf16[512,256]{1,0:T(8,128)(2,1)S(1)}, bf16[512,256]{1,0:T(8,128)(2,1)S(1)}, u32[]{:S(2)}, u32[]{:S(2)}) collective-permute-start(bf16[512,256]{1,0:T(8,128)(2,1)S(1)} %gradient.4), channel_id=1, source_target_pairs={{0,8},{24,16},{1,9},{25,17},{2,10},{26,18},{3,11},{27,19},{4,12},{... | collective-permute-start | bytes 786440 | tf_op jit(solution)/shard_map/ppermute | solution.py:329
  41.7 1.9 %collective-permute-start.24 = (bf16[256,256]{1,0:T(8,128)(2,1)S(1)}, bf16[256,256]{1,0:T(8,128)(2,1)S(1)}, u32[]{:S(2)}, u32[]{:S(2)}) collective-permute-start(bf16[256,256]{1,0:T(8,128)(2,1)S(1)} %reduce-precision_convert_fusion.5), channel_id=1, source_target_pairs={{8,16},{16,8},{9,17},{17,9},{10,18},{18,10},{11,19},{19,11},{12,20... | collective-permute-start | bytes 393224 | tf_op jit(solution)/shard_map/ppermute | solution.py:336
  42.9 6.3 %collective-permute-start.16 = (bf16[256,256]{1,0:T(8,128)(2,1)S(1)}, bf16[256,256]{1,0:T(8,128)(2,1)S(1)}, u32[]{:S(2)}, u32[]{:S(2)}) collective-permute-start(bf16[256,256]{1,0:T(8,128)(2,1)S(1)} %reduce-precision_convert_fusion.7), channel_id=1, source_target_pairs={{8,16},{16,8},{9,17},{17,9},{10,18},{18,10},{11,19},{19,11},{12,20... | collective-permute-start | bytes 393224 | tf_op jit(solution)/shard_map/ppermute | solution.py:336
  43.6 10.5 %collective-permute-start.25 = (bf16[256,256]{1,0:T(8,128)(2,1)S(1)}, bf16[256,256]{1,0:T(8,128)(2,1)S(1)}, u32[]{:S(2)}, u32[]{:S(2)}) collective-permute-start(bf16[256,256]{1,0:T(8,128)(2,1)S(1)} %reduce-precision_convert_fusion.4.sent_ref), channel_id=1, source_target_pairs={{8,0},{16,24},{9,1},{17,25},{10,2},{18,26},{11,3},{19,27},{12,4},{... | collective-permute-start | bytes 393224 | tf_op jit(solution)/shard_map/ppermute | solution.py:347
  48.5 6.3 %collective-permute-start.20 = (bf16[512,256]{1,0:T(8,128)(2,1)S(1)}, bf16[512,256]{1,0:T(8,128)(2,1)S(1)}, u32[]{:S(2)}, u32[]{:S(2)}) collective-permute-start(bf16[512,256]{1,0:T(8,128)(2,1)S(1)} %reduce-precision_convert_fusion.2), channel_id=1, source_target_pairs={{8,16},{16,8},{9,17},{17,9},{10,18},{18,10},{11,19},{19,11},{12,20... | collective-permute-start | bytes 786440 | tf_op jit(solution)/shard_map/ppermute | solution.py:336
  49.3 9.5 %collective-permute-start.22 = (bf16[256,256]{1,0:T(8,128)(2,1)S(1)}, bf16[256,256]{1,0:T(8,128)(2,1)S(1)}, u32[]{:S(2)}, u32[]{:S(2)}) collective-permute-start(bf16[256,256]{1,0:T(8,128)(2,1)S(1)} %reduce-precision_convert_fusion.6.sent_ref), channel_id=1, source_target_pairs={{8,0},{16,24},{9,1},{17,25},{10,2},{18,26},{11,3},{19,27},{12,4},{... | collective-permute-start | bytes 393224 | tf_op jit(solution)/shard_map/ppermute | solution.py:347
  53.4 2.8 %collective-permute-start.18 = (bf16[512,256]{1,0:T(8,128)(2,1)S(1)}, bf16[512,256]{1,0:T(8,128)(2,1)S(1)}, u32[]{:S(2)}, u32[]{:S(2)}) collective-permute-start(bf16[512,256]{1,0:T(8,128)(2,1)S(1)} %reduce-precision_convert_fusion.3), channel_id=1, source_target_pairs={{8,16},{16,8},{9,17},{17,9},{10,18},{18,10},{11,19},{19,11},{12,20... | collective-permute-start | bytes 786440 | tf_op jit(solution)/shard_map/ppermute | solution.py:336
  54.9 13.2 %collective-permute-start.21 = (bf16[512,256]{1,0:T(8,128)(2,1)S(1)}, bf16[512,256]{1,0:T(8,128)(2,1)S(1)}, u32[]{:S(2)}, u32[]{:S(2)}) collective-permute-start(bf16[512,256]{1,0:T(8,128)(2,1)S(1)} %reduce-precision_convert_fusion.sent_ref), channel_id=1, source_target_pairs={{8,0},{16,24},{9,1},{17,25},{10,2},{18,26},{11,3},{19,27},{12,4},{... | collective-permute-start | bytes 786440 | tf_op jit(solution)/shard_map/ppermute | solution.py:347
  56.3 16.3 %collective-permute-start.19 = (bf16[512,256]{1,0:T(8,128)(2,1)S(1)}, bf16[512,256]{1,0:T(8,128)(2,1)S(1)}, u32[]{:S(2)}, u32[]{:S(2)}) collective-permute-start(bf16[512,256]{1,0:T(8,128)(2,1)S(1)} %reduce-precision_convert_fusion.1.sent_ref), channel_id=1, source_target_pairs={{8,0},{16,24},{9,1},{17,25},{10,2},{18,26},{11,3},{19,27},{12,4},{... | collective-permute-start | bytes 786440 | tf_op jit(solution)/shard_map/ppermute | solution.py:347
